TPU v7x, 512 devices: a whole 4x4x16 slice. The times are simulated.
512 devices in a mesh: pix: 128 (over z, x_lo, y), comp: 4 (over x_hi, core).
Axes of the slice: x: 4 (x_hi: 2, x_lo: 2; x = x_hi * 2 + x_lo), y: 4, z: 16, core: 2. Of those that a mesh axis runs over, the one named last changes fastest.
Arguments:
- atmos_state: bfloat16 [2, 8, 4096, 128], P(None, None, 'pix'), may hold values from -6 to 6
- ocean_state: bfloat16 [2, 8, 4096, 128], P(None, None, 'pix'), may hold values from -6 to 6
- conv_weight: bfloat16 [4, 2, 9, 128, 128], P('comp'), may hold values from -0.1875 to 0.1875
- rotation: int32 [128, 2], P('pix'), may hold values from 0 to 3
- sea_mask: int32 [8, 4096], P(None, 'pix'), may hold values 0 or 1
Outputs:
- atmos_next: bfloat16 [2, 8, 4096, 128], P(None, 'comp', 'pix')
- ocean_next: bfloat16 [2, 8, 4096, 128], P(None, 'comp', 'pix')
All inputs are finite; a program needn't handle non-finite values. No bound on the sum of `sea_mask` on one device may be relied on, other than what follows from the above.
Results may differ from a plain program's by a relative error of at most 0.025.
Values may be sent and summed in bfloat16 or wider, within the bound.
No kernel may reach another device: no remote copies, remote signals or barrier semaphores. Data moves between devices by JAX's collectives and lax.ppermute only.
A program may use at most 64 MiB of HBM per device.

v0:
```python
import jax
import jax.numpy as jnp
from jax import lax
from jax.sharding import PartitionSpec as P

STEPS = 2


def with_halo(value, sides, width):
    for axis, dim in sides:
        count, length = (lax.axis_size(axis), value.shape[dim])
        up = [(i, (i + 1) % count) for i in range(count)]
        down = [(j, i) for i, j in up]
        last = lax.slice_in_dim(value, length - width, length, axis=dim)
        leading = lax.slice_in_dim(value, 0, width, axis=dim)
        before = lax.ppermute(last, axis, up)
        after = lax.ppermute(leading, axis, down)
        value = jnp.concatenate([before, value, after], axis=dim)
    return value


def from_behind(block, axis, distance):
    devices = range(lax.axis_size(axis))
    route = [(i - distance, i) for i in devices if i - distance in devices]
    return lax.ppermute(block, axis, route)


def spread(block, axis, owner):
    block = jnp.where(lax.axis_index(axis) == owner, block, jnp.zeros_like(block))
    return lax.psum(block, axis)


def turn_pairs(column, turn_code):
    half_width = column.shape[-1] // 2
    first_part = column[..., :half_width].astype(jnp.float32)
    second_part = column[..., half_width:].astype(jnp.float32)
    cosine = jnp.where(turn_code == 0, 1.0, jnp.where(turn_code == 2, -1.0, 0.0)).astype(
        jnp.float32
    )[..., None]
    sine_term = jnp.where(turn_code == 1, 1.0, jnp.where(turn_code == 3, -1.0, 0.0)).astype(
        jnp.float32
    )[..., None]
    turned = jnp.concatenate(
        [
            cosine * first_part - sine_term * second_part,
            sine_term * first_part + cosine * second_part,
        ],
        axis=-1,
    )
    return turned.astype(jnp.bfloat16)


def convolve_local(field_in, weights, turn_codes):
    batch_count, row_count, tile_width, channels = field_in.shape
    padded = with_halo(field_in, (("pix", 2),), 1)
    left_column = turn_pairs(padded[:, :, 0], turn_codes[0, 0])
    right_column = turn_pairs(padded[:, :, tile_width + 1], turn_codes[0, 1])
    padded = jnp.concatenate([left_column[:, :, None], field_in, right_column[:, :, None]], axis=2)
    padded = jnp.pad(padded, ((0, 0), (1, 1), (0, 0), (0, 0)))
    total_sum = jnp.zeros((batch_count, row_count, tile_width, channels), jnp.float32)
    for offset in range(9):
        row_shift, column_shift = (offset // 3, offset % 3)
        window = padded[
            :, row_shift : row_shift + row_count, column_shift : column_shift + tile_width
        ]
        total_sum = total_sum + jnp.einsum(
            "krwc,cd->krwd", window, weights[offset], preferred_element_type=jnp.float32
        )
    return total_sum


def residual_block(field_in, weights, turn_codes, base_field, gate_field):
    inner_field = jax.nn.gelu(convolve_local(field_in, weights[0], turn_codes)).astype(jnp.bfloat16)
    return (
        base_field.astype(jnp.float32)
        + gate_field * convolve_local(inner_field, weights[1], turn_codes)
    ).astype(jnp.bfloat16)


def per_device(atmos_state, ocean_state, conv_weight, rotation, sea_mask):
    sections = lax.axis_size("comp")
    segment_index = lax.axis_index("comp")
    last_segment = sections - 1
    sea_field = sea_mask.astype(jnp.float32)[:, :, None]
    band_rows = atmos_state.shape[1] // sections
    row_start = segment_index * band_rows
    weights = conv_weight[0]
    members = atmos_state.shape[0]
    is_ocean = segment_index == last_segment
    first_segment = segment_index == 0
    gate_field = jnp.where(is_ocean, sea_field, jnp.ones_like(sea_field))
    atmos_now, ocean_now = (atmos_state, ocean_state)
    for step_index in range(STEPS):
        received = jnp.zeros((1,) + atmos_now.shape[1:], jnp.bfloat16)
        kept_atmos = []
        kept_ocean = []
        for tick_index in range(members + last_segment):
            if tick_index < members:
                feed_input = (
                    atmos_now[tick_index : tick_index + 1].astype(jnp.float32)
                    + sea_field * ocean_now[tick_index : tick_index + 1].astype(jnp.float32)
                ).astype(jnp.bfloat16)
            else:
                feed_input = jnp.zeros_like(received)
            source = jnp.where(first_segment, feed_input, received)
            member_index = jnp.clip(tick_index - segment_index, 0, members - 1)
            current_ocean = lax.dynamic_slice_in_dim(ocean_now, member_index, 1, 0)
            mixed_input = (source.astype(jnp.float32) + current_ocean.astype(jnp.float32)).astype(
                jnp.bfloat16
            )
            entering = jnp.where(is_ocean, mixed_input, source)
            base_field = jnp.where(is_ocean, current_ocean, source)
            produced = residual_block(entering, weights, rotation, base_field, gate_field)
            if tick_index >= last_segment:
                kept_atmos.append(source)
                kept_ocean.append(produced)
            if tick_index < members + last_segment - 1:
                received = from_behind(produced, "comp", 1)
        atmos_now = jnp.concatenate(kept_atmos, axis=0)
        ocean_now = jnp.concatenate(kept_ocean, axis=0)
        atmos_now, ocean_now = (
            spread(atmos_now, "comp", last_segment),
            spread(ocean_now, "comp", last_segment),
        )
    atmos_rows = lax.dynamic_slice_in_dim(atmos_now, row_start, band_rows, 1)
    ocean_rows = lax.dynamic_slice_in_dim(ocean_now, row_start, band_rows, 1)
    return (atmos_rows, ocean_rows)


def solution(mesh):
    in_specs = (
        P(None, None, "pix", None),
        P(None, None, "pix", None),
        P("comp", None, None, None, None),
        P("pix", None),
        P(None, "pix"),
    )
    out_specs = (P(None, "comp", "pix", None), P(None, "comp", "pix", None))
    return jax.shard_map(
        per_device, mesh=mesh, in_specs=in_specs, out_specs=out_specs, check_vma=False
    )
```

profile of v0, /device:TPU:1, one launch (start us, length us, event | category | flops | bytes accessed | tf_op | source)
XLA Modules:
  0.0 474.0 jit_solution(10866973784567519995)
XLA Ops:
  9.4 15.3 %collective-permute-start.1 = (bf16[1,8,1,128]{3,1,2,0:T(8,128)(2,1)S(1)}, bf16[1,8,1,128]{3,1,2,0:T(8,128)(2,1)S(1)}, u32[]{:S(2)}, u32[]{:S(2)}) collective-permute-start(bf16[1,8,1,128]{3,1,2,0:T(8,128)(2,1)S(1)} %get-tuple-element.290), channel_id=1, source_target_pairs={{4,0},{8,4},{12,8},{16,12},{20,16},{24,20},{28,24},{32,28},{36,32}... | collective-permute-start | bytes 6152 | tf_op jit(solution)/shard_map/ppermute | solution.py:17
  24.7 1.9 collective-permute-start
  35.9 6.8 %collective-permute-start.3 = (bf16[1,8,1,128]{3,1,2,0:T(8,128)(2,1)S(1)}, bf16[1,8,1,128]{3,1,2,0:T(8,128)(2,1)S(1)}, u32[]{:S(2)}, u32[]{:S(2)}) collective-permute-start(bf16[1,8,1,128]{3,1,2,0:T(8,128)(2,1)S(1)} %get-tuple-element.286), channel_id=1, source_target_pairs={{4,0},{8,4},{12,8},{16,12},{20,16},{24,20},{28,24},{32,28},{36,32}... | collective-permute-start | bytes 6152 | tf_op jit(solution)/shard_map/ppermute | solution.py:17
  42.7 1.9 collective-permute-start.2
  44.7 6.5 %collective-permute-done.2 = bf16[1,8,1,128]{3,1,2,0:T(8,128)(2,1)S(1)} collective-permute-done((bf16[1,8,1,128]{3,1,2,0:T(8,128)(2,1)S(1)}, bf16[1,8,1,128]{3,1,2,0:T(8,128)(2,1)S(1)}, u32[]{:S(2)}, u32[]{:S(2)}) %collective-permute-start.2) | collective-permute-done | bytes 2080 | tf_op jit(solution)/shard_map/ppermute | solution.py:16
  53.1 6.9 %collective-permute-start.4 = (bf16[1,8,32,128]{3,1,2,0:T(8,128)(2,1)S(1)}, bf16[1,8,32,128]{3,1,2,0:T(8,128)(2,1)S(1)}, u32[]{:S(2)}, u32[]{:S(2)}) collective-permute-start(bf16[1,8,32,128]{3,1,2,0:T(8,128)(2,1)S(1)} %fusion.128), channel_id=1, source_target_pairs={{0,1},{1,2},{2,3},{4,5},{5,6},{6,7},{8,9},{9,10},{10,11},{12,13},{... | collective-permute-start | bytes 196616 | tf_op jit(solution)/shard_map/ppermute | solution.py:25
  61.4 1.9 collective-permute-start.6
  63.4 3.4 collective-permute-start.5
  66.8 5.1 %collective-permute-done.5 = bf16[1,8,1,128]{3,1,2,0:T(8,128)(2,1)S(1)} collective-permute-done((bf16[1,8,1,128]{3,1,2,0:T(8,128)(2,1)S(1)}, bf16[1,8,1,128]{3,1,2,0:T(8,128)(2,1)S(1)}, u32[]{:S(2)}, u32[]{:S(2)}) %collective-permute-start.5) | collective-permute-done | bytes 2080 | tf_op jit(solution)/shard_map/ppermute | solution.py:16
  73.7 1.9 collective-permute-start.8
  75.6 3.4 collective-permute-start.7
  79.1 5.1 %collective-permute-done.7 = bf16[1,8,1,128]{3,1,2,0:T(8,128)(2,1)S(1)} collective-permute-done((bf16[1,8,1,128]{3,1,2,0:T(8,128)(2,1)S(1)}, bf16[1,8,1,128]{3,1,2,0:T(8,128)(2,1)S(1)}, u32[]{:S(2)}, u32[]{:S(2)}) %collective-permute-start.7) | collective-permute-done | bytes 2080 | tf_op jit(solution)/shard_map/ppermute | solution.py:16
  85.9 8.1 %collective-permute-start.9 = (bf16[1,8,32,128]{3,1,2,0:T(8,128)(2,1)S(1)}, bf16[1,8,32,128]{3,1,2,0:T(8,128)(2,1)S(1)}, u32[]{:S(2)}, u32[]{:S(2)}) collective-permute-start(bf16[1,8,32,128]{3,1,2,0:T(8,128)(2,1)S(1)} %fusion.127), channel_id=1, source_target_pairs={{0,1},{1,2},{2,3},{4,5},{5,6},{6,7},{8,9},{9,10},{10,11},{12,13},{... | collective-permute-start | bytes 196616 | tf_op jit(solution)/shard_map/ppermute | solution.py:25
  95.4 1.9 collective-permute-start.11
  97.3 3.4 collective-permute-start.10
  100.8 5.1 %collective-permute-done.10 = bf16[1,8,1,128]{3,1,2,0:T(8,128)(2,1)S(1)} collective-permute-done((bf16[1,8,1,128]{3,1,2,0:T(8,128)(2,1)S(1)}, bf16[1,8,1,128]{3,1,2,0:T(8,128)(2,1)S(1)}, u32[]{:S(2)}, u32[]{:S(2)}) %collective-permute-start.10) | collective-permute-done | bytes 2080 | tf_op jit(solution)/shard_map/ppermute | solution.py:16
  107.6 1.9 collective-permute-start.13
  109.5 3.4 collective-permute-start.12
  113.0 5.1 %collective-permute-done.12 = bf16[1,8,1,128]{3,1,2,0:T(8,128)(2,1)S(1)} collective-permute-done((bf16[1,8,1,128]{3,1,2,0:T(8,128)(2,1)S(1)}, bf16[1,8,1,128]{3,1,2,0:T(8,128)(2,1)S(1)}, u32[]{:S(2)}, u32[]{:S(2)}) %collective-permute-start.12) | collective-permute-done | bytes 2080 | tf_op jit(solution)/shard_map/ppermute | solution.py:16
  119.9 8.1 %collective-permute-start.14 = (bf16[1,8,32,128]{3,1,2,0:T(8,128)(2,1)S(1)}, bf16[1,8,32,128]{3,1,2,0:T(8,128)(2,1)S(1)}, u32[]{:S(2)}, u32[]{:S(2)}) collective-permute-start(bf16[1,8,32,128]{3,1,2,0:T(8,128)(2,1)S(1)} %fusion.126), channel_id=1, source_target_pairs={{0,1},{1,2},{2,3},{4,5},{5,6},{6,7},{8,9},{9,10},{10,11},{12,13},{... | collective-permute-start | bytes 196616 | tf_op jit(solution)/shard_map/ppermute | solution.py:25
  129.3 1.9 collective-permute-start.16
  131.2 3.4 collective-permute-start.15
  134.7 5.1 %collective-permute-done.15 = bf16[1,8,1,128]{3,1,2,0:T(8,128)(2,1)S(1)} collective-permute-done((bf16[1,8,1,128]{3,1,2,0:T(8,128)(2,1)S(1)}, bf16[1,8,1,128]{3,1,2,0:T(8,128)(2,1)S(1)}, u32[]{:S(2)}, u32[]{:S(2)}) %collective-permute-start.15) | collective-permute-done | bytes 2080 | tf_op jit(solution)/shard_map/ppermute | solution.py:16
  141.5 1.9 collective-permute-start.18
  143.5 3.4 collective-permute-start.17
  146.9 5.1 %collective-permute-done.17 = bf16[1,8,1,128]{3,1,2,0:T(8,128)(2,1)S(1)} collective-permute-done((bf16[1,8,1,128]{3,1,2,0:T(8,128)(2,1)S(1)}, bf16[1,8,1,128]{3,1,2,0:T(8,128)(2,1)S(1)}, u32[]{:S(2)}, u32[]{:S(2)}) %collective-permute-start.17) | collective-permute-done | bytes 2080 | tf_op jit(solution)/shard_map/ppermute | solution.py:16
  153.8 8.1 %collective-permute-start.19 = (bf16[1,8,32,128]{3,1,2,0:T(8,128)(2,1)S(1)}, bf16[1,8,32,128]{3,1,2,0:T(8,128)(2,1)S(1)}, u32[]{:S(2)}, u32[]{:S(2)}) collective-permute-start(bf16[1,8,32,128]{3,1,2,0:T(8,128)(2,1)S(1)} %fusion.125), channel_id=1, source_target_pairs={{0,1},{1,2},{2,3},{4,5},{5,6},{6,7},{8,9},{9,10},{10,11},{12,13},{... | collective-permute-start | bytes 196616 | tf_op jit(solution)/shard_map/ppermute | solution.py:25
  163.2 1.9 collective-permute-start.21
  165.2 3.4 collective-permute-start.20
  168.6 5.1 %collective-permute-done.20 = bf16[1,8,1,128]{3,1,2,0:T(8,128)(2,1)S(1)} collective-permute-done((bf16[1,8,1,128]{3,1,2,0:T(8,128)(2,1)S(1)}, bf16[1,8,1,128]{3,1,2,0:T(8,128)(2,1)S(1)}, u32[]{:S(2)}, u32[]{:S(2)}) %collective-permute-start.20) | collective-permute-done | bytes 2080 | tf_op jit(solution)/shard_map/ppermute | solution.py:16
  175.5 1.9 collective-permute-start.23
  178.0 3.4 collective-permute-start.22
  181.5 5.1 %collective-permute-done.22 = bf16[1,8,1,128]{3,1,2,0:T(8,128)(2,1)S(1)} collective-permute-done((bf16[1,8,1,128]{3,1,2,0:T(8,128)(2,1)S(1)}, bf16[1,8,1,128]{3,1,2,0:T(8,128)(2,1)S(1)}, u32[]{:S(2)}, u32[]{:S(2)}) %collective-permute-start.22) | collective-permute-done | bytes 2080 | tf_op jit(solution)/shard_map/ppermute | solution.py:16
  189.1 52.2 %all-reduce.27.cloned.1.call-done = (bf16[2,8,32,128]{3,1,2,0:T(8,128)(2,1)}, bf16[2,8,32,128]{3,1,2,0:T(8,128)(2,1)}) async-done(((bf16[2,8,32,128]{3,1,2,0:T(8,128)(2,1)}, bf16[2,8,32,128]{3,1,2,0:T(8,128)(2,1)}), (bf16[2,8,32,128]{3,1,2,0:T(8,128)(2,1)}, bf16[2,8,32,128]{3,1,2,0:T(8,128)(2,1)})) %all-reduce.27.cloned.1.call-update) | async-done | bytes 262160 | tf_op jit(solution)/shard_map/psum | solution.py:30
  242.3 7.9 %collective-permute-start.25 = (bf16[1,8,1,128]{3,1,2,0:T(8,128)(2,1)S(1)}, bf16[1,8,1,128]{3,1,2,0:T(8,128)(2,1)S(1)}, u32[]{:S(2)}, u32[]{:S(2)}) collective-permute-start(bf16[1,8,1,128]{3,1,2,0:T(8,128)(2,1)S(1)} %get-tuple-element.250), channel_id=1, source_target_pairs={{4,0},{8,4},{12,8},{16,12},{20,16},{24,20},{28,24},{32,28},{36,32}... | collective-permute-start | bytes 6152 | tf_op jit(solution)/shard_map/ppermute | solution.py:17
  250.2 1.9 collective-permute-start.24
  252.2 6.5 %collective-permute-done.24 = bf16[1,8,1,128]{3,1,2,0:T(8,128)(2,1)S(1)} collective-permute-done((bf16[1,8,1,128]{3,1,2,0:T(8,128)(2,1)S(1)}, bf16[1,8,1,128]{3,1,2,0:T(8,128)(2,1)S(1)}, u32[]{:S(2)}, u32[]{:S(2)}) %collective-permute-start.24) | collective-permute-done | bytes 2080 | tf_op jit(solution)/shard_map/ppermute | solution.py:16
  262.4 3.4 collective-permute-start.26
  265.9 5.1 %collective-permute-done.26 = bf16[1,8,1,128]{3,1,2,0:T(8,128)(2,1)S(1)} collective-permute-done((bf16[1,8,1,128]{3,1,2,0:T(8,128)(2,1)S(1)}, bf16[1,8,1,128]{3,1,2,0:T(8,128)(2,1)S(1)}, u32[]{:S(2)}, u32[]{:S(2)}) %collective-permute-start.26) | collective-permute-done | bytes 2080 | tf_op jit(solution)/shard_map/ppermute | solution.py:16
  273.5 6.3 %collective-permute-start.28 = (bf16[1,8,32,128]{3,1,2,0:T(8,128)(2,1)S(1)}, bf16[1,8,32,128]{3,1,2,0:T(8,128)(2,1)S(1)}, u32[]{:S(2)}, u32[]{:S(2)}) collective-permute-start(bf16[1,8,32,128]{3,1,2,0:T(8,128)(2,1)S(1)} %fusion.123), channel_id=1, source_target_pairs={{0,1},{1,2},{2,3},{4,5},{5,6},{6,7},{8,9},{9,10},{10,11},{12,13},{... | collective-permute-start | bytes 196616 | tf_op jit(solution)/shard_map/ppermute | solution.py:25
  283.3 3.4 collective-permute-start.29
  286.7 5.1 %collective-permute-done.29 = bf16[1,8,1,128]{3,1,2,0:T(8,128)(2,1)S(1)} collective-permute-done((bf16[1,8,1,128]{3,1,2,0:T(8,128)(2,1)S(1)}, bf16[1,8,1,128]{3,1,2,0:T(8,128)(2,1)S(1)}, u32[]{:S(2)}, u32[]{:S(2)}) %collective-permute-start.29) | collective-permute-done | bytes 2080 | tf_op jit(solution)/shard_map/ppermute | solution.py:16
  295.5 3.5 collective-permute-start.31
  299.1 4.9 %collective-permute-done.31 = bf16[1,8,1,128]{3,1,2,0:T(8,128)(2,1)S(1)} collective-permute-done((bf16[1,8,1,128]{3,1,2,0:T(8,128)(2,1)S(1)}, bf16[1,8,1,128]{3,1,2,0:T(8,128)(2,1)S(1)}, u32[]{:S(2)}, u32[]{:S(2)}) %collective-permute-start.31) | collective-permute-done | bytes 2080 | tf_op jit(solution)/shard_map/ppermute | solution.py:16
  305.8 8.1 %collective-permute-start.33 = (bf16[1,8,32,128]{3,1,2,0:T(8,128)(2,1)S(1)}, bf16[1,8,32,128]{3,1,2,0:T(8,128)(2,1)S(1)}, u32[]{:S(2)}, u32[]{:S(2)}) collective-permute-start(bf16[1,8,32,128]{3,1,2,0:T(8,128)(2,1)S(1)} %fusion.122), channel_id=1, source_target_pairs={{0,1},{1,2},{2,3},{4,5},{5,6},{6,7},{8,9},{9,10},{10,11},{12,13},{... | collective-permute-start | bytes 196616 | tf_op jit(solution)/shard_map/ppermute | solution.py:25
  317.2 3.4 collective-permute-start.34
  320.6 5.1 %collective-permute-done.34 = bf16[1,8,1,128]{3,1,2,0:T(8,128)(2,1)S(1)} collective-permute-done((bf16[1,8,1,128]{3,1,2,0:T(8,128)(2,1)S(1)}, bf16[1,8,1,128]{3,1,2,0:T(8,128)(2,1)S(1)}, u32[]{:S(2)}, u32[]{:S(2)}) %collective-permute-start.34) | collective-permute-done | bytes 2080 | tf_op jit(solution)/shard_map/ppermute | solution.py:16
  327.5 1.9 collective-permute-start.37
  329.4 3.4 collective-permute-start.36
  332.9 5.1 %collective-permute-done.36 = bf16[1,8,1,128]{3,1,2,0:T(8,128)(2,1)S(1)} collective-permute-done((bf16[1,8,1,128]{3,1,2,0:T(8,128)(2,1)S(1)}, bf16[1,8,1,128]{3,1,2,0:T(8,128)(2,1)S(1)}, u32[]{:S(2)}, u32[]{:S(2)}) %collective-permute-start.36) | collective-permute-done | bytes 2080 | tf_op jit(solution)/shard_map/ppermute | solution.py:16
  339.7 8.1 %collective-permute-start.38 = (bf16[1,8,32,128]{3,1,2,0:T(8,128)(2,1)S(1)}, bf16[1,8,32,128]{3,1,2,0:T(8,128)(2,1)S(1)}, u32[]{:S(2)}, u32[]{:S(2)}) collective-permute-start(bf16[1,8,32,128]{3,1,2,0:T(8,128)(2,1)S(1)} %fusion.121), channel_id=1, source_target_pairs={{0,1},{1,2},{2,3},{4,5},{5,6},{6,7},{8,9},{9,10},{10,11},{12,13},{... | collective-permute-start | bytes 196616 | tf_op jit(solution)/shard_map/ppermute | solution.py:25
  349.1 1.9 collective-permute-start.40
  351.1 3.4 collective-permute-start.39
  354.5 5.1 %collective-permute-done.39 = bf16[1,8,1,128]{3,1,2,0:T(8,128)(2,1)S(1)} collective-permute-done((bf16[1,8,1,128]{3,1,2,0:T(8,128)(2,1)S(1)}, bf16[1,8,1,128]{3,1,2,0:T(8,128)(2,1)S(1)}, u32[]{:S(2)}, u32[]{:S(2)}) %collective-permute-start.39) | collective-permute-done | bytes 2080 | tf_op jit(solution)/shard_map/ppermute | solution.py:16
  361.4 1.9 collective-permute-start.42
  363.3 3.4 collective-permute-start.41
  366.8 5.1 %collective-permute-done.41 = bf16[1,8,1,128]{3,1,2,0:T(8,128)(2,1)S(1)} collective-permute-done((bf16[1,8,1,128]{3,1,2,0:T(8,128)(2,1)S(1)}, bf16[1,8,1,128]{3,1,2,0:T(8,128)(2,1)S(1)}, u32[]{:S(2)}, u32[]{:S(2)}) %collective-permute-start.41) | collective-permute-done | bytes 2080 | tf_op jit(solution)/shard_map/ppermute | solution.py:16
  373.6 8.1 %collective-permute-start.43 = (bf16[1,8,32,128]{3,1,2,0:T(8,128)(2,1)S(1)}, bf16[1,8,32,128]{3,1,2,0:T(8,128)(2,1)S(1)}, u32[]{:S(2)}, u32[]{:S(2)}) collective-permute-start(bf16[1,8,32,128]{3,1,2,0:T(8,128)(2,1)S(1)} %fusion.120), channel_id=1, source_target_pairs={{0,1},{1,2},{2,3},{4,5},{5,6},{6,7},{8,9},{9,10},{10,11},{12,13},{... | collective-permute-start | bytes 196616 | tf_op jit(solution)/shard_map/ppermute | solution.py:25
  385.0 3.4 collective-permute-start.44
  388.4 5.1 %collective-permute-done.44 = bf16[1,8,1,128]{3,1,2,0:T(8,128)(2,1)S(1)} collective-permute-done((bf16[1,8,1,128]{3,1,2,0:T(8,128)(2,1)S(1)}, bf16[1,8,1,128]{3,1,2,0:T(8,128)(2,1)S(1)}, u32[]{:S(2)}, u32[]{:S(2)}) %collective-permute-start.44) | collective-permute-done | bytes 2080 | tf_op jit(solution)/shard_map/ppermute | solution.py:16
  395.3 1.9 collective-permute-start.47
  397.9 3.4 collective-permute-start.46
  401.3 5.1 %collective-permute-done.46 = bf16[1,8,1,128]{3,1,2,0:T(8,128)(2,1)S(1)} collective-permute-done((bf16[1,8,1,128]{3,1,2,0:T(8,128)(2,1)S(1)}, bf16[1,8,1,128]{3,1,2,0:T(8,128)(2,1)S(1)}, u32[]{:S(2)}, u32[]{:S(2)}) %collective-permute-start.46) | collective-permute-done | bytes 2080 | tf_op jit(solution)/shard_map/ppermute | solution.py:16
  408.9 55.1 %all-reduce.25.cloned.1.call-done = (bf16[2,8,32,128]{3,1,2,0:T(8,128)(2,1)}, bf16[2,8,32,128]{3,1,2,0:T(8,128)(2,1)}) async-done(((bf16[2,8,32,128]{3,1,2,0:T(8,128)(2,1)}, bf16[2,8,32,128]{3,1,2,0:T(8,128)(2,1)}), (bf16[2,8,32,128]{3,1,2,0:T(8,128)(2,1)}, bf16[2,8,32,128]{3,1,2,0:T(8,128)(2,1)})) %all-reduce.25.cloned.1.call-update) | async-done | bytes 262160 | tf_op jit(solution)/shard_map/psum | solution.py:30
  (391 shorter events, 68.4 us)
Async XLA Ops:
  7.2 234.1 %all-reduce.27.cloned.1.call-start = ((), (), s32[]{:S(2)}) async-start(), calls=%async_computation.1 | async-start | bytes 524288 | tf_op jit(solution)/shard_map/psum | solution.py:30
  7.2 0.7 copy-start.3
  9.4 17.3 %copy-start.4 = (s32[1,2]{1,0:T(1,128)S(1)}, s32[1,2]{1,0:T(1,128)}, u32[]{:S(2)}) copy-start(s32[1,2]{1,0:T(1,128)} %param.8) | copy-start | bytes 28
  9.4 23.1 %collective-permute-start.1 = (bf16[1,8,1,128]{3,1,2,0:T(8,128)(2,1)S(1)}, bf16[1,8,1,128]{3,1,2,0:T(8,128)(2,1)S(1)}, u32[]{:S(2)}, u32[]{:S(2)}) collective-permute-start(bf16[1,8,1,128]{3,1,2,0:T(8,128)(2,1)S(1)} %get-tuple-element.290), channel_id=1, source_target_pairs={{4,0},{8,4},{12,8},{16,12},{20,16},{24,20},{28,24},{32,28},{36,32}... | collective-permute-start | bytes 6152 | tf_op jit(solution)/shard_map/ppermute | solution.py:17
  24.7 8.5 %collective-permute-start = (bf16[1,8,1,128]{3,1,2,0:T(8,128)(2,1)S(1)}, bf16[1,8,1,128]{3,1,2,0:T(8,128)(2,1)S(1)}, u32[]{:S(2)}, u32[]{:S(2)}) collective-permute-start(bf16[1,8,1,128]{3,1,2,0:T(8,128)(2,1)S(1)} %get-tuple-element.289), channel_id=1, source_target_pairs={{0,4},{4,8},{8,12},{12,16},{16,20},{20,24},{24,28},{28,32},{32,36}... | collective-permute-start | bytes 6152 | tf_op jit(solution)/shard_map/ppermute | solution.py:16
  33.3 1.1 copy-start
  35.9 8.8 %collective-permute-start.3 = (bf16[1,8,1,128]{3,1,2,0:T(8,128)(2,1)S(1)}, bf16[1,8,1,128]{3,1,2,0:T(8,128)(2,1)S(1)}, u32[]{:S(2)}, u32[]{:S(2)}) collective-permute-start(bf16[1,8,1,128]{3,1,2,0:T(8,128)(2,1)S(1)} %get-tuple-element.286), channel_id=1, source_target_pairs={{4,0},{8,4},{12,8},{16,12},{20,16},{24,20},{28,24},{32,28},{36,32}... | collective-permute-start | bytes 6152 | tf_op jit(solution)/shard_map/ppermute | solution.py:17
  42.7 8.5 %collective-permute-start.2 = (bf16[1,8,1,128]{3,1,2,0:T(8,128)(2,1)S(1)}, bf16[1,8,1,128]{3,1,2,0:T(8,128)(2,1)S(1)}, u32[]{:S(2)}, u32[]{:S(2)}) collective-permute-start(bf16[1,8,1,128]{3,1,2,0:T(8,128)(2,1)S(1)} %get-tuple-element.285), channel_id=1, source_target_pairs={{0,4},{4,8},{8,12},{12,16},{16,20},{20,24},{24,28},{28,32},{32,36}... | collective-permute-start | bytes 6152 | tf_op jit(solution)/shard_map/ppermute | solution.py:16
  53.1 8.2 %collective-permute-start.4 = (bf16[1,8,32,128]{3,1,2,0:T(8,128)(2,1)S(1)}, bf16[1,8,32,128]{3,1,2,0:T(8,128)(2,1)S(1)}, u32[]{:S(2)}, u32[]{:S(2)}) collective-permute-start(bf16[1,8,32,128]{3,1,2,0:T(8,128)(2,1)S(1)} %fusion.128), channel_id=1, source_target_pairs={{0,1},{1,2},{2,3},{4,5},{5,6},{6,7},{8,9},{9,10},{10,11},{12,13},{... | collective-permute-start | bytes 196616 | tf_op jit(solution)/shard_map/ppermute | solution.py:25
  61.4 5.3 %collective-permute-start.6 = (bf16[1,8,1,128]{3,1,2,0:T(8,128)(2,1)S(1)}, bf16[1,8,1,128]{3,1,2,0:T(8,128)(2,1)S(1)}, u32[]{:S(2)}, u32[]{:S(2)}) collective-permute-start(bf16[1,8,1,128]{3,1,2,0:T(8,128)(2,1)S(1)} %get-tuple-element.282), channel_id=1, source_target_pairs={{4,0},{8,4},{12,8},{16,12},{20,16},{24,20},{28,24},{32,28},{36,32}... | collective-permute-start | bytes 6152 | tf_op jit(solution)/shard_map/ppermute | solution.py:17
  63.4 8.5 %collective-permute-start.5 = (bf16[1,8,1,128]{3,1,2,0:T(8,128)(2,1)S(1)}, bf16[1,8,1,128]{3,1,2,0:T(8,128)(2,1)S(1)}, u32[]{:S(2)}, u32[]{:S(2)}) collective-permute-start(bf16[1,8,1,128]{3,1,2,0:T(8,128)(2,1)S(1)} %get-tuple-element.281), channel_id=1, source_target_pairs={{0,4},{4,8},{8,12},{12,16},{16,20},{20,24},{24,28},{28,32},{32,36}... | collective-permute-start | bytes 6152 | tf_op jit(solution)/shard_map/ppermute | solution.py:16
  73.7 5.3 %collective-permute-start.8 = (bf16[1,8,1,128]{3,1,2,0:T(8,128)(2,1)S(1)}, bf16[1,8,1,128]{3,1,2,0:T(8,128)(2,1)S(1)}, u32[]{:S(2)}, u32[]{:S(2)}) collective-permute-start(bf16[1,8,1,128]{3,1,2,0:T(8,128)(2,1)S(1)} %get-tuple-element.278), channel_id=1, source_target_pairs={{4,0},{8,4},{12,8},{16,12},{20,16},{24,20},{28,24},{32,28},{36,32}... | collective-permute-start | bytes 6152 | tf_op jit(solution)/shard_map/ppermute | solution.py:17
  75.6 8.5 %collective-permute-start.7 = (bf16[1,8,1,128]{3,1,2,0:T(8,128)(2,1)S(1)}, bf16[1,8,1,128]{3,1,2,0:T(8,128)(2,1)S(1)}, u32[]{:S(2)}, u32[]{:S(2)}) collective-permute-start(bf16[1,8,1,128]{3,1,2,0:T(8,128)(2,1)S(1)} %get-tuple-element.277), channel_id=1, source_target_pairs={{0,4},{4,8},{8,12},{12,16},{16,20},{20,24},{24,28},{28,32},{32,36}... | collective-permute-start | bytes 6152 | tf_op jit(solution)/shard_map/ppermute | solution.py:16
  85.9 9.4 %collective-permute-start.9 = (bf16[1,8,32,128]{3,1,2,0:T(8,128)(2,1)S(1)}, bf16[1,8,32,128]{3,1,2,0:T(8,128)(2,1)S(1)}, u32[]{:S(2)}, u32[]{:S(2)}) collective-permute-start(bf16[1,8,32,128]{3,1,2,0:T(8,128)(2,1)S(1)} %fusion.127), channel_id=1, source_target_pairs={{0,1},{1,2},{2,3},{4,5},{5,6},{6,7},{8,9},{9,10},{10,11},{12,13},{... | collective-permute-start | bytes 196616 | tf_op jit(solution)/shard_map/ppermute | solution.py:25
  95.4 5.3 %collective-permute-start.11 = (bf16[1,8,1,128]{3,1,2,0:T(8,128)(2,1)S(1)}, bf16[1,8,1,128]{3,1,2,0:T(8,128)(2,1)S(1)}, u32[]{:S(2)}, u32[]{:S(2)}) collective-permute-start(bf16[1,8,1,128]{3,1,2,0:T(8,128)(2,1)S(1)} %get-tuple-element.274), channel_id=1, source_target_pairs={{4,0},{8,4},{12,8},{16,12},{20,16},{24,20},{28,24},{32,28},{36,32}... | collective-permute-start | bytes 6152 | tf_op jit(solution)/shard_map/ppermute | solution.py:17
  97.3 8.5 %collective-permute-start.10 = (bf16[1,8,1,128]{3,1,2,0:T(8,128)(2,1)S(1)}, bf16[1,8,1,128]{3,1,2,0:T(8,128)(2,1)S(1)}, u32[]{:S(2)}, u32[]{:S(2)}) collective-permute-start(bf16[1,8,1,128]{3,1,2,0:T(8,128)(2,1)S(1)} %get-tuple-element.273), channel_id=1, source_target_pairs={{0,4},{4,8},{8,12},{12,16},{16,20},{20,24},{24,28},{28,32},{32,36}... | collective-permute-start | bytes 6152 | tf_op jit(solution)/shard_map/ppermute | solution.py:16
  107.6 5.3 %collective-permute-start.13 = (bf16[1,8,1,128]{3,1,2,0:T(8,128)(2,1)S(1)}, bf16[1,8,1,128]{3,1,2,0:T(8,128)(2,1)S(1)}, u32[]{:S(2)}, u32[]{:S(2)}) collective-permute-start(bf16[1,8,1,128]{3,1,2,0:T(8,128)(2,1)S(1)} %get-tuple-element.270), channel_id=1, source_target_pairs={{4,0},{8,4},{12,8},{16,12},{20,16},{24,20},{28,24},{32,28},{36,32}... | collective-permute-start | bytes 6152 | tf_op jit(solution)/shard_map/ppermute | solution.py:17
  109.5 8.5 %collective-permute-start.12 = (bf16[1,8,1,128]{3,1,2,0:T(8,128)(2,1)S(1)}, bf16[1,8,1,128]{3,1,2,0:T(8,128)(2,1)S(1)}, u32[]{:S(2)}, u32[]{:S(2)}) collective-permute-start(bf16[1,8,1,128]{3,1,2,0:T(8,128)(2,1)S(1)} %get-tuple-element.269), channel_id=1, source_target_pairs={{0,4},{4,8},{8,12},{12,16},{16,20},{20,24},{24,28},{28,32},{32,36}... | collective-permute-start | bytes 6152 | tf_op jit(solution)/shard_map/ppermute | solution.py:16
  119.9 9.4 %collective-permute-start.14 = (bf16[1,8,32,128]{3,1,2,0:T(8,128)(2,1)S(1)}, bf16[1,8,32,128]{3,1,2,0:T(8,128)(2,1)S(1)}, u32[]{:S(2)}, u32[]{:S(2)}) collective-permute-start(bf16[1,8,32,128]{3,1,2,0:T(8,128)(2,1)S(1)} %fusion.126), channel_id=1, source_target_pairs={{0,1},{1,2},{2,3},{4,5},{5,6},{6,7},{8,9},{9,10},{10,11},{12,13},{... | collective-permute-start | bytes 196616 | tf_op jit(solution)/shard_map/ppermute | solution.py:25
  129.3 5.3 %collective-permute-start.16 = (bf16[1,8,1,128]{3,1,2,0:T(8,128)(2,1)S(1)}, bf16[1,8,1,128]{3,1,2,0:T(8,128)(2,1)S(1)}, u32[]{:S(2)}, u32[]{:S(2)}) collective-permute-start(bf16[1,8,1,128]{3,1,2,0:T(8,128)(2,1)S(1)} %get-tuple-element.266), channel_id=1, source_target_pairs={{4,0},{8,4},{12,8},{16,12},{20,16},{24,20},{28,24},{32,28},{36,32}... | collective-permute-start | bytes 6152 | tf_op jit(solution)/shard_map/ppermute | solution.py:17
  131.2 8.5 %collective-permute-start.15 = (bf16[1,8,1,128]{3,1,2,0:T(8,128)(2,1)S(1)}, bf16[1,8,1,128]{3,1,2,0:T(8,128)(2,1)S(1)}, u32[]{:S(2)}, u32[]{:S(2)}) collective-permute-start(bf16[1,8,1,128]{3,1,2,0:T(8,128)(2,1)S(1)} %get-tuple-element.265), channel_id=1, source_target_pairs={{0,4},{4,8},{8,12},{12,16},{16,20},{20,24},{24,28},{28,32},{32,36}... | collective-permute-start | bytes 6152 | tf_op jit(solution)/shard_map/ppermute | solution.py:16
  141.5 5.3 %collective-permute-start.18 = (bf16[1,8,1,128]{3,1,2,0:T(8,128)(2,1)S(1)}, bf16[1,8,1,128]{3,1,2,0:T(8,128)(2,1)S(1)}, u32[]{:S(2)}, u32[]{:S(2)}) collective-permute-start(bf16[1,8,1,128]{3,1,2,0:T(8,128)(2,1)S(1)} %get-tuple-element.262), channel_id=1, source_target_pairs={{4,0},{8,4},{12,8},{16,12},{20,16},{24,20},{28,24},{32,28},{36,32}... | collective-permute-start | bytes 6152 | tf_op jit(solution)/shard_map/ppermute | solution.py:17
  143.5 8.5 %collective-permute-start.17 = (bf16[1,8,1,128]{3,1,2,0:T(8,128)(2,1)S(1)}, bf16[1,8,1,128]{3,1,2,0:T(8,128)(2,1)S(1)}, u32[]{:S(2)}, u32[]{:S(2)}) collective-permute-start(bf16[1,8,1,128]{3,1,2,0:T(8,128)(2,1)S(1)} %get-tuple-element.261), channel_id=1, source_target_pairs={{0,4},{4,8},{8,12},{12,16},{16,20},{20,24},{24,28},{28,32},{32,36}... | collective-permute-start | bytes 6152 | tf_op jit(solution)/shard_map/ppermute | solution.py:16
  153.8 9.4 %collective-permute-start.19 = (bf16[1,8,32,128]{3,1,2,0:T(8,128)(2,1)S(1)}, bf16[1,8,32,128]{3,1,2,0:T(8,128)(2,1)S(1)}, u32[]{:S(2)}, u32[]{:S(2)}) collective-permute-start(bf16[1,8,32,128]{3,1,2,0:T(8,128)(2,1)S(1)} %fusion.125), channel_id=1, source_target_pairs={{0,1},{1,2},{2,3},{4,5},{5,6},{6,7},{8,9},{9,10},{10,11},{12,13},{... | collective-permute-start | bytes 196616 | tf_op jit(solution)/shard_map/ppermute | solution.py:25
  163.2 5.3 %collective-permute-start.21 = (bf16[1,8,1,128]{3,1,2,0:T(8,128)(2,1)S(1)}, bf16[1,8,1,128]{3,1,2,0:T(8,128)(2,1)S(1)}, u32[]{:S(2)}, u32[]{:S(2)}) collective-permute-start(bf16[1,8,1,128]{3,1,2,0:T(8,128)(2,1)S(1)} %get-tuple-element.258), channel_id=1, source_target_pairs={{4,0},{8,4},{12,8},{16,12},{20,16},{24,20},{28,24},{32,28},{36,32}... | collective-permute-start | bytes 6152 | tf_op jit(solution)/shard_map/ppermute | solution.py:17
  165.2 8.5 %collective-permute-start.20 = (bf16[1,8,1,128]{3,1,2,0:T(8,128)(2,1)S(1)}, bf16[1,8,1,128]{3,1,2,0:T(8,128)(2,1)S(1)}, u32[]{:S(2)}, u32[]{:S(2)}) collective-permute-start(bf16[1,8,1,128]{3,1,2,0:T(8,128)(2,1)S(1)} %get-tuple-element.257), channel_id=1, source_target_pairs={{0,4},{4,8},{8,12},{12,16},{16,20},{20,24},{24,28},{28,32},{32,36}... | collective-permute-start | bytes 6152 | tf_op jit(solution)/shard_map/ppermute | solution.py:16
  175.5 6.0 %collective-permute-start.23 = (bf16[1,8,1,128]{3,1,2,0:T(8,128)(2,1)S(1)}, bf16[1,8,1,128]{3,1,2,0:T(8,128)(2,1)S(1)}, u32[]{:S(2)}, u32[]{:S(2)}) collective-permute-start(bf16[1,8,1,128]{3,1,2,0:T(8,128)(2,1)S(1)} %get-tuple-element.254), channel_id=1, source_target_pairs={{4,0},{8,4},{12,8},{16,12},{20,16},{24,20},{28,24},{32,28},{36,32}... | collective-permute-start | bytes 6152 | tf_op jit(solution)/shard_map/ppermute | solution.py:17
  178.0 8.5 %collective-permute-start.22 = (bf16[1,8,1,128]{3,1,2,0:T(8,128)(2,1)S(1)}, bf16[1,8,1,128]{3,1,2,0:T(8,128)(2,1)S(1)}, u32[]{:S(2)}, u32[]{:S(2)}) collective-permute-start(bf16[1,8,1,128]{3,1,2,0:T(8,128)(2,1)S(1)} %get-tuple-element.253), channel_id=1, source_target_pairs={{0,4},{4,8},{8,12},{12,16},{16,20},{20,24},{24,28},{28,32},{32,36}... | collective-permute-start | bytes 6152 | tf_op jit(solution)/shard_map/ppermute | solution.py:16
  189.1 274.9 %all-reduce.25.cloned.1.call-start = ((), (), s32[]{:S(2)}) async-start(), calls=%async_computation | async-start | bytes 524288 | tf_op jit(solution)/shard_map/psum | solution.py:30
  242.3 9.8 %collective-permute-start.25 = (bf16[1,8,1,128]{3,1,2,0:T(8,128)(2,1)S(1)}, bf16[1,8,1,128]{3,1,2,0:T(8,128)(2,1)S(1)}, u32[]{:S(2)}, u32[]{:S(2)}) collective-permute-start(bf16[1,8,1,128]{3,1,2,0:T(8,128)(2,1)S(1)} %get-tuple-element.250), channel_id=1, source_target_pairs={{4,0},{8,4},{12,8},{16,12},{20,16},{24,20},{28,24},{32,28},{36,32}... | collective-permute-start | bytes 6152 | tf_op jit(solution)/shard_map/ppermute | solution.py:17
  250.2 8.5 %collective-permute-start.24 = (bf16[1,8,1,128]{3,1,2,0:T(8,128)(2,1)S(1)}, bf16[1,8,1,128]{3,1,2,0:T(8,128)(2,1)S(1)}, u32[]{:S(2)}, u32[]{:S(2)}) collective-permute-start(bf16[1,8,1,128]{3,1,2,0:T(8,128)(2,1)S(1)} %get-tuple-element.249), channel_id=1, source_target_pairs={{0,4},{4,8},{8,12},{12,16},{16,20},{20,24},{24,28},{28,32},{32,36}... | collective-permute-start | bytes 6152 | tf_op jit(solution)/shard_map/ppermute | solution.py:16
  260.5 5.3 %collective-permute-start.27 = (bf16[1,8,1,128]{3,1,2,0:T(8,128)(2,1)S(1)}, bf16[1,8,1,128]{3,1,2,0:T(8,128)(2,1)S(1)}, u32[]{:S(2)}, u32[]{:S(2)}) collective-permute-start(bf16[1,8,1,128]{3,1,2,0:T(8,128)(2,1)S(1)} %get-tuple-element.246), channel_id=1, source_target_pairs={{4,0},{8,4},{12,8},{16,12},{20,16},{24,20},{28,24},{32,28},{36,32}... | collective-permute-start | bytes 6152 | tf_op jit(solution)/shard_map/ppermute | solution.py:17
  262.4 8.5 %collective-permute-start.26 = (bf16[1,8,1,128]{3,1,2,0:T(8,128)(2,1)S(1)}, bf16[1,8,1,128]{3,1,2,0:T(8,128)(2,1)S(1)}, u32[]{:S(2)}, u32[]{:S(2)}) collective-permute-start(bf16[1,8,1,128]{3,1,2,0:T(8,128)(2,1)S(1)} %get-tuple-element.245), channel_id=1, source_target_pairs={{0,4},{4,8},{8,12},{12,16},{16,20},{20,24},{24,28},{28,32},{32,36}... | collective-permute-start | bytes 6152 | tf_op jit(solution)/shard_map/ppermute | solution.py:16
  272.4 0.9 copy-start.1
  272.5 1.0 copy-start.2
  273.5 7.7 %collective-permute-start.28 = (bf16[1,8,32,128]{3,1,2,0:T(8,128)(2,1)S(1)}, bf16[1,8,32,128]{3,1,2,0:T(8,128)(2,1)S(1)}, u32[]{:S(2)}, u32[]{:S(2)}) collective-permute-start(bf16[1,8,32,128]{3,1,2,0:T(8,128)(2,1)S(1)} %fusion.123), channel_id=1, source_target_pairs={{0,1},{1,2},{2,3},{4,5},{5,6},{6,7},{8,9},{9,10},{10,11},{12,13},{... | collective-permute-start | bytes 196616 | tf_op jit(solution)/shard_map/ppermute | solution.py:25
  281.3 5.3 %collective-permute-start.30 = (bf16[1,8,1,128]{3,1,2,0:T(8,128)(2,1)S(1)}, bf16[1,8,1,128]{3,1,2,0:T(8,128)(2,1)S(1)}, u32[]{:S(2)}, u32[]{:S(2)}) collective-permute-start(bf16[1,8,1,128]{3,1,2,0:T(8,128)(2,1)S(1)} %get-tuple-element.242), channel_id=1, source_target_pairs={{4,0},{8,4},{12,8},{16,12},{20,16},{24,20},{28,24},{32,28},{36,32}... | collective-permute-start | bytes 6152 | tf_op jit(solution)/shard_map/ppermute | solution.py:17
  283.3 8.5 %collective-permute-start.29 = (bf16[1,8,1,128]{3,1,2,0:T(8,128)(2,1)S(1)}, bf16[1,8,1,128]{3,1,2,0:T(8,128)(2,1)S(1)}, u32[]{:S(2)}, u32[]{:S(2)}) collective-permute-start(bf16[1,8,1,128]{3,1,2,0:T(8,128)(2,1)S(1)} %get-tuple-element.241), channel_id=1, source_target_pairs={{0,4},{4,8},{8,12},{12,16},{16,20},{20,24},{24,28},{28,32},{32,36}... | collective-permute-start | bytes 6152 | tf_op jit(solution)/shard_map/ppermute | solution.py:16
  293.6 5.5 %collective-permute-start.32 = (bf16[1,8,1,128]{3,1,2,0:T(8,128)(2,1)S(1)}, bf16[1,8,1,128]{3,1,2,0:T(8,128)(2,1)S(1)}, u32[]{:S(2)}, u32[]{:S(2)}) collective-permute-start(bf16[1,8,1,128]{3,1,2,0:T(8,128)(2,1)S(1)} %get-tuple-element.238), channel_id=1, source_target_pairs={{4,0},{8,4},{12,8},{16,12},{20,16},{24,20},{28,24},{32,28},{36,32}... | collective-permute-start | bytes 6152 | tf_op jit(solution)/shard_map/ppermute | solution.py:17
  295.5 8.5 %collective-permute-start.31 = (bf16[1,8,1,128]{3,1,2,0:T(8,128)(2,1)S(1)}, bf16[1,8,1,128]{3,1,2,0:T(8,128)(2,1)S(1)}, u32[]{:S(2)}, u32[]{:S(2)}) collective-permute-start(bf16[1,8,1,128]{3,1,2,0:T(8,128)(2,1)S(1)} %get-tuple-element.237), channel_id=1, source_target_pairs={{0,4},{4,8},{8,12},{12,16},{16,20},{20,24},{24,28},{28,32},{32,36}... | collective-permute-start | bytes 6152 | tf_op jit(solution)/shard_map/ppermute | solution.py:16
  305.8 9.4 %collective-permute-start.33 = (bf16[1,8,32,128]{3,1,2,0:T(8,128)(2,1)S(1)}, bf16[1,8,32,128]{3,1,2,0:T(8,128)(2,1)S(1)}, u32[]{:S(2)}, u32[]{:S(2)}) collective-permute-start(bf16[1,8,32,128]{3,1,2,0:T(8,128)(2,1)S(1)} %fusion.122), channel_id=1, source_target_pairs={{0,1},{1,2},{2,3},{4,5},{5,6},{6,7},{8,9},{9,10},{10,11},{12,13},{... | collective-permute-start | bytes 196616 | tf_op jit(solution)/shard_map/ppermute | solution.py:25
  315.2 5.3 %collective-permute-start.35 = (bf16[1,8,1,128]{3,1,2,0:T(8,128)(2,1)S(1)}, bf16[1,8,1,128]{3,1,2,0:T(8,128)(2,1)S(1)}, u32[]{:S(2)}, u32[]{:S(2)}) collective-permute-start(bf16[1,8,1,128]{3,1,2,0:T(8,128)(2,1)S(1)} %get-tuple-element.234), channel_id=1, source_target_pairs={{4,0},{8,4},{12,8},{16,12},{20,16},{24,20},{28,24},{32,28},{36,32}... | collective-permute-start | bytes 6152 | tf_op jit(solution)/shard_map/ppermute | solution.py:17
  317.2 8.5 %collective-permute-start.34 = (bf16[1,8,1,128]{3,1,2,0:T(8,128)(2,1)S(1)}, bf16[1,8,1,128]{3,1,2,0:T(8,128)(2,1)S(1)}, u32[]{:S(2)}, u32[]{:S(2)}) collective-permute-start(bf16[1,8,1,128]{3,1,2,0:T(8,128)(2,1)S(1)} %get-tuple-element.233), channel_id=1, source_target_pairs={{0,4},{4,8},{8,12},{12,16},{16,20},{20,24},{24,28},{28,32},{32,36}... | collective-permute-start | bytes 6152 | tf_op jit(solution)/shard_map/ppermute | solution.py:16
  327.5 5.3 %collective-permute-start.37 = (bf16[1,8,1,128]{3,1,2,0:T(8,128)(2,1)S(1)}, bf16[1,8,1,128]{3,1,2,0:T(8,128)(2,1)S(1)}, u32[]{:S(2)}, u32[]{:S(2)}) collective-permute-start(bf16[1,8,1,128]{3,1,2,0:T(8,128)(2,1)S(1)} %get-tuple-element.230), channel_id=1, source_target_pairs={{4,0},{8,4},{12,8},{16,12},{20,16},{24,20},{28,24},{32,28},{36,32}... | collective-permute-start | bytes 6152 | tf_op jit(solution)/shard_map/ppermute | solution.py:17
  329.4 8.5 %collective-permute-start.36 = (bf16[1,8,1,128]{3,1,2,0:T(8,128)(2,1)S(1)}, bf16[1,8,1,128]{3,1,2,0:T(8,128)(2,1)S(1)}, u32[]{:S(2)}, u32[]{:S(2)}) collective-permute-start(bf16[1,8,1,128]{3,1,2,0:T(8,128)(2,1)S(1)} %get-tuple-element.229), channel_id=1, source_target_pairs={{0,4},{4,8},{8,12},{12,16},{16,20},{20,24},{24,28},{28,32},{32,36}... | collective-permute-start | bytes 6152 | tf_op jit(solution)/shard_map/ppermute | solution.py:16
  339.7 9.4 %collective-permute-start.38 = (bf16[1,8,32,128]{3,1,2,0:T(8,128)(2,1)S(1)}, bf16[1,8,32,128]{3,1,2,0:T(8,128)(2,1)S(1)}, u32[]{:S(2)}, u32[]{:S(2)}) collective-permute-start(bf16[1,8,32,128]{3,1,2,0:T(8,128)(2,1)S(1)} %fusion.121), channel_id=1, source_target_pairs={{0,1},{1,2},{2,3},{4,5},{5,6},{6,7},{8,9},{9,10},{10,11},{12,13},{... | collective-permute-start | bytes 196616 | tf_op jit(solution)/shard_map/ppermute | solution.py:25
  349.1 5.3 %collective-permute-start.40 = (bf16[1,8,1,128]{3,1,2,0:T(8,128)(2,1)S(1)}, bf16[1,8,1,128]{3,1,2,0:T(8,128)(2,1)S(1)}, u32[]{:S(2)}, u32[]{:S(2)}) collective-permute-start(bf16[1,8,1,128]{3,1,2,0:T(8,128)(2,1)S(1)} %get-tuple-element.226), channel_id=1, source_target_pairs={{4,0},{8,4},{12,8},{16,12},{20,16},{24,20},{28,24},{32,28},{36,32}... | collective-permute-start | bytes 6152 | tf_op jit(solution)/shard_map/ppermute | solution.py:17
  351.1 8.5 %collective-permute-start.39 = (bf16[1,8,1,128]{3,1,2,0:T(8,128)(2,1)S(1)}, bf16[1,8,1,128]{3,1,2,0:T(8,128)(2,1)S(1)}, u32[]{:S(2)}, u32[]{:S(2)}) collective-permute-start(bf16[1,8,1,128]{3,1,2,0:T(8,128)(2,1)S(1)} %get-tuple-element.225), channel_id=1, source_target_pairs={{0,4},{4,8},{8,12},{12,16},{16,20},{20,24},{24,28},{28,32},{32,36}... | collective-permute-start | bytes 6152 | tf_op jit(solution)/shard_map/ppermute | solution.py:16
  361.4 5.3 %collective-permute-start.42 = (bf16[1,8,1,128]{3,1,2,0:T(8,128)(2,1)S(1)}, bf16[1,8,1,128]{3,1,2,0:T(8,128)(2,1)S(1)}, u32[]{:S(2)}, u32[]{:S(2)}) collective-permute-start(bf16[1,8,1,128]{3,1,2,0:T(8,128)(2,1)S(1)} %get-tuple-element.222), channel_id=1, source_target_pairs={{4,0},{8,4},{12,8},{16,12},{20,16},{24,20},{28,24},{32,28},{36,32}... | collective-permute-start | bytes 6152 | tf_op jit(solution)/shard_map/ppermute | solution.py:17
  363.3 8.5 %collective-permute-start.41 = (bf16[1,8,1,128]{3,1,2,0:T(8,128)(2,1)S(1)}, bf16[1,8,1,128]{3,1,2,0:T(8,128)(2,1)S(1)}, u32[]{:S(2)}, u32[]{:S(2)}) collective-permute-start(bf16[1,8,1,128]{3,1,2,0:T(8,128)(2,1)S(1)} %get-tuple-element.221), channel_id=1, source_target_pairs={{0,4},{4,8},{8,12},{12,16},{16,20},{20,24},{24,28},{28,32},{32,36}... | collective-permute-start | bytes 6152 | tf_op jit(solution)/shard_map/ppermute | solution.py:16
  373.6 9.4 %collective-permute-start.43 = (bf16[1,8,32,128]{3,1,2,0:T(8,128)(2,1)S(1)}, bf16[1,8,32,128]{3,1,2,0:T(8,128)(2,1)S(1)}, u32[]{:S(2)}, u32[]{:S(2)}) collective-permute-start(bf16[1,8,32,128]{3,1,2,0:T(8,128)(2,1)S(1)} %fusion.120), channel_id=1, source_target_pairs={{0,1},{1,2},{2,3},{4,5},{5,6},{6,7},{8,9},{9,10},{10,11},{12,13},{... | collective-permute-start | bytes 196616 | tf_op jit(solution)/shard_map/ppermute | solution.py:25
  383.1 5.3 %collective-permute-start.45 = (bf16[1,8,1,128]{3,1,2,0:T(8,128)(2,1)S(1)}, bf16[1,8,1,128]{3,1,2,0:T(8,128)(2,1)S(1)}, u32[]{:S(2)}, u32[]{:S(2)}) collective-permute-start(bf16[1,8,1,128]{3,1,2,0:T(8,128)(2,1)S(1)} %get-tuple-element.218), channel_id=1, source_target_pairs={{4,0},{8,4},{12,8},{16,12},{20,16},{24,20},{28,24},{32,28},{36,32}... | collective-permute-start | bytes 6152 | tf_op jit(solution)/shard_map/ppermute | solution.py:17
  385.0 8.5 %collective-permute-start.44 = (bf16[1,8,1,128]{3,1,2,0:T(8,128)(2,1)S(1)}, bf16[1,8,1,128]{3,1,2,0:T(8,128)(2,1)S(1)}, u32[]{:S(2)}, u32[]{:S(2)}) collective-permute-start(bf16[1,8,1,128]{3,1,2,0:T(8,128)(2,1)S(1)} %get-tuple-element.217), channel_id=1, source_target_pairs={{0,4},{4,8},{8,12},{12,16},{16,20},{20,24},{24,28},{28,32},{32,36}... | collective-permute-start | bytes 6152 | tf_op jit(solution)/shard_map/ppermute | solution.py:16
  395.3 6.0 %collective-permute-start.47 = (bf16[1,8,1,128]{3,1,2,0:T(8,128)(2,1)S(1)}, bf16[1,8,1,128]{3,1,2,0:T(8,128)(2,1)S(1)}, u32[]{:S(2)}, u32[]{:S(2)}) collective-permute-start(bf16[1,8,1,128]{3,1,2,0:T(8,128)(2,1)S(1)} %get-tuple-element.214), channel_id=1, source_target_pairs={{4,0},{8,4},{12,8},{16,12},{20,16},{24,20},{28,24},{32,28},{36,32}... | collective-permute-start | bytes 6152 | tf_op jit(solution)/shard_map/ppermute | solution.py:17
  397.9 8.5 %collective-permute-start.46 = (bf16[1,8,1,128]{3,1,2,0:T(8,128)(2,1)S(1)}, bf16[1,8,1,128]{3,1,2,0:T(8,128)(2,1)S(1)}, u32[]{:S(2)}, u32[]{:S(2)}) collective-permute-start(bf16[1,8,1,128]{3,1,2,0:T(8,128)(2,1)S(1)} %get-tuple-element.213), channel_id=1, source_target_pairs={{0,4},{4,8},{8,12},{12,16},{16,20},{20,24},{24,28},{28,32},{32,36}... | collective-permute-start | bytes 6152 | tf_op jit(solution)/shard_map/ppermute | solution.py:16
Sparse Core Ops, SparseCore 0:
  189.2 52.0 all-reduce.26
  409.0 54.9 all-reduce.24
where the time goes:
time: 476 us; the launch traced here: 474 us
  waiting for transfers between devices  218 us (46%)
  starting transfers between devices  188 us (39%)
  matrix products  27 us (6%)
  between operations  21.1 us (4%)
  other arithmetic  11.6 us (2%)
  local copies, waits for them, and re-layouts  8.77 us (2%)
    psum x2, waiting for transfers between devices, spread(): return lax.psum(block, axis)  107 us
    ppermute x20, waiting for transfers between devices, with_halo(): before = lax.ppermute(last, axis, up)  100 us
    ppermute x20, starting transfers between devices, with_halo(): before = lax.ppermute(last, axis, up)  63.1 us
    ppermute x20, starting transfers between devices, with_halo(): after = lax.ppermute(leading, axis, down)  62.7 us
    ppermute x8, starting transfers between devices, from_behind(): return lax.ppermute(block, axis, route)  61.7 us
    dot_general x180, matrix products, convolve_local(): jnp.einsum('krwc,cd->krwd', window, weights[offset], preferred_element_ty...  27 us
    ppermute x8, waiting for transfers between devices, from_behind(): return lax.ppermute(block, axis, route)  10.5 us
  transfers between devices with their start and end apart: 50, of which 30 were waited for; matrix products, arithmetic and copies ran while one was open for 1% of the time, Pallas kernels for 0%

commit v1 on v0

v1 whole, which is shorter than its diff:
```python
import functools

import jax
import jax.numpy as jnp
from jax import lax
from jax.experimental import pallas as pl
from jax.experimental.pallas import tpu as pltpu
from jax.sharding import PartitionSpec as P

STEPS = 2
BF = jnp.bfloat16
F32 = jnp.float32

DEPTH = 16
WIDTH = 32
OWN = DEPTH + 2
RIGHT = OWN + WIDTH + 2
TOTAL = RIGHT + DEPTH


def pack_kernel(atmos_ref, ocean_ref, rotation_ref, mask_ref, fields_ref, up_ref, down_ref, tile):
    for index, ref in enumerate((atmos_ref, ocean_ref)):
        value = ref[...].astype(F32).reshape(16, WIDTH, 128)
        value = jnp.swapaxes(value, 0, 1).astype(BF)
        fields_ref[pl.ds(index * WIDTH, WIDTH)] = value
        up_ref[pl.ds(index * DEPTH, DEPTH)] = value[WIDTH - DEPTH :]
        down_ref[pl.ds(index * DEPTH, DEPTH)] = value[:DEPTH]
    lane = lax.broadcasted_iota(jnp.int32, (16, 128), 1)
    first = rotation_ref[0, 0].astype(F32)
    second = rotation_ref[0, 1].astype(F32)
    tile[...] = jnp.where(lane == 64, first, jnp.where(lane == 65, second, 0.0))
    mask = mask_ref[...].astype(F32)
    tile[0:8, 0:WIDTH] = mask
    tile[8:16, 0:WIDTH] = mask
    packed = tile[...].astype(BF)
    fields_ref[2 * WIDTH] = packed
    up_ref[2 * DEPTH] = packed
    down_ref[2 * DEPTH] = packed


def conv(source, weight, done):
    start = done + 1
    count = TOTAL - 2 * start
    left = jnp.concatenate(
        [source[pl.ds(start - 1, count)], source[pl.ds(start, count)], source[pl.ds(start + 1, count)]], axis=-1
    ).reshape(count * 16, 384)
    right = jnp.concatenate(
        [jnp.concatenate([weight[3 * a + b] for a in range(3)], axis=1) for b in range(3)], axis=0
    )
    product = lax.dot_general(left, right, (((1,), (0,)), ((), ())), preferred_element_type=F32)
    above, here, below = (product[:, 128 * a : 128 * a + 128].reshape(count * 2, 8, 128) for a in range(3))
    row = lax.broadcasted_iota(jnp.int32, (1, 8, 128), 1)
    above = jnp.where(row == 0, 0.0, pltpu.roll(above, 1, 1))
    below = jnp.where(row == 7, 0.0, pltpu.roll(below, 7, 1))
    return (here + above + below).reshape(count, 16, 128)


def turn_factors(code):
    lane = lax.broadcasted_iota(jnp.int32, (16, 128), 1)
    side = jnp.where(lane < 64, -1.0, 1.0)
    keep = jnp.where(code == 0.0, 1.0, jnp.where(code == 2.0, -1.0, 0.0))
    swap = jnp.where(code == 1.0, side, jnp.where(code == 3.0, -side, 0.0))
    return keep, swap


def main_kernel(
    fields_ref, before_ref, after_ref, own_ref, sibling_ref, far_ref, far_sibling_ref, atmos_out, ocean_out,
    weight, hidden, inner, ocean, sea, flux, final, semaphores,
):
    comp = lax.axis_index("comp")
    core = lax.rem(comp, 2)
    half = lax.div(comp, 2)
    places = (comp, half * 2 + 1 - core, (1 - half) * 2 + core, (1 - half) * 2 + 1 - core)
    copies = [
        pltpu.make_async_copy(ref.at[0], weight.at[place], semaphores.at[index])
        for index, (ref, place) in enumerate(zip((own_ref, sibling_ref, far_ref, far_sibling_ref), places))
    ]
    for copy in copies:
        copy.start()

    def broadcast(tile, column):
        return jnp.broadcast_to(tile[:, column : column + 1], (16, 128))

    own_tile = fields_ref[2 * WIDTH].astype(F32)
    before_tile = before_ref[2 * DEPTH].astype(F32)
    after_tile = after_ref[2 * DEPTH].astype(F32)
    seams = (
        (DEPTH, OWN, turn_factors(broadcast(before_tile, 65))),
        (DEPTH + 1, DEPTH - 1, turn_factors(broadcast(own_tile, 64))),
        (OWN + WIDTH, RIGHT, turn_factors(broadcast(own_tile, 65))),
        (RIGHT - 1, OWN + WIDTH - 1, turn_factors(broadcast(after_tile, 64))),
    )

    def close_seams(ref):
        for place, origin, (keep, swap) in seams:
            value = ref[origin].astype(F32)
            ref[place] = (keep * value + swap * pltpu.roll(value, 64, 1)).astype(BF)

    for ref, offset in ((hidden, 0), (ocean, 1)):
        ref[pl.ds(0, DEPTH)] = before_ref[pl.ds(offset * DEPTH, DEPTH)]
        ref[pl.ds(OWN, WIDTH)] = fields_ref[pl.ds(offset * WIDTH, WIDTH)]
        ref[pl.ds(RIGHT, DEPTH)] = after_ref[pl.ds(offset * DEPTH, DEPTH)]
    nothing = jnp.zeros((2, 16, 128), BF)
    for ref in (hidden, ocean, sea):
        ref[pl.ds(DEPTH, 2)] = nothing
        ref[pl.ds(RIGHT - 2, 2)] = nothing
    for column in range(DEPTH):
        sea[column] = broadcast(before_tile, WIDTH - DEPTH + column).astype(BF)
        sea[RIGHT + column] = broadcast(after_tile, column).astype(BF)
    for column in range(WIDTH):
        sea[OWN + column] = broadcast(own_tile, column).astype(BF)
    for copy in copies:
        copy.wait()

    done = 0
    for step in range(STEPS):
        span = pl.ds(done, TOTAL - 2 * done)
        hidden[span] = (hidden[span].astype(F32) + sea[span].astype(F32) * ocean[span].astype(F32)).astype(BF)
        close_seams(hidden)
        for section in range(4):
            if section == 3:
                span = pl.ds(done, TOTAL - 2 * done)
                flux[span] = (hidden[span].astype(F32) + ocean[span].astype(F32)).astype(BF)
                close_seams(flux)
            source = flux if section == 3 else hidden
            value = jax.nn.gelu(conv(source, weight.at[section, 0], done)).astype(BF)
            done += 1
            inner[pl.ds(done, TOTAL - 2 * done)] = value
            close_seams(inner)
            value = conv(inner, weight.at[section, 1], done)
            done += 1
            span = pl.ds(done, TOTAL - 2 * done)
            if section == 3:
                ocean[span] = (ocean[span].astype(F32) + sea[span].astype(F32) * value).astype(BF)
            else:
                hidden[span] = (hidden[span].astype(F32) + value).astype(BF)
                close_seams(hidden)

    for source, out in ((hidden, atmos_out), (ocean, ocean_out)):
        final[...] = jnp.swapaxes(source[pl.ds(OWN, WIDTH)].astype(F32), 0, 1)
        for member in range(2):
            out[member] = final[pl.ds(member * 8 + 2 * comp, 2)].astype(BF)


def per_device(atmos_state, ocean_state, conv_weight, rotation, sea_mask):
    tiles = lax.axis_size("pix")
    vmem = pl.BlockSpec(memory_space=pltpu.VMEM)
    fields, up, down = pl.pallas_call(
        pack_kernel,
        out_shape=(
            jax.ShapeDtypeStruct((2 * WIDTH + 1, 16, 128), BF),
            jax.ShapeDtypeStruct((2 * DEPTH + 1, 16, 128), BF),
            jax.ShapeDtypeStruct((2 * DEPTH + 1, 16, 128), BF),
        ),
        in_specs=[vmem, vmem, pl.BlockSpec(memory_space=pltpu.SMEM), vmem],
        out_specs=(vmem, vmem, vmem),
        scratch_shapes=[pltpu.VMEM((16, 128), F32)],
    )(atmos_state, ocean_state, rotation, sea_mask)

    names = ("pix", "comp")
    flip = 4 if tiles % 8 == 0 else 0
    swap = [(p * 4 + c, p * 4 + (c ^ 1)) for p in range(tiles) for c in range(4)]
    across = [(p * 4 + c, (p ^ flip) * 4 + (c ^ 2)) for p in range(tiles) for c in range(4)]
    far = lax.ppermute(conv_weight, names, across)
    sibling = lax.ppermute(conv_weight, names, swap)
    rightward = [(i, (i + 1) % tiles) for i in range(tiles)]
    before = lax.ppermute(up, "pix", rightward)
    after = lax.ppermute(down, "pix", [(j, i) for i, j in rightward])
    far_sibling = lax.ppermute(far, names, swap)

    anywhere = pl.BlockSpec(memory_space=pl.ANY)
    band = jax.ShapeDtypeStruct((2, 2, WIDTH, 128), BF)
    field = pltpu.VMEM((TOTAL, 16, 128), BF)
    return pl.pallas_call(
        main_kernel,
        out_shape=(band, band),
        in_specs=[vmem, vmem, vmem] + [anywhere] * 4,
        out_specs=(vmem, vmem),
        scratch_shapes=[
            pltpu.VMEM((4,) + conv_weight.shape[1:], BF),
            field,
            field,
            field,
            field,
            field,
            pltpu.VMEM((16, WIDTH, 128), F32),
            pltpu.SemaphoreType.DMA((4,)),
        ],
        compiler_params=pltpu.CompilerParams(vmem_limit_bytes=40 << 20),
    )(fields, before, after, conv_weight, sibling, far, far_sibling)


def solution(mesh):
    in_specs = (
        P(None, None, "pix", None),
        P(None, None, "pix", None),
        P("comp", None, None, None, None),
        P("pix", None),
        P(None, "pix"),
    )
    out_specs = (P(None, "comp", "pix", None), P(None, "comp", "pix", None))
    return jax.shard_map(
        per_device, mesh=mesh, in_specs=in_specs, out_specs=out_specs, check_vma=False
    )
```

time: 476 us -> 54.5 us (0.11)
  waiting for transfers between devices: 218 us -> 7.41 us
  starting transfers between devices: 188 us -> 32.9 us
  matrix products: 27 us -> 0 us
  between operations: 21.1 us -> 0.68 us
  other arithmetic: 11.6 us -> 0 us
  Pallas kernels: 0 us -> 11 us
  local copies, waits for them, and re-layouts: 8.77 us -> 2.02 us
    ppermute x48 -> x5, starting transfers between devices: 187 us -> 32.9 us  [the longest x1 12 us: per_device(): after = lax.ppermute(down, 'pix', [(j, i) for i, j in rightward])]
    psum x2 -> x0, waiting for transfers between devices: 107 us -> none  [spread(): return lax.psum(block, axis)]
    ppermute x48 -> x5, waiting for transfers between devices: 111 us -> 7.41 us  [the longest x1 4.11 us: per_device(): far = lax.ppermute(conv_weight, names, across)]
    dot_general x180 -> x0, matrix products: 27 us -> none  [convolve_local(): jnp.einsum('krwc,cd->krwd', window, weights[offset], preferred_element_ty...]
    pallas_call x0 -> x2, Pallas kernels: none -> 11 us  [the longest x1 9.15 us: per_device(): pl.pallas_call(main_kernel, out_shape=(band, band), in_specs=[vmem, vmem,...]
    concatenate x66 -> x0, other arithmetic: 5.24 us -> none  [the longest x40 3.05 us: turn_pairs(): jnp.concatenate([cosine * first_part - sine_term * second_part, sine_term...]
  transfers between devices with their start and end apart: 50 -> 5, of which waited for: 30 -> 3; matrix products, arithmetic and copies ran while one was open for 1% -> 0% of each run, Pallas kernels for 0% -> 3%
where the time goes in v1:
time: 54.5 us; the launch traced here: 54 us
  starting transfers between devices  32.9 us (60%)
  Pallas kernels  11 us (20%)
  waiting for transfers between devices  7.41 us (14%)
  local copies, waits for them, and re-layouts  2.02 us (4%)
  between operations  0.68 us (1%)
    ppermute x1, starting transfers between devices, per_device(): after = lax.ppermute(down, 'pix', [(j, i) for i, j in rightward])  12 us
    pallas_call x1, Pallas kernels, per_device(): pl.pallas_call(main_kernel, out_shape=(band, band), in_specs=[vmem, vmem,...  9.15 us
    ppermute x1, starting transfers between devices, per_device(): far_sibling = lax.ppermute(far, names, swap)  7.14 us
    ppermute x1, starting transfers between devices, per_device(): sibling = lax.ppermute(conv_weight, names, swap)  5.49 us
    ppermute x1, starting transfers between devices, per_device(): far = lax.ppermute(conv_weight, names, across)  5.22 us
    ppermute x1, waiting for transfers between devices, per_device(): far = lax.ppermute(conv_weight, names, across)  4.11 us
    ppermute x1, starting transfers between devices, per_device(): before = lax.ppermute(up, 'pix', rightward)  3 us
    ppermute x1, waiting for transfers between devices, per_device(): before = lax.ppermute(up, 'pix', rightward)  2.21 us
  transfers between devices with their start and end apart: 5, of which 3 were waited for; matrix products, arithmetic and copies ran while one was open for 0% of the time, Pallas kernels for 3%

profile of v1, /device:TPU:1, one launch (start us, length us, event | category | flops | bytes accessed | tf_op | source)
XLA Modules:
  0.0 54.0 jit_solution(778028761618405941)
XLA Ops:
  0.6 5.2 %collective-permute-start.3 = (bf16[1,2,9,128,128]{4,3,2,1,0:T(8,128)(2,1)}, bf16[1,2,9,128,128]{4,3,2,1,0:T(8,128)(2,1)S(1)}, u32[]{:S(2)}, u32[]{:S(2)}) collective-permute-start(bf16[1,2,9,128,128]{4,3,2,1,0:T(8,128)(2,1)} %own_ref.1), channel_id=1, source_target_pairs={{0,18},{1,19},{2,16},{3,17},{4,22},{5,23},{6,20},{7,21},{8,26},{9,... | collective-permute-start | bytes 1769480 | tf_op jit(solution)/shard_map/ppermute | solution.py:164
  5.9 5.5 %collective-permute-start.2 = (bf16[1,2,9,128,128]{4,3,2,1,0:T(8,128)(2,1)}, bf16[1,2,9,128,128]{4,3,2,1,0:T(8,128)(2,1)S(1)}, u32[]{:S(2)}, u32[]{:S(2)}) collective-permute-start(bf16[1,2,9,128,128]{4,3,2,1,0:T(8,128)(2,1)} %own_ref.1), channel_id=1, source_target_pairs={{0,1},{1,0},{2,3},{3,2},{4,5},{5,4},{6,7},{7,6},{8,9},{9,8},{10,11... | collective-permute-start | bytes 1769480 | tf_op jit(solution)/shard_map/ppermute | solution.py:165
  11.4 4.1 %collective-permute-done.3.far_ref = bf16[1,2,9,128,128]{4,3,2,1,0:T(8,128)(2,1)S(1)} collective-permute-done((bf16[1,2,9,128,128]{4,3,2,1,0:T(8,128)(2,1)}, bf16[1,2,9,128,128]{4,3,2,1,0:T(8,128)(2,1)S(1)}, u32[]{:S(2)}, u32[]{:S(2)}) %collective-permute-start.3) | collective-permute-done | bytes 589856 | tf_op jit(solution)/shard_map/ppermute | solution.py:164
  15.5 7.1 %collective-permute-start.4 = (bf16[1,2,9,128,128]{4,3,2,1,0:T(8,128)(2,1)S(1)}, bf16[1,2,9,128,128]{4,3,2,1,0:T(8,128)(2,1)S(1)}, u32[]{:S(2)}, u32[]{:S(2)}) collective-permute-start(bf16[1,2,9,128,128]{4,3,2,1,0:T(8,128)(2,1)S(1)} %collective-permute-done.3.far_ref), channel_id=1, source_target_pairs={{0,1},{1,0},{2,3},{3,2},{4,5},{5,4},{6,7},{7,6},{8,9},{9,8},{10,11... | collective-permute-start | bytes 1769480 | tf_op jit(solution)/shard_map/ppermute | solution.py:169
  22.6 1.9 %shard_map.68 = (bf16[65,16,128]{2,1,0:T(8,128)(2,1)}, bf16[33,16,128]{2,1,0:T(8,128)(2,1)}, bf16[33,16,128]{2,1,0:T(8,128)(2,1)}) custom-call(bf16[2,8,32,128]{3,2,1,0:T(8,128)(2,1)} %atmos_ref.1, bf16[2,8,32,128]{3,2,1,0:T(8,128)(2,1)} %ocean_ref.1, s32[1,2]{1,0:T(1,128)} %rotation_ref.1, s32[8,32]{1,0:T(8,128)} %mask_ref.1), custom_call_target="tpu_custom_call" | custom-call | tf_op jit(solution)/shard_map/pallas_call | solution.py:148
  24.5 3.0 %collective-permute-start = (bf16[33,16,128]{2,1,0:T(8,128)(2,1)}, bf16[33,16,128]{2,1,0:T(8,128)(2,1)S(1)}, u32[]{:S(2)}, u32[]{:S(2)}) collective-permute-start(bf16[33,16,128]{2,1,0:T(8,128)(2,1)} %get-tuple-element.6), channel_id=1, source_target_pairs={{0,4},{4,8},{8,12},{12,16},{16,20},{20,24},{24,28},{28,32},{32,36}... | collective-permute-start | bytes 405512 | tf_op jit(solution)/shard_map/ppermute | solution.py:167
  27.5 12.0 %collective-permute-start.1 = (bf16[33,16,128]{2,1,0:T(8,128)(2,1)}, bf16[33,16,128]{2,1,0:T(8,128)(2,1)S(1)}, u32[]{:S(2)}, u32[]{:S(2)}) collective-permute-start(bf16[33,16,128]{2,1,0:T(8,128)(2,1)} %get-tuple-element.7), channel_id=1, source_target_pairs={{4,0},{8,4},{12,8},{16,12},{20,16},{24,20},{28,24},{32,28},{36,32}... | collective-permute-start | bytes 405512 | tf_op jit(solution)/shard_map/ppermute | solution.py:168
  39.5 2.2 %collective-permute-done.before_ref = bf16[33,16,128]{2,1,0:T(8,128)(2,1)S(1)} collective-permute-done((bf16[33,16,128]{2,1,0:T(8,128)(2,1)}, bf16[33,16,128]{2,1,0:T(8,128)(2,1)S(1)}, u32[]{:S(2)}, u32[]{:S(2)}) %collective-permute-start) | collective-permute-done | bytes 135200 | tf_op jit(solution)/shard_map/ppermute | solution.py:167
  41.7 1.1 %collective-permute-done.1.after_ref = bf16[33,16,128]{2,1,0:T(8,128)(2,1)S(1)} collective-permute-done((bf16[33,16,128]{2,1,0:T(8,128)(2,1)}, bf16[33,16,128]{2,1,0:T(8,128)(2,1)S(1)}, u32[]{:S(2)}, u32[]{:S(2)}) %collective-permute-start.1) | collective-permute-done | bytes 135200 | tf_op jit(solution)/shard_map/ppermute | solution.py:168
  42.8 0.0 collective-permute-done.2.sibling_ref
  42.8 0.0 collective-permute-done.4.far_sibling_ref
  42.8 0.0 copy-start
  42.8 1.1 %copy-done = bf16[1,2,9,128,128]{4,3,2,1,0:T(8,128)(2,1)S(1)} copy-done((bf16[1,2,9,128,128]{4,3,2,1,0:T(8,128)(2,1)S(1)}, bf16[1,2,9,128,128]{4,3,2,1,0:T(8,128)(2,1)}, u32[]{:S(2)}) %copy-start) | copy-done | bytes 589848
  43.9 0.0 copy-start.1
  43.9 0.9 %copy-done.1 = bf16[65,16,128]{2,1,0:T(8,128)(2,1)S(1)} copy-done((bf16[65,16,128]{2,1,0:T(8,128)(2,1)S(1)}, bf16[65,16,128]{2,1,0:T(8,128)(2,1)}, u32[]{:S(2)}) %copy-start.1) | copy-done | bytes 266264
  44.8 9.2 %shard_map.69 = (bf16[2,2,32,128]{3,2,1,0:T(8,128)(2,1)}, bf16[2,2,32,128]{3,2,1,0:T(8,128)(2,1)}) custom-call(bf16[65,16,128]{2,1,0:T(8,128)(2,1)S(1)} %copy-done.1, bf16[33,16,128]{2,1,0:T(8,128)(2,1)S(1)} %collective-permute-done.before_ref, bf16[33,16,128]{2,1,0:T(8,128)(2,1)S(1)} %collective-permute-done.1.after_ref, ...), custom_call_target="tpu_custom_call" | custom-call | tf_op jit(solution)/shard_map/pallas_call | solution.py:174
Async XLA Ops:
  0.6 14.8 %collective-permute-start.3 = (bf16[1,2,9,128,128]{4,3,2,1,0:T(8,128)(2,1)}, bf16[1,2,9,128,128]{4,3,2,1,0:T(8,128)(2,1)S(1)}, u32[]{:S(2)}, u32[]{:S(2)}) collective-permute-start(bf16[1,2,9,128,128]{4,3,2,1,0:T(8,128)(2,1)} %own_ref.1), channel_id=1, source_target_pairs={{0,18},{1,19},{2,16},{3,17},{4,22},{5,23},{6,20},{7,21},{8,26},{9,... | collective-permute-start | bytes 1769480 | tf_op jit(solution)/shard_map/ppermute | solution.py:164
  5.9 37.0 %collective-permute-start.2 = (bf16[1,2,9,128,128]{4,3,2,1,0:T(8,128)(2,1)}, bf16[1,2,9,128,128]{4,3,2,1,0:T(8,128)(2,1)S(1)}, u32[]{:S(2)}, u32[]{:S(2)}) collective-permute-start(bf16[1,2,9,128,128]{4,3,2,1,0:T(8,128)(2,1)} %own_ref.1), channel_id=1, source_target_pairs={{0,1},{1,0},{2,3},{3,2},{4,5},{5,4},{6,7},{7,6},{8,9},{9,8},{10,11... | collective-permute-start | bytes 1769480 | tf_op jit(solution)/shard_map/ppermute | solution.py:165
  15.5 27.3 %collective-permute-start.4 = (bf16[1,2,9,128,128]{4,3,2,1,0:T(8,128)(2,1)S(1)}, bf16[1,2,9,128,128]{4,3,2,1,0:T(8,128)(2,1)S(1)}, u32[]{:S(2)}, u32[]{:S(2)}) collective-permute-start(bf16[1,2,9,128,128]{4,3,2,1,0:T(8,128)(2,1)S(1)} %collective-permute-done.3.far_ref), channel_id=1, source_target_pairs={{0,1},{1,0},{2,3},{3,2},{4,5},{5,4},{6,7},{7,6},{8,9},{9,8},{10,11... | collective-permute-start | bytes 1769480 | tf_op jit(solution)/shard_map/ppermute | solution.py:169
  24.5 17.2 %collective-permute-start = (bf16[33,16,128]{2,1,0:T(8,128)(2,1)}, bf16[33,16,128]{2,1,0:T(8,128)(2,1)S(1)}, u32[]{:S(2)}, u32[]{:S(2)}) collective-permute-start(bf16[33,16,128]{2,1,0:T(8,128)(2,1)} %get-tuple-element.6), channel_id=1, source_target_pairs={{0,4},{4,8},{8,12},{12,16},{16,20},{20,24},{24,28},{28,32},{32,36}... | collective-permute-start | bytes 405512 | tf_op jit(solution)/shard_map/ppermute | solution.py:167
  27.5 15.3 %collective-permute-start.1 = (bf16[33,16,128]{2,1,0:T(8,128)(2,1)}, bf16[33,16,128]{2,1,0:T(8,128)(2,1)S(1)}, u32[]{:S(2)}, u32[]{:S(2)}) collective-permute-start(bf16[33,16,128]{2,1,0:T(8,128)(2,1)} %get-tuple-element.7), channel_id=1, source_target_pairs={{4,0},{8,4},{12,8},{16,12},{20,16},{24,20},{28,24},{32,28},{36,32}... | collective-permute-start | bytes 405512 | tf_op jit(solution)/shard_map/ppermute | solution.py:168
  42.8 1.1 %copy-start = (bf16[1,2,9,128,128]{4,3,2,1,0:T(8,128)(2,1)S(1)}, bf16[1,2,9,128,128]{4,3,2,1,0:T(8,128)(2,1)}, u32[]{:S(2)}) copy-start(bf16[1,2,9,128,128]{4,3,2,1,0:T(8,128)(2,1)} %own_ref.1) | copy-start | bytes 1769476
  43.9 1.0 %copy-start.1 = (bf16[65,16,128]{2,1,0:T(8,128)(2,1)S(1)}, bf16[65,16,128]{2,1,0:T(8,128)(2,1)}, u32[]{:S(2)}) copy-start(bf16[65,16,128]{2,1,0:T(8,128)(2,1)} %get-tuple-element.5.fields_ref) | copy-start | bytes 798724

commit v2 on v1

v2 whole, which is shorter than its diff:
```python
import functools

import jax
import jax.numpy as jnp
from jax import lax
from jax.experimental import pallas as pl
from jax.experimental.pallas import tpu as pltpu
from jax.sharding import PartitionSpec as P

STEPS = 2
BF = jnp.bfloat16
F32 = jnp.float32

DEPTH = 16
WIDTH = 32
OWN = DEPTH + 2
RIGHT = OWN + WIDTH + 2
TOTAL = RIGHT + DEPTH
CUT = 48


def pack_kernel(atmos_ref, ocean_ref, rotation_ref, mask_ref, fields_ref, up_ref, down_ref, tile):
    for index, ref in enumerate((atmos_ref, ocean_ref)):
        value = ref[...].astype(F32).reshape(16, WIDTH, 128)
        value = jnp.swapaxes(value, 0, 1).astype(BF)
        fields_ref[pl.ds(index * WIDTH, WIDTH)] = value
        up_ref[pl.ds(index * DEPTH, DEPTH)] = value[WIDTH - DEPTH :]
        down_ref[pl.ds(index * DEPTH, DEPTH)] = value[:DEPTH]
    lane = lax.broadcasted_iota(jnp.int32, (16, 128), 1)
    first = rotation_ref[0, 0].astype(F32)
    second = rotation_ref[0, 1].astype(F32)
    tile[...] = jnp.where(lane == 64, first, jnp.where(lane == 65, second, 0.0))
    mask = mask_ref[...].astype(F32)
    tile[0:8, 0:WIDTH] = mask
    tile[8:16, 0:WIDTH] = mask
    packed = tile[...].astype(BF)
    fields_ref[2 * WIDTH] = packed
    up_ref[2 * DEPTH] = packed
    down_ref[2 * DEPTH] = packed


def product(source, weight, start, stop):
    count = stop - start
    left = jnp.concatenate([source[pl.ds(start + b - 1, count)] for b in range(3)], axis=-1)
    right = jnp.concatenate(
        [jnp.concatenate([weight[3 * a + b] for a in range(3)], axis=1) for b in range(3)], axis=0
    )
    return lax.dot_general(
        left.reshape(count * 16, 384), right, (((1,), (0,)), ((), ())), preferred_element_type=F32
    )


def add_rows(value, count):
    above, here, below = (value[:, 128 * a : 128 * a + 128].reshape(count * 2, 8, 128) for a in range(3))
    row = lax.broadcasted_iota(jnp.int32, (1, 8, 128), 1)
    above = jnp.where(row == 0, 0.0, pltpu.roll(above, 1, 1))
    below = jnp.where(row == 7, 0.0, pltpu.roll(below, 7, 1))
    return (here + above + below).reshape(count, 16, 128)


def gelu(value):
    half = 0.5 * value
    return half + half * jnp.tanh(value * (0.7978845608028654 + 0.035677408136300125 * (value * value)))


SEAMS = ((DEPTH, OWN), (DEPTH + 1, DEPTH - 1), (OWN + WIDTH, RIGHT), (RIGHT - 1, OWN + WIDTH - 1))


def close_seams(ref, factors, which):
    for index in which:
        place, origin = SEAMS[index]
        value = ref[origin].astype(F32)
        turned = factors[2 * index].astype(F32) * value + factors[2 * index + 1].astype(F32) * pltpu.roll(value, 64, 1)
        ref[place] = turned.astype(BF)


def turn_factors(code):
    lane = lax.broadcasted_iota(jnp.int32, (16, 128), 1)
    side = jnp.where(lane < 64, -1.0, 1.0)
    keep = jnp.where(code == 0.0, 1.0, jnp.where(code == 2.0, -1.0, 0.0))
    swap = jnp.where(code == 1.0, side, jnp.where(code == 3.0, -side, 0.0))
    return keep.astype(BF), swap.astype(BF)


def state_kernel(fields_ref, before_ref, after_ref, own_ref, sibling_ref, state_ref, weight_ref, semaphores):
    comp = lax.axis_index("comp")
    copies = (
        pltpu.make_async_copy(own_ref.at[0], weight_ref.at[comp], semaphores.at[0]),
        pltpu.make_async_copy(sibling_ref.at[0], weight_ref.at[comp + 1 - 2 * lax.rem(comp, 2)], semaphores.at[1]),
    )
    for copy in copies:
        copy.start()

    def broadcast(tile, column):
        return jnp.broadcast_to(tile[:, column : column + 1], (16, 128))

    own_tile = fields_ref[2 * WIDTH].astype(F32)
    before_tile = before_ref[2 * DEPTH].astype(F32)
    after_tile = after_ref[2 * DEPTH].astype(F32)
    hidden, ocean, sea, factors = (
        state_ref.at[pl.ds(TOTAL * index, TOTAL if index < 3 else 2 * len(SEAMS))] for index in range(4)
    )
    for index, (tile, lane) in enumerate(((before_tile, 65), (own_tile, 64), (own_tile, 65), (after_tile, 64))):
        factors[2 * index], factors[2 * index + 1] = turn_factors(broadcast(tile, lane))
    for column in range(DEPTH):
        sea[column] = broadcast(before_tile, WIDTH - DEPTH + column).astype(BF)
        sea[RIGHT + column] = broadcast(after_tile, column).astype(BF)
    for column in range(WIDTH):
        sea[OWN + column] = broadcast(own_tile, column).astype(BF)
    nothing = jnp.zeros((2, 16, 128), BF)
    for ref in (ocean, sea):
        ref[pl.ds(DEPTH, 2)] = nothing
        ref[pl.ds(RIGHT - 2, 2)] = nothing
    for ref, origin, count, place in (
        (before_ref, 0, DEPTH, 0),
        (fields_ref, 0, WIDTH, OWN),
        (after_ref, 0, DEPTH, RIGHT),
    ):
        span = pl.ds(place, count)
        ocean_value = ref[pl.ds(origin + count, count)]
        ocean[span] = ocean_value
        atmos_value = ref[pl.ds(origin, count)].astype(F32)
        hidden[span] = (atmos_value + sea[span].astype(F32) * ocean_value.astype(F32)).astype(BF)
    close_seams(hidden, factors, range(4))
    for copy in copies:
        copy.wait()


def main_kernel(
    state_ref, weight_ref, far_ref, far_sibling_ref, atmos_out, ocean_out, weight_out,
    hidden_ref, inner, ocean_ref, flux, final, semaphores,
):
    comp = lax.axis_index("comp")
    core = lax.rem(comp, 2)
    other = 2 - 2 * lax.div(comp, 2)
    copies = (
        pltpu.make_async_copy(far_ref.at[0], weight_out.at[other + core], semaphores.at[0]),
        pltpu.make_async_copy(far_sibling_ref.at[0], weight_out.at[other + 1 - core], semaphores.at[1]),
    )
    for copy in copies:
        copy.start()
    hidden, ocean, sea, factors = (
        state_ref.at[pl.ds(TOTAL * index, TOTAL if index < 3 else 2 * len(SEAMS))] for index in range(4)
    )
    for copy in copies:
        copy.wait()

    def load(ref, span):
        return ref[span].astype(F32)

    def convolve(source, weight, done, finish, out):
        bounds = (done, CUT - done, TOTAL - done)
        for part in range(2):
            start, stop = bounds[part : part + 2]
            span = pl.ds(start, stop - start)
            value = add_rows(product(source, weight, start, stop), stop - start)
            out[span] = finish(span, value).astype(BF)
            if done < DEPTH:
                close_seams(out, factors, (0, 1) if part == 0 else (2, 3))

    done = 0
    for step in range(STEPS):
        if step > 0:
            for start, stop, seams in ((done, CUT - done, (0, 1)), (CUT - done, TOTAL - done, (2, 3))):
                span = pl.ds(start, stop - start)
                hidden_ref[span] = (load(hidden, span) + load(sea, span) * load(ocean, span)).astype(BF)
                close_seams(hidden_ref, factors, seams)
        for section in range(4):
            source = hidden
            if section == 3:
                source = flux
                for start, stop, seams in ((done, CUT - done, (0, 1)), (CUT - done, TOTAL - done, (2, 3))):
                    span = pl.ds(start, stop - start)
                    flux[span] = (load(hidden, span) + load(ocean, span)).astype(BF)
                    close_seams(flux, factors, seams)
            weight = weight_out.at[section]
            done += 1
            convolve(source, weight.at[0], done, lambda span, value: gelu(value), inner)
            done += 1
            if section == 3:
                base = ocean
                convolve(
                    inner, weight.at[1], done,
                    lambda span, value: load(base, span) + load(sea, span) * value, ocean_ref,
                )
                ocean = ocean_ref
            else:
                base = hidden
                convolve(inner, weight.at[1], done, lambda span, value: load(base, span) + value, hidden_ref)
                hidden = hidden_ref

    for source, out in ((hidden, atmos_out), (ocean, ocean_out)):
        final[...] = jnp.swapaxes(source[pl.ds(OWN, WIDTH)].astype(F32), 0, 1)
        for member in range(2):
            out[member] = final[pl.ds(member * 8 + 2 * comp, 2)].astype(BF)


def per_device(atmos_state, ocean_state, conv_weight, rotation, sea_mask):
    tiles = lax.axis_size("pix")
    vmem = pl.BlockSpec(memory_space=pltpu.VMEM)
    fields, up, down = pl.pallas_call(
        pack_kernel,
        out_shape=(
            jax.ShapeDtypeStruct((2 * WIDTH + 1, 16, 128), BF),
            jax.ShapeDtypeStruct((2 * DEPTH + 1, 16, 128), BF),
            jax.ShapeDtypeStruct((2 * DEPTH + 1, 16, 128), BF),
        ),
        in_specs=[vmem, vmem, pl.BlockSpec(memory_space=pltpu.SMEM), vmem],
        out_specs=(vmem, vmem, vmem),
        scratch_shapes=[pltpu.VMEM((16, 128), F32)],
    )(atmos_state, ocean_state, rotation, sea_mask)

    names = ("pix", "comp")
    flip = 4 if tiles % 8 == 0 else 0
    swap = [(p * 4 + c, p * 4 + (c ^ 1)) for p in range(tiles) for c in range(4)]
    across = [(p * 4 + c, (p ^ flip) * 4 + (c ^ 2)) for p in range(tiles) for c in range(4)]
    far = lax.ppermute(conv_weight, names, across)
    sibling = lax.ppermute(conv_weight, names, swap)
    rightward = [(i, (i + 1) % tiles) for i in range(tiles)]
    before = lax.ppermute(up, "pix", rightward)
    after = lax.ppermute(down, "pix", [(j, i) for i, j in rightward])
    far, before, after = lax.optimization_barrier((far, before, after))
    far_sibling = lax.ppermute(far, names, swap)

    anywhere = pl.BlockSpec(memory_space=pl.ANY)
    all_weights = jax.ShapeDtypeStruct((4,) + conv_weight.shape[1:], BF)
    params = pltpu.CompilerParams(vmem_limit_bytes=40 << 20)
    state, weight = pl.pallas_call(
        state_kernel,
        out_shape=(jax.ShapeDtypeStruct((3 * TOTAL + 2 * len(SEAMS), 16, 128), BF), all_weights),
        in_specs=[vmem, vmem, vmem, anywhere, anywhere],
        out_specs=(vmem, vmem),
        scratch_shapes=[pltpu.SemaphoreType.DMA((2,))],
        compiler_params=params,
    )(fields, before, after, conv_weight, sibling)

    band = jax.ShapeDtypeStruct((2, 2, WIDTH, 128), BF)
    field = pltpu.VMEM((TOTAL, 16, 128), BF)
    return pl.pallas_call(
        main_kernel,
        out_shape=(band, band, all_weights),
        in_specs=[vmem, vmem, anywhere, anywhere],
        out_specs=(vmem, vmem, vmem),
        input_output_aliases={1: 2},
        scratch_shapes=[
            field,
            field,
            field,
            field,
            pltpu.VMEM((16, WIDTH, 128), F32),
            pltpu.SemaphoreType.DMA((2,)),
        ],
        compiler_params=params,
    )(state, weight, far, far_sibling)[:2]


def solution(mesh):
    in_specs = (
        P(None, None, "pix", None),
        P(None, None, "pix", None),
        P("comp", None, None, None, None),
        P("pix", None),
        P(None, "pix"),
    )
    out_specs = (P(None, "comp", "pix", None), P(None, "comp", "pix", None))
    return jax.shard_map(
        per_device, mesh=mesh, in_specs=in_specs, out_specs=out_specs, check_vma=False
    )
```

time: 54.5 us -> 39.2 us (0.72)
  waiting for transfers between devices: 7.41 us -> 0.01 us
  starting transfers between devices: 32.9 us -> 26.3 us
  Pallas kernels: 11 us -> 9.79 us
    ppermute x1, starting transfers between devices: 7.14 us -> 2.81 us  [per_device(): far_sibling = lax.ppermute(far, names, swap)]
    ppermute x1, waiting for transfers between devices: 4.11 us -> 0.01 us  [per_device(): far = lax.ppermute(conv_weight, names, across)]
    ppermute x1, starting transfers between devices: 5.49 us -> 3.15 us  [per_device(): sibling = lax.ppermute(conv_weight, names, swap)]
    ppermute x1, waiting for transfers between devices: 2.21 us -> 0.01 us  [per_device(): before = lax.ppermute(up, 'pix', rightward)]
    pallas_call x1 -> x2, Pallas kernels: 9.15 us -> 7.94 us  [the longest x1 7.4 us: per_device(): pl.pallas_call(main_kernel, out_shape=(band, band, all_weights), in_specs...]
    ppermute x1, waiting for transfers between devices: 1.08 us -> 0.01 us  [per_device(): after = lax.ppermute(down, 'pix', [(j, i) for i, j in rightward])]
  transfers between devices with their start and end apart: 5 -> 5, of which waited for: 3 -> 0; matrix products, arithmetic and copies ran while one was open for 0% -> 0% of each run, Pallas kernels for 3% -> 6%
where the time goes in v2:
time: 39.2 us; the launch traced here: 38.9 us
  starting transfers between devices  26.3 us (67%)
  Pallas kernels  9.79 us (25%)
  local copies, waits for them, and re-layouts  2.01 us (5%)
  between operations  0.73 us (2%)
    ppermute x1, starting transfers between devices, per_device(): after = lax.ppermute(down, 'pix', [(j, i) for i, j in rightward])  11.9 us
    pallas_call x1, Pallas kernels, per_device(): pl.pallas_call(main_kernel, out_shape=(band, band, all_weights), in_specs...  7.4 us
    ppermute x1, starting transfers between devices, per_device(): far = lax.ppermute(conv_weight, names, across)  5.22 us
    ppermute x1, starting transfers between devices, per_device(): before = lax.ppermute(up, 'pix', rightward)  3.19 us
    ppermute x1, starting transfers between devices, per_device(): sibling = lax.ppermute(conv_weight, names, swap)  3.15 us
    ppermute x1, starting transfers between devices, per_device(): far_sibling = lax.ppermute(far, names, swap)  2.81 us
    unnamed x4, local copies, waits for them, and re-layouts  2.01 us
    pallas_call x1, Pallas kernels, per_device(): pl.pallas_call(pack_kernel, out_shape=(jax.ShapeDtypeStruct((2 * WIDTH +...  1.85 us
  transfers between devices with their start and end apart: 5, of which 0 were waited for; matrix products, arithmetic and copies ran while one was open for 0% of the time, Pallas kernels for 6%

profile of v2, /device:TPU:1, one launch (start us, length us, event | category | flops | bytes accessed | tf_op | source)
XLA Modules:
  0.0 38.9 jit_solution(8220348115498689321)
XLA Ops:
  0.6 5.2 %collective-permute-start = (bf16[1,2,9,128,128]{4,3,2,1,0:T(8,128)(2,1)}, bf16[1,2,9,128,128]{4,3,2,1,0:T(8,128)(2,1)S(1)}, u32[]{:S(2)}, u32[]{:S(2)}) collective-permute-start(bf16[1,2,9,128,128]{4,3,2,1,0:T(8,128)(2,1)} %own_ref.1), channel_id=1, source_target_pairs={{0,18},{1,19},{2,16},{3,17},{4,22},{5,23},{6,20},{7,21},{8,26},{9,... | collective-permute-start | bytes 1769480 | tf_op jit(solution)/shard_map/ppermute | solution.py:217
  5.9 1.8 %shard_map.68 = (bf16[65,16,128]{2,1,0:T(8,128)(2,1)}, bf16[33,16,128]{2,1,0:T(8,128)(2,1)}, bf16[33,16,128]{2,1,0:T(8,128)(2,1)}) custom-call(bf16[2,8,32,128]{3,2,1,0:T(8,128)(2,1)} %atmos_ref.1, bf16[2,8,32,128]{3,2,1,0:T(8,128)(2,1)} %ocean_ref.1, s32[1,2]{1,0:T(1,128)} %rotation_ref.1, s32[8,32]{1,0:T(8,128)} %mask_ref.1), custom_call_target="tpu_custom_call" | custom-call | tf_op jit(solution)/shard_map/pallas_call | solution.py:201
  7.7 3.2 %collective-permute-start.1 = (bf16[33,16,128]{2,1,0:T(8,128)(2,1)}, bf16[33,16,128]{2,1,0:T(8,128)(2,1)S(1)}, u32[]{:S(2)}, u32[]{:S(2)}) collective-permute-start(bf16[33,16,128]{2,1,0:T(8,128)(2,1)} %get-tuple-element.13), channel_id=1, source_target_pairs={{0,4},{4,8},{8,12},{12,16},{16,20},{20,24},{24,28},{28,32},{32,36}... | collective-permute-start | bytes 405512 | tf_op jit(solution)/shard_map/ppermute | solution.py:220
  10.9 11.9 %collective-permute-start.2 = (bf16[33,16,128]{2,1,0:T(8,128)(2,1)}, bf16[33,16,128]{2,1,0:T(8,128)(2,1)S(1)}, u32[]{:S(2)}, u32[]{:S(2)}) collective-permute-start(bf16[33,16,128]{2,1,0:T(8,128)(2,1)} %get-tuple-element.14), channel_id=1, source_target_pairs={{4,0},{8,4},{12,8},{16,12},{20,16},{24,20},{28,24},{32,28},{36,32}... | collective-permute-start | bytes 405512 | tf_op jit(solution)/shard_map/ppermute | solution.py:221
  22.9 3.1 %collective-permute-start.3 = (bf16[1,2,9,128,128]{4,3,2,1,0:T(8,128)(2,1)}, bf16[1,2,9,128,128]{4,3,2,1,0:T(8,128)(2,1)S(1)}, u32[]{:S(2)}, u32[]{:S(2)}) collective-permute-start(bf16[1,2,9,128,128]{4,3,2,1,0:T(8,128)(2,1)} %own_ref.1), channel_id=1, source_target_pairs={{0,1},{1,0},{2,3},{3,2},{4,5},{5,4},{6,7},{7,6},{8,9},{9,8},{10,11... | collective-permute-start | bytes 1769480 | tf_op jit(solution)/shard_map/ppermute | solution.py:218
  26.0 0.0 collective-permute-done.1.before_ref
  26.0 0.0 collective-permute-done.2.after_ref
  26.0 0.0 collective-permute-done.far_ref
  26.0 2.8 %collective-permute-start.4 = (bf16[1,2,9,128,128]{4,3,2,1,0:T(8,128)(2,1)S(1)}, bf16[1,2,9,128,128]{4,3,2,1,0:T(8,128)(2,1)S(1)}, u32[]{:S(2)}, u32[]{:S(2)}) collective-permute-start(bf16[1,2,9,128,128]{4,3,2,1,0:T(8,128)(2,1)S(1)} %collective-permute-done.far_ref), channel_id=1, source_target_pairs={{0,1},{1,0},{2,3},{3,2},{4,5},{5,4},{6,7},{7,6},{8,9},{9,8},{10,11... | collective-permute-start | bytes 1769480 | tf_op jit(solution)/shard_map/ppermute | solution.py:223
  28.9 0.0 collective-permute-done.3.sibling_ref
  28.9 0.0 copy-start
  28.9 1.1 %copy-done = bf16[1,2,9,128,128]{4,3,2,1,0:T(8,128)(2,1)S(1)} copy-done((bf16[1,2,9,128,128]{4,3,2,1,0:T(8,128)(2,1)S(1)}, bf16[1,2,9,128,128]{4,3,2,1,0:T(8,128)(2,1)}, u32[]{:S(2)}) %copy-start) | copy-done | bytes 589848
  29.9 0.0 copy-start.1
  29.9 0.9 %copy-done.1 = bf16[65,16,128]{2,1,0:T(8,128)(2,1)S(1)} copy-done((bf16[65,16,128]{2,1,0:T(8,128)(2,1)S(1)}, bf16[65,16,128]{2,1,0:T(8,128)(2,1)}, u32[]{:S(2)}) %copy-start.1) | copy-done | bytes 266264
  30.9 0.5 %shard_map.69 = (bf16[212,16,128]{2,1,0:T(8,128)(2,1)S(1)}, bf16[4,2,9,128,128]{4,3,2,1,0:T(8,128)(2,1)S(1)}) custom-call(bf16[65,16,128]{2,1,0:T(8,128)(2,1)S(1)} %copy-done.1, bf16[33,16,128]{2,1,0:T(8,128)(2,1)S(1)} %collective-permute-done.1.before_ref, bf16[33,16,128]{2,1,0:T(8,128)(2,1)S(1)} %collective-permute-done.2.after_ref, ...), custom_call_target="tpu_custom_call" | custom-call | tf_op jit(solution)/shard_map/pallas_call | solution.py:228
  31.4 0.0 collective-permute-done.4.far_sibling_ref
  31.5 7.4 %shard_map.70 = (bf16[2,2,32,128]{3,2,1,0:T(8,128)(2,1)}, bf16[2,2,32,128]{3,2,1,0:T(8,128)(2,1)}, bf16[4,2,9,128,128]{4,3,2,1,0:T(8,128)(2,1)S(1)}) custom-call(bf16[212,16,128]{2,1,0:T(8,128)(2,1)S(1)} %get-tuple-element.17.state_ref, bf16[4,2,9,128,128]{4,3,2,1,0:T(8,128)(2,1)S(1)} %get-tuple-element.18.weight_ref, ...), custom_call_target="tpu_custom_call", output_to_operand_aliasing={{2}: (1, {})} | custom-call | tf_op jit(solution)/shard_map/pallas_call | solution.py:239
Async XLA Ops:
  0.6 25.4 %collective-permute-start = (bf16[1,2,9,128,128]{4,3,2,1,0:T(8,128)(2,1)}, bf16[1,2,9,128,128]{4,3,2,1,0:T(8,128)(2,1)S(1)}, u32[]{:S(2)}, u32[]{:S(2)}) collective-permute-start(bf16[1,2,9,128,128]{4,3,2,1,0:T(8,128)(2,1)} %own_ref.1), channel_id=1, source_target_pairs={{0,18},{1,19},{2,16},{3,17},{4,22},{5,23},{6,20},{7,21},{8,26},{9,... | collective-permute-start | bytes 1769480 | tf_op jit(solution)/shard_map/ppermute | solution.py:217
  7.7 18.3 %collective-permute-start.1 = (bf16[33,16,128]{2,1,0:T(8,128)(2,1)}, bf16[33,16,128]{2,1,0:T(8,128)(2,1)S(1)}, u32[]{:S(2)}, u32[]{:S(2)}) collective-permute-start(bf16[33,16,128]{2,1,0:T(8,128)(2,1)} %get-tuple-element.13), channel_id=1, source_target_pairs={{0,4},{4,8},{8,12},{12,16},{16,20},{20,24},{24,28},{28,32},{32,36}... | collective-permute-start | bytes 405512 | tf_op jit(solution)/shard_map/ppermute | solution.py:220
  10.9 15.1 %collective-permute-start.2 = (bf16[33,16,128]{2,1,0:T(8,128)(2,1)}, bf16[33,16,128]{2,1,0:T(8,128)(2,1)S(1)}, u32[]{:S(2)}, u32[]{:S(2)}) collective-permute-start(bf16[33,16,128]{2,1,0:T(8,128)(2,1)} %get-tuple-element.14), channel_id=1, source_target_pairs={{4,0},{8,4},{12,8},{16,12},{20,16},{24,20},{28,24},{32,28},{36,32}... | collective-permute-start | bytes 405512 | tf_op jit(solution)/shard_map/ppermute | solution.py:221
  22.9 6.0 %collective-permute-start.3 = (bf16[1,2,9,128,128]{4,3,2,1,0:T(8,128)(2,1)}, bf16[1,2,9,128,128]{4,3,2,1,0:T(8,128)(2,1)S(1)}, u32[]{:S(2)}, u32[]{:S(2)}) collective-permute-start(bf16[1,2,9,128,128]{4,3,2,1,0:T(8,128)(2,1)} %own_ref.1), channel_id=1, source_target_pairs={{0,1},{1,0},{2,3},{3,2},{4,5},{5,4},{6,7},{7,6},{8,9},{9,8},{10,11... | collective-permute-start | bytes 1769480 | tf_op jit(solution)/shard_map/ppermute | solution.py:218
  26.0 5.4 %collective-permute-start.4 = (bf16[1,2,9,128,128]{4,3,2,1,0:T(8,128)(2,1)S(1)}, bf16[1,2,9,128,128]{4,3,2,1,0:T(8,128)(2,1)S(1)}, u32[]{:S(2)}, u32[]{:S(2)}) collective-permute-start(bf16[1,2,9,128,128]{4,3,2,1,0:T(8,128)(2,1)S(1)} %collective-permute-done.far_ref), channel_id=1, source_target_pairs={{0,1},{1,0},{2,3},{3,2},{4,5},{5,4},{6,7},{7,6},{8,9},{9,8},{10,11... | collective-permute-start | bytes 1769480 | tf_op jit(solution)/shard_map/ppermute | solution.py:223
  28.9 1.1 %copy-start = (bf16[1,2,9,128,128]{4,3,2,1,0:T(8,128)(2,1)S(1)}, bf16[1,2,9,128,128]{4,3,2,1,0:T(8,128)(2,1)}, u32[]{:S(2)}) copy-start(bf16[1,2,9,128,128]{4,3,2,1,0:T(8,128)(2,1)} %own_ref.1) | copy-start | bytes 1769476
  29.9 1.0 %copy-start.1 = (bf16[65,16,128]{2,1,0:T(8,128)(2,1)S(1)}, bf16[65,16,128]{2,1,0:T(8,128)(2,1)}, u32[]{:S(2)}) copy-start(bf16[65,16,128]{2,1,0:T(8,128)(2,1)} %get-tuple-element.12.fields_ref) | copy-start | bytes 798724

commit v3 on v2

--- a/solution.py
+++ b/solution.py
@@ -19,7 +19,7 @@
 CUT = 48
 
 
-def pack_kernel(atmos_ref, ocean_ref, rotation_ref, mask_ref, fields_ref, up_ref, down_ref, tile):
+def pack_kernel(atmos_ref, ocean_ref, rotation_ref, mask_ref, fields_ref, down_ref, up_ref, tile):
     for index, ref in enumerate((atmos_ref, ocean_ref)):
         value = ref[...].astype(F32).reshape(16, WIDTH, 128)
         value = jnp.swapaxes(value, 0, 1).astype(BF)
@@ -42,9 +42,7 @@
 def product(source, weight, start, stop):
     count = stop - start
     left = jnp.concatenate([source[pl.ds(start + b - 1, count)] for b in range(3)], axis=-1)
-    right = jnp.concatenate(
-        [jnp.concatenate([weight[3 * a + b] for a in range(3)], axis=1) for b in range(3)], axis=0
-    )
+    right = jnp.concatenate([jnp.concatenate([weight(3 * a + b) for a in range(3)], axis=1) for b in range(3)], axis=0)
     return lax.dot_general(
         left.reshape(count * 16, 384), right, (((1,), (0,)), ((), ())), preferred_element_type=F32
     )
@@ -82,12 +80,15 @@
     return keep.astype(BF), swap.astype(BF)
 
 
-def state_kernel(fields_ref, before_ref, after_ref, own_ref, sibling_ref, state_ref, weight_ref, semaphores):
+def state_kernel(fields_ref, after_ref, before_ref, own_ref, sibling_ref, far_ref, state_ref, weight_ref, semaphores):
     comp = lax.axis_index("comp")
-    copies = (
-        pltpu.make_async_copy(own_ref.at[0], weight_ref.at[comp], semaphores.at[0]),
-        pltpu.make_async_copy(sibling_ref.at[0], weight_ref.at[comp + 1 - 2 * lax.rem(comp, 2)], semaphores.at[1]),
-    )
+    core = lax.rem(comp, 2)
+    copies = [
+        pltpu.make_async_copy(ref.at[0], weight_ref.at[place], semaphores.at[index])
+        for index, (ref, place) in enumerate(
+            ((own_ref, comp), (sibling_ref, comp + 1 - 2 * core), (far_ref, lax.rem(comp + 2, 4)))
+        )
+    ]
     for copy in copies:
         copy.start()
 
@@ -127,23 +128,19 @@
 
 
 def main_kernel(
-    state_ref, weight_ref, far_ref, far_sibling_ref, atmos_out, ocean_out, weight_out,
-    hidden_ref, inner, ocean_ref, flux, final, semaphores,
+    state_ref, weight_in, last_ref, atmos_out, ocean_out, weight_ref, hidden_ref, inner, ocean_ref, flux, final, semaphore
 ):
     comp = lax.axis_index("comp")
-    core = lax.rem(comp, 2)
-    other = 2 - 2 * lax.div(comp, 2)
-    copies = (
-        pltpu.make_async_copy(far_ref.at[0], weight_out.at[other + core], semaphores.at[0]),
-        pltpu.make_async_copy(far_sibling_ref.at[0], weight_out.at[other + 1 - core], semaphores.at[1]),
-    )
-    for copy in copies:
-        copy.start()
+    last = 3 - comp
+    copy = pltpu.make_async_copy(last_ref.at[0], weight_ref.at[last], semaphore)
+    copy.start()
+
+    def taps(section, which):
+        return lambda index: weight_ref[section, which, index]
+
     hidden, ocean, sea, factors = (
         state_ref.at[pl.ds(TOTAL * index, TOTAL if index < 3 else 2 * len(SEAMS))] for index in range(4)
     )
-    for copy in copies:
-        copy.wait()
 
     def load(ref, span):
         return ref[span].astype(F32)
@@ -173,20 +170,21 @@
                     span = pl.ds(start, stop - start)
                     flux[span] = (load(hidden, span) + load(ocean, span)).astype(BF)
                     close_seams(flux, factors, seams)
-            weight = weight_out.at[section]
+            if step == 0:
+                pl.when(last == section)(copy.wait)
             done += 1
-            convolve(source, weight.at[0], done, lambda span, value: gelu(value), inner)
+            convolve(source, taps(section, 0), done, lambda span, value: gelu(value), inner)
             done += 1
             if section == 3:
                 base = ocean
                 convolve(
-                    inner, weight.at[1], done,
+                    inner, taps(section, 1), done,
                     lambda span, value: load(base, span) + load(sea, span) * value, ocean_ref,
                 )
                 ocean = ocean_ref
             else:
                 base = hidden
-                convolve(inner, weight.at[1], done, lambda span, value: load(base, span) + value, hidden_ref)
+                convolve(inner, taps(section, 1), done, lambda span, value: load(base, span) + value, hidden_ref)
                 hidden = hidden_ref
 
     for source, out in ((hidden, atmos_out), (ocean, ocean_out)):
@@ -198,10 +196,10 @@
 def per_device(atmos_state, ocean_state, conv_weight, rotation, sea_mask):
     tiles = lax.axis_size("pix")
     vmem = pl.BlockSpec(memory_space=pltpu.VMEM)
-    fields, up, down = pl.pallas_call(
+    fields, down, up = pl.pallas_call(
         pack_kernel,
         out_shape=(
-            jax.ShapeDtypeStruct((2 * WIDTH + 1, 16, 128), BF),
+            pltpu.VMEM((2 * WIDTH + 1, 16, 128), BF),
             jax.ShapeDtypeStruct((2 * DEPTH + 1, 16, 128), BF),
             jax.ShapeDtypeStruct((2 * DEPTH + 1, 16, 128), BF),
         ),
@@ -215,43 +213,37 @@
     swap = [(p * 4 + c, p * 4 + (c ^ 1)) for p in range(tiles) for c in range(4)]
     across = [(p * 4 + c, (p ^ flip) * 4 + (c ^ 2)) for p in range(tiles) for c in range(4)]
     far = lax.ppermute(conv_weight, names, across)
+    rightward = [(i, (i + 1) % tiles) for i in range(tiles)]
     sibling = lax.ppermute(conv_weight, names, swap)
-    rightward = [(i, (i + 1) % tiles) for i in range(tiles)]
+    after = lax.ppermute(down, "pix", [(j, i) for i, j in rightward])
     before = lax.ppermute(up, "pix", rightward)
-    after = lax.ppermute(down, "pix", [(j, i) for i, j in rightward])
-    far, before, after = lax.optimization_barrier((far, before, after))
+    far, _ = lax.optimization_barrier((far, (up, down)))
     far_sibling = lax.ppermute(far, names, swap)
 
     anywhere = pl.BlockSpec(memory_space=pl.ANY)
-    all_weights = jax.ShapeDtypeStruct((4,) + conv_weight.shape[1:], BF)
+    section_weights = pltpu.VMEM((4,) + conv_weight.shape[1:], BF)
     params = pltpu.CompilerParams(vmem_limit_bytes=40 << 20)
     state, weight = pl.pallas_call(
         state_kernel,
-        out_shape=(jax.ShapeDtypeStruct((3 * TOTAL + 2 * len(SEAMS), 16, 128), BF), all_weights),
-        in_specs=[vmem, vmem, vmem, anywhere, anywhere],
+        out_shape=(pltpu.VMEM((3 * TOTAL + 2 * len(SEAMS), 16, 128), BF), section_weights),
+        in_specs=[vmem, vmem, vmem, pl.BlockSpec(memory_space=pltpu.HBM), anywhere, anywhere],
         out_specs=(vmem, vmem),
-        scratch_shapes=[pltpu.SemaphoreType.DMA((2,))],
+        scratch_shapes=[pltpu.SemaphoreType.DMA((3,))],
+        cost_estimate=pl.CostEstimate(flops=2 * 10**10, bytes_accessed=1 << 20, transcendentals=0),
         compiler_params=params,
-    )(fields, before, after, conv_weight, sibling)
+    )(fields, after, before, pltpu.with_memory_space_constraint(conv_weight, pltpu.HBM), sibling, far)
 
     band = jax.ShapeDtypeStruct((2, 2, WIDTH, 128), BF)
     field = pltpu.VMEM((TOTAL, 16, 128), BF)
     return pl.pallas_call(
         main_kernel,
-        out_shape=(band, band, all_weights),
-        in_specs=[vmem, vmem, anywhere, anywhere],
+        out_shape=(band, band, section_weights),
+        in_specs=[vmem, vmem, anywhere],
         out_specs=(vmem, vmem, vmem),
         input_output_aliases={1: 2},
-        scratch_shapes=[
-            field,
-            field,
-            field,
-            field,
-            pltpu.VMEM((16, WIDTH, 128), F32),
-            pltpu.SemaphoreType.DMA((2,)),
-        ],
+        scratch_shapes=[field, field, field, field, pltpu.VMEM((16, WIDTH, 128), F32), pltpu.SemaphoreType.DMA(())],
         compiler_params=params,
-    )(state, weight, far, far_sibling)[:2]
+    )(state, weight, far_sibling)[:2]
 
 
 def solution(mesh):

time: 39.2 us -> 44.4 us (1.13)
  waiting for transfers between devices: 0.01 us -> 7.06 us
  local copies, waits for them, and re-layouts: 2.01 us -> 0 us
  Pallas kernels: 9.79 us -> 10.9 us
  starting transfers between devices: 26.3 us -> 25.4 us
    ppermute x1, waiting for transfers between devices: 0.01 us -> 7.05 us  [per_device(): before = lax.ppermute(up, 'pix', rightward)]
    ppermute x1, starting transfers between devices: 3.15 us -> 5.49 us  [per_device(): sibling = lax.ppermute(conv_weight, names, swap)]
    unnamed x4 -> x0, local copies, waits for them, and re-layouts: 2.01 us -> none
    ppermute x1, starting transfers between devices: 11.9 us -> 10.6 us  [per_device(): after = lax.ppermute(down, 'pix', [(j, i) for i, j in rightward])]
    ppermute x1, starting transfers between devices: 3.19 us -> 1.92 us  [per_device(): before = lax.ppermute(up, 'pix', rightward)]
    pallas_call x3, Pallas kernels: 9.79 us -> 10.9 us  [the longest x1 7.97 us: per_device(): pl.pallas_call(main_kernel, out_shape=(band, band, section_weights), in_s...]
    ppermute x1, starting transfers between devices: 2.81 us -> 2.2 us  [per_device(): far_sibling = lax.ppermute(far, names, swap)]
  transfers between devices with their start and end apart: 5 -> 5, of which waited for: 0 -> 1; matrix products, arithmetic and copies ran while one was open for 0% -> 0% of each run, Pallas kernels for 6% -> 7%
where the time goes in v3:
time: 44.4 us; the launch traced here: 44.1 us
  starting transfers between devices  25.4 us (57%)
  Pallas kernels  10.9 us (25%)
  waiting for transfers between devices  7.06 us (16%)
  between operations  0.7 us (2%)
    ppermute x1, starting transfers between devices, per_device(): after = lax.ppermute(down, 'pix', [(j, i) for i, j in rightward])  10.6 us
    pallas_call x1, Pallas kernels, per_device(): pl.pallas_call(main_kernel, out_shape=(band, band, section_weights), in_s...  7.97 us
    ppermute x1, waiting for transfers between devices, per_device(): before = lax.ppermute(up, 'pix', rightward)  7.05 us
    ppermute x1, starting transfers between devices, per_device(): sibling = lax.ppermute(conv_weight, names, swap)  5.49 us
    ppermute x1, starting transfers between devices, per_device(): far = lax.ppermute(conv_weight, names, across)  5.22 us
    ppermute x1, starting transfers between devices, per_device(): far_sibling = lax.ppermute(far, names, swap)  2.2 us
    ppermute x1, starting transfers between devices, per_device(): before = lax.ppermute(up, 'pix', rightward)  1.92 us
    pallas_call x1, Pallas kernels, per_device(): pl.pallas_call(pack_kernel, out_shape=(pltpu.VMEM((2 * WIDTH + 1, 16, 128...  1.83 us
  transfers between devices with their start and end apart: 5, of which 1 were waited for; matrix products, arithmetic and copies ran while one was open for 0% of the time, Pallas kernels for 7%

profile of v3, /device:TPU:1, one launch (start us, length us, event | category | flops | bytes accessed | tf_op | source)
XLA Modules:
  0.0 44.1 jit_solution(13792147713930198953)
XLA Ops:
  0.6 5.2 %collective-permute-start.3 = (bf16[1,2,9,128,128]{4,3,2,1,0:T(8,128)(2,1)}, bf16[1,2,9,128,128]{4,3,2,1,0:T(8,128)(2,1)S(1)}, u32[]{:S(2)}, u32[]{:S(2)}) collective-permute-start(bf16[1,2,9,128,128]{4,3,2,1,0:T(8,128)(2,1)} %own_ref.1), channel_id=1, source_target_pairs={{0,18},{1,19},{2,16},{3,17},{4,22},{5,23},{6,20},{7,21},{8,26},{9,... | collective-permute-start | bytes 1769480 | tf_op jit(solution)/shard_map/ppermute | solution.py:215
  5.9 5.5 %collective-permute-start.2 = (bf16[1,2,9,128,128]{4,3,2,1,0:T(8,128)(2,1)}, bf16[1,2,9,128,128]{4,3,2,1,0:T(8,128)(2,1)S(1)}, u32[]{:S(2)}, u32[]{:S(2)}) collective-permute-start(bf16[1,2,9,128,128]{4,3,2,1,0:T(8,128)(2,1)} %own_ref.1), channel_id=1, source_target_pairs={{0,1},{1,0},{2,3},{3,2},{4,5},{5,4},{6,7},{7,6},{8,9},{9,8},{10,11... | collective-permute-start | bytes 1769480 | tf_op jit(solution)/shard_map/ppermute | solution.py:217
  11.4 1.8 %shard_map.68 = (bf16[65,16,128]{2,1,0:T(8,128)(2,1)S(1)}, bf16[33,16,128]{2,1,0:T(8,128)(2,1)}, bf16[33,16,128]{2,1,0:T(8,128)(2,1)}) custom-call(bf16[2,8,32,128]{3,2,1,0:T(8,128)(2,1)} %atmos_ref.1, bf16[2,8,32,128]{3,2,1,0:T(8,128)(2,1)} %ocean_ref.1, s32[1,2]{1,0:T(1,128)} %rotation_ref.1, s32[8,32]{1,0:T(8,128)} %mask_ref.1), custom_call_target="tpu_custom_call" | custom-call | tf_op jit(solution)/shard_map/pallas_call | solution.py:199
  13.2 10.6 %collective-permute-start = (bf16[33,16,128]{2,1,0:T(8,128)(2,1)}, bf16[33,16,128]{2,1,0:T(8,128)(2,1)S(1)}, u32[]{:S(2)}, u32[]{:S(2)}) collective-permute-start(bf16[33,16,128]{2,1,0:T(8,128)(2,1)} %get-tuple-element.11), channel_id=1, source_target_pairs={{4,0},{8,4},{12,8},{16,12},{20,16},{24,20},{28,24},{32,28},{36,32}... | collective-permute-start | bytes 405512 | tf_op jit(solution)/shard_map/ppermute | solution.py:218
  23.8 1.9 %collective-permute-start.1 = (bf16[33,16,128]{2,1,0:T(8,128)(2,1)}, bf16[33,16,128]{2,1,0:T(8,128)(2,1)S(1)}, u32[]{:S(2)}, u32[]{:S(2)}) collective-permute-start(bf16[33,16,128]{2,1,0:T(8,128)(2,1)} %get-tuple-element.12), channel_id=1, source_target_pairs={{0,4},{4,8},{8,12},{12,16},{16,20},{20,24},{24,28},{28,32},{32,36}... | collective-permute-start | bytes 405512 | tf_op jit(solution)/shard_map/ppermute | solution.py:219
  25.7 0.0 collective-permute-done.3.far_ref
  25.7 2.2 %collective-permute-start.4 = (bf16[1,2,9,128,128]{4,3,2,1,0:T(8,128)(2,1)S(1)}, bf16[1,2,9,128,128]{4,3,2,1,0:T(8,128)(2,1)S(1)}, u32[]{:S(2)}, u32[]{:S(2)}) collective-permute-start(bf16[1,2,9,128,128]{4,3,2,1,0:T(8,128)(2,1)S(1)} %collective-permute-done.3.far_ref), channel_id=1, source_target_pairs={{0,1},{1,0},{2,3},{3,2},{4,5},{5,4},{6,7},{7,6},{8,9},{9,8},{10,11... | collective-permute-start | bytes 1769480 | tf_op jit(solution)/shard_map/ppermute | solution.py:221
  27.9 0.0 collective-permute-done.after_ref
  27.9 7.1 %collective-permute-done.1.before_ref = bf16[33,16,128]{2,1,0:T(8,128)(2,1)S(1)} collective-permute-done((bf16[33,16,128]{2,1,0:T(8,128)(2,1)}, bf16[33,16,128]{2,1,0:T(8,128)(2,1)S(1)}, u32[]{:S(2)}, u32[]{:S(2)}) %collective-permute-start.1) | collective-permute-done | bytes 135200 | tf_op jit(solution)/shard_map/ppermute | solution.py:219
  35.0 0.0 collective-permute-done.2.sibling_ref
  35.0 1.1 %shard_map.69 = (bf16[212,16,128]{2,1,0:T(8,128)(2,1)S(1)}, bf16[4,2,9,128,128]{4,3,2,1,0:T(8,128)(2,1)S(1)}) custom-call(bf16[65,16,128]{2,1,0:T(8,128)(2,1)S(1)} %get-tuple-element.10.fields_ref, bf16[33,16,128]{2,1,0:T(8,128)(2,1)S(1)} %collective-permute-done.after_ref, bf16[33,16,128]{2,1,0:T(8,128)(2,1)S(1)} %collective-permute-done.1.before_ref, ...), custom_call_target="tpu_custom_call" | custom-call | flops 20000000000 | bytes 1048576 | tf_op jit(solution)/shard_map/pallas_call | solution.py:226
  36.1 0.0 collective-permute-done.4.last_ref
  36.1 8.0 %shard_map.70 = (bf16[2,2,32,128]{3,2,1,0:T(8,128)(2,1)}, bf16[2,2,32,128]{3,2,1,0:T(8,128)(2,1)}, bf16[4,2,9,128,128]{4,3,2,1,0:T(8,128)(2,1)S(1)}) custom-call(bf16[212,16,128]{2,1,0:T(8,128)(2,1)S(1)} %get-tuple-element.14.state_ref, bf16[4,2,9,128,128]{4,3,2,1,0:T(8,128)(2,1)S(1)} %get-tuple-element.15.weight_in, ...), custom_call_target="tpu_custom_call", output_to_operand_aliasing={{2}: (1, {})} | custom-call | tf_op jit(solution)/shard_map/pallas_call | solution.py:238
Async XLA Ops:
  0.6 25.1 %collective-permute-start.3 = (bf16[1,2,9,128,128]{4,3,2,1,0:T(8,128)(2,1)}, bf16[1,2,9,128,128]{4,3,2,1,0:T(8,128)(2,1)S(1)}, u32[]{:S(2)}, u32[]{:S(2)}) collective-permute-start(bf16[1,2,9,128,128]{4,3,2,1,0:T(8,128)(2,1)} %own_ref.1), channel_id=1, source_target_pairs={{0,18},{1,19},{2,16},{3,17},{4,22},{5,23},{6,20},{7,21},{8,26},{9,... | collective-permute-start | bytes 1769480 | tf_op jit(solution)/shard_map/ppermute | solution.py:215
  5.9 29.1 %collective-permute-start.2 = (bf16[1,2,9,128,128]{4,3,2,1,0:T(8,128)(2,1)}, bf16[1,2,9,128,128]{4,3,2,1,0:T(8,128)(2,1)S(1)}, u32[]{:S(2)}, u32[]{:S(2)}) collective-permute-start(bf16[1,2,9,128,128]{4,3,2,1,0:T(8,128)(2,1)} %own_ref.1), channel_id=1, source_target_pairs={{0,1},{1,0},{2,3},{3,2},{4,5},{5,4},{6,7},{7,6},{8,9},{9,8},{10,11... | collective-permute-start | bytes 1769480 | tf_op jit(solution)/shard_map/ppermute | solution.py:217
  13.2 14.8 %collective-permute-start = (bf16[33,16,128]{2,1,0:T(8,128)(2,1)}, bf16[33,16,128]{2,1,0:T(8,128)(2,1)S(1)}, u32[]{:S(2)}, u32[]{:S(2)}) collective-permute-start(bf16[33,16,128]{2,1,0:T(8,128)(2,1)} %get-tuple-element.11), channel_id=1, source_target_pairs={{4,0},{8,4},{12,8},{16,12},{20,16},{24,20},{28,24},{32,28},{36,32}... | collective-permute-start | bytes 405512 | tf_op jit(solution)/shard_map/ppermute | solution.py:218
  23.8 11.2 %collective-permute-start.1 = (bf16[33,16,128]{2,1,0:T(8,128)(2,1)}, bf16[33,16,128]{2,1,0:T(8,128)(2,1)S(1)}, u32[]{:S(2)}, u32[]{:S(2)}) collective-permute-start(bf16[33,16,128]{2,1,0:T(8,128)(2,1)} %get-tuple-element.12), channel_id=1, source_target_pairs={{0,4},{4,8},{8,12},{12,16},{16,20},{20,24},{24,28},{28,32},{32,36}... | collective-permute-start | bytes 405512 | tf_op jit(solution)/shard_map/ppermute | solution.py:219
  25.7 10.4 %collective-permute-start.4 = (bf16[1,2,9,128,128]{4,3,2,1,0:T(8,128)(2,1)S(1)}, bf16[1,2,9,128,128]{4,3,2,1,0:T(8,128)(2,1)S(1)}, u32[]{:S(2)}, u32[]{:S(2)}) collective-permute-start(bf16[1,2,9,128,128]{4,3,2,1,0:T(8,128)(2,1)S(1)} %collective-permute-done.3.far_ref), channel_id=1, source_target_pairs={{0,1},{1,0},{2,3},{3,2},{4,5},{5,4},{6,7},{7,6},{8,9},{9,8},{10,11... | collective-permute-start | bytes 1769480 | tf_op jit(solution)/shard_map/ppermute | solution.py:221

commit v4 on v3

v4 whole, which is shorter than its diff:
```python
import functools

import jax
import jax.numpy as jnp
from jax import lax
from jax.experimental import pallas as pl
from jax.experimental.pallas import tpu as pltpu
from jax.sharding import PartitionSpec as P

STEPS = 2
BF = jnp.bfloat16
F32 = jnp.float32

DEPTH = 16
WIDTH = 32
OWN = DEPTH + 2
RIGHT = OWN + WIDTH + 2
TOTAL = RIGHT + DEPTH
PARTS = 4


def pack_kernel(atmos_ref, ocean_ref, rotation_ref, mask_ref, fields_ref, up_ref, down_ref, tile):
    for index, ref in enumerate((atmos_ref, ocean_ref)):
        value = ref[...].astype(F32).reshape(16, WIDTH, 128)
        value = jnp.swapaxes(value, 0, 1).astype(BF)
        fields_ref[pl.ds(index * WIDTH, WIDTH)] = value
        up_ref[pl.ds(index * DEPTH, DEPTH)] = value[WIDTH - DEPTH :]
        down_ref[pl.ds(index * DEPTH, DEPTH)] = value[:DEPTH]
    lane = lax.broadcasted_iota(jnp.int32, (16, 128), 1)
    first = rotation_ref[0, 0].astype(F32)
    second = rotation_ref[0, 1].astype(F32)
    tile[...] = jnp.where(lane == 64, first, jnp.where(lane == 65, second, 0.0))
    mask = mask_ref[...].astype(F32)
    tile[0:8, 0:WIDTH] = mask
    tile[8:16, 0:WIDTH] = mask
    packed = tile[...].astype(BF)
    fields_ref[2 * WIDTH] = packed
    up_ref[2 * DEPTH] = packed
    down_ref[2 * DEPTH] = packed


def shift_rows(value, by):
    count = value.shape[0]
    row = lax.broadcasted_iota(jnp.int32, (1, 8, 128), 1)
    rolled = pltpu.roll(value.reshape(count * 2, 8, 128), by % 8, 1)
    return jnp.where(row == (0 if by == 1 else 7), 0.0, rolled).reshape(count, 16, 128)


def convolve_columns(field, weight, start, stop):
    count = stop - start
    left = jnp.concatenate([ref[pl.ds(start + b - 1, count)] for b in range(3) for ref in field], axis=-1)
    nothing = jnp.zeros((128, 128), BF)
    right = []
    for b in range(3):
        right.append(jnp.concatenate([weight[3 + b], weight[6 + b]], axis=1))
        right.append(jnp.concatenate([weight[b], nothing], axis=1))
    value = lax.dot_general(
        left.reshape(count * 16, 768), jnp.concatenate(right, axis=0), (((1,), (0,)), ((), ())),
        preferred_element_type=F32,
    )
    return value[:, :128].reshape(count, 16, 128) + shift_rows(value[:, 128:].reshape(count, 16, 128), -1)


def store(field, span, value):
    field[0][span] = value.astype(BF)
    field[1][span] = shift_rows(value, 1).astype(BF)


def gelu(value):
    half = 0.5 * value
    return half + half * jnp.tanh(value * (0.7978845608028654 + 0.035677408136300125 * (value * value)))


SEAMS = ((DEPTH, OWN), (DEPTH + 1, DEPTH - 1), (OWN + WIDTH, RIGHT), (RIGHT - 1, OWN + WIDTH - 1))


def close_seams(field, factors):
    for ref in field:
        for index, (place, origin) in enumerate(SEAMS):
            value = ref[origin].astype(F32)
            keep, swap = factors[2 * index].astype(F32), factors[2 * index + 1].astype(F32)
            ref[place] = (keep * value + swap * pltpu.roll(value, 64, 1)).astype(BF)


def parts_of(state_ref):
    return [state_ref.at[pl.ds(TOTAL * index, TOTAL if index < 4 else 2 * len(SEAMS))] for index in range(5)]


def turn_factors(code):
    lane = lax.broadcasted_iota(jnp.int32, (16, 128), 1)
    side = jnp.where(lane < 64, -1.0, 1.0)
    keep = jnp.where(code == 0.0, 1.0, jnp.where(code == 2.0, -1.0, 0.0))
    swap = jnp.where(code == 1.0, side, jnp.where(code == 3.0, -side, 0.0))
    return keep.astype(BF), swap.astype(BF)


def state_kernel(fields_ref, before_ref, after_ref, own_ref, sibling_ref, far_ref, state_ref, weight_ref, semaphores):
    comp = lax.axis_index("comp")
    core = lax.rem(comp, 2)
    copies = [
        pltpu.make_async_copy(ref.at[0], weight_ref.at[place], semaphores.at[index])
        for index, (ref, place) in enumerate(
            ((own_ref, comp), (sibling_ref, comp + 1 - 2 * core), (far_ref, lax.rem(comp + 2, 4)))
        )
    ]
    for copy in copies:
        copy.start()

    def broadcast(tile, column):
        return jnp.broadcast_to(tile[:, column : column + 1], (16, 128))

    own_tile = fields_ref[2 * WIDTH].astype(F32)
    before_tile = before_ref[2 * DEPTH].astype(F32)
    after_tile = after_ref[2 * DEPTH].astype(F32)
    hidden, hidden_down, ocean, sea, factors = parts_of(state_ref)
    for index, (tile, lane) in enumerate(((before_tile, 65), (own_tile, 64), (own_tile, 65), (after_tile, 64))):
        factors[2 * index], factors[2 * index + 1] = turn_factors(broadcast(tile, lane))
    for column in range(DEPTH):
        sea[column] = broadcast(before_tile, WIDTH - DEPTH + column).astype(BF)
        sea[RIGHT + column] = broadcast(after_tile, column).astype(BF)
    for column in range(WIDTH):
        sea[OWN + column] = broadcast(own_tile, column).astype(BF)
    nothing = jnp.zeros((2, 16, 128), BF)
    for ref in (ocean, sea):
        ref[pl.ds(DEPTH, 2)] = nothing
        ref[pl.ds(RIGHT - 2, 2)] = nothing
    for ref, origin, count, place in (
        (before_ref, 0, DEPTH, 0),
        (fields_ref, 0, WIDTH, OWN),
        (after_ref, 0, DEPTH, RIGHT),
    ):
        span = pl.ds(place, count)
        ocean_value = ref[pl.ds(origin + count, count)]
        ocean[span] = ocean_value
        atmos_value = ref[pl.ds(origin, count)].astype(F32)
        store((hidden, hidden_down), span, atmos_value + sea[span].astype(F32) * ocean_value.astype(F32))
    close_seams((hidden, hidden_down), factors)
    for copy in copies:
        copy.wait()


def main_kernel(
    state_ref, weight_in, last_ref, atmos_out, ocean_out, weight_ref,
    hidden_ref, hidden_down, inner, inner_down, flux, flux_down, ocean_ref, final, semaphore,
):
    comp = lax.axis_index("comp")
    copy = pltpu.make_async_copy(last_ref.at[0], weight_ref.at[3 - comp], semaphore)
    copy.start()
    hidden, first_down, ocean, sea, factors = parts_of(state_ref)
    field = (hidden, first_down)
    copy.wait()

    def load(ref, span):
        return ref[span].astype(F32)

    def pieces(done):
        count = TOTAL - 2 * done
        bounds = [done + count * part // PARTS for part in range(PARTS + 1)]
        return zip(bounds[:-1], bounds[1:])

    done = 0
    for step in range(STEPS):
        if step > 0:
            for start, stop in pieces(done):
                span = pl.ds(start, stop - start)
                store(field, span, load(hidden, span) + load(sea, span) * load(ocean, span))
            close_seams(field, factors)
        for section in range(4):
            source = field
            if section == 3:
                source = (flux, flux_down)
                for start, stop in pieces(done):
                    span = pl.ds(start, stop - start)
                    store(source, span, load(hidden, span) + load(ocean, span))
                close_seams(source, factors)
            done += 1
            for start, stop in pieces(done):
                value = convolve_columns(source, weight_ref.at[section, 0], start, stop)
                store((inner, inner_down), pl.ds(start, stop - start), gelu(value))
            close_seams((inner, inner_down), factors)
            done += 1
            for start, stop in pieces(done):
                span = pl.ds(start, stop - start)
                value = convolve_columns((inner, inner_down), weight_ref.at[section, 1], start, stop)
                if section == 3:
                    ocean_ref[span] = (load(ocean, span) + load(sea, span) * value).astype(BF)
                else:
                    store((hidden_ref, hidden_down), span, load(hidden, span) + value)
            if section == 3:
                ocean = ocean_ref
            else:
                hidden, field = hidden_ref, (hidden_ref, hidden_down)
                close_seams(field, factors)

    for source, out in ((hidden, atmos_out), (ocean, ocean_out)):
        final[...] = jnp.swapaxes(source[pl.ds(OWN, WIDTH)].astype(F32), 0, 1)
        for member in range(2):
            out[member] = final[pl.ds(member * 8 + 2 * comp, 2)].astype(BF)


def per_device(atmos_state, ocean_state, conv_weight, rotation, sea_mask):
    tiles = lax.axis_size("pix")
    vmem = pl.BlockSpec(memory_space=pltpu.VMEM)
    fields, up, down = pl.pallas_call(
        pack_kernel,
        out_shape=(
            pltpu.VMEM((2 * WIDTH + 1, 16, 128), BF),
            jax.ShapeDtypeStruct((2 * DEPTH + 1, 16, 128), BF),
            jax.ShapeDtypeStruct((2 * DEPTH + 1, 16, 128), BF),
        ),
        in_specs=[vmem, vmem, pl.BlockSpec(memory_space=pltpu.SMEM), vmem],
        out_specs=(vmem, vmem, vmem),
        scratch_shapes=[pltpu.VMEM((16, 128), F32)],
    )(atmos_state, ocean_state, rotation, sea_mask)

    names = ("pix", "comp")
    flip = 4 if tiles % 8 == 0 else 0
    swap = [(p * 4 + c, p * 4 + (c ^ 1)) for p in range(tiles) for c in range(4)]
    across = [(p * 4 + c, (p ^ flip) * 4 + (c ^ 2)) for p in range(tiles) for c in range(4)]
    far = lax.ppermute(conv_weight, names, across)
    rightward = [(i, (i + 1) % tiles) for i in range(tiles)]
    sibling = lax.ppermute(conv_weight, names, swap)
    before = lax.ppermute(up, "pix", rightward)
    after = lax.ppermute(down, "pix", [(j, i) for i, j in rightward])
    far, _ = lax.optimization_barrier((far, (up, down)))
    far_sibling = lax.ppermute(far, names, swap)

    anywhere = pl.BlockSpec(memory_space=pl.ANY)
    section_weights = pltpu.VMEM((4,) + conv_weight.shape[1:], BF)
    params = pltpu.CompilerParams(vmem_limit_bytes=40 << 20)
    state, weight = pl.pallas_call(
        state_kernel,
        out_shape=(pltpu.VMEM((4 * TOTAL + 2 * len(SEAMS), 16, 128), BF), section_weights),
        in_specs=[vmem, vmem, vmem, pl.BlockSpec(memory_space=pltpu.HBM), anywhere, anywhere],
        out_specs=(vmem, vmem),
        scratch_shapes=[pltpu.SemaphoreType.DMA((3,))],
        cost_estimate=pl.CostEstimate(flops=2 * 10**10, bytes_accessed=1 << 20, transcendentals=0),
        compiler_params=params,
    )(fields, before, after, pltpu.with_memory_space_constraint(conv_weight, pltpu.HBM), sibling, far)

    band = jax.ShapeDtypeStruct((2, 2, WIDTH, 128), BF)
    field = pltpu.VMEM((TOTAL, 16, 128), BF)
    return pl.pallas_call(
        main_kernel,
        out_shape=(band, band, section_weights),
        in_specs=[vmem, vmem, anywhere],
        out_specs=(vmem, vmem, vmem),
        input_output_aliases={1: 2},
        scratch_shapes=[field] * 7 + [pltpu.VMEM((16, WIDTH, 128), F32), pltpu.SemaphoreType.DMA(())],
        compiler_params=params,
    )(state, weight, far_sibling)[:2]


def solution(mesh):
    in_specs = (
        P(None, None, "pix", None),
        P(None, None, "pix", None),
        P("comp", None, None, None, None),
        P("pix", None),
        P(None, "pix"),
    )
    out_specs = (P(None, "comp", "pix", None), P(None, "comp", "pix", None))
    return jax.shard_map(
        per_device, mesh=mesh, in_specs=in_specs, out_specs=out_specs, check_vma=False
    )
```

time: 44.4 us -> 37.3 us (0.84)
  waiting for transfers between devices: 7.06 us -> 1.08 us
  Pallas kernels: 10.9 us -> 9.79 us
    ppermute x1, waiting for transfers between devices: 7.05 us -> 0.01 us  [per_device(): before = lax.ppermute(up, 'pix', rightward)]
    pallas_call x1, Pallas kernels: 7.97 us -> 6.87 us  [per_device(): pl.pallas_call(main_kernel, out_shape=(band, band, section_weights), in_s...]
    ppermute x1, waiting for transfers between devices: 0.01 us -> 1.07 us  [per_device(): after = lax.ppermute(down, 'pix', [(j, i) for i, j in rightward])]
  transfers between devices with their start and end apart: 5 -> 5, of which waited for: 1 -> 1; matrix products, arithmetic and copies ran while one was open for 0% -> 0% of each run, Pallas kernels for 7% -> 8%
where the time goes in v4:
time: 37.3 us; the launch traced here: 37 us
  starting transfers between devices  25.4 us (68%)
  Pallas kernels  9.79 us (26%)
  waiting for transfers between devices  1.08 us (3%)
  between operations  0.7 us (2%)
    ppermute x1, starting transfers between devices, per_device(): after = lax.ppermute(down, 'pix', [(j, i) for i, j in rightward])  10.6 us
    pallas_call x1, Pallas kernels, per_device(): pl.pallas_call(main_kernel, out_shape=(band, band, section_weights), in_s...  6.87 us
    ppermute x1, starting transfers between devices, per_device(): sibling = lax.ppermute(conv_weight, names, swap)  5.49 us
    ppermute x1, starting transfers between devices, per_device(): far = lax.ppermute(conv_weight, names, across)  5.22 us
    ppermute x1, starting transfers between devices, per_device(): far_sibling = lax.ppermute(far, names, swap)  2.2 us
    ppermute x1, starting transfers between devices, per_device(): before = lax.ppermute(up, 'pix', rightward)  1.91 us
    pallas_call x1, Pallas kernels, per_device(): pl.pallas_call(pack_kernel, out_shape=(pltpu.VMEM((2 * WIDTH + 1, 16, 128...  1.83 us
    pallas_call x1, Pallas kernels, per_device(): pl.pallas_call(state_kernel, out_shape=(pltpu.VMEM((4 * TOTAL + 2 * len(S...  1.09 us
  transfers between devices with their start and end apart: 5, of which 1 were waited for; matrix products, arithmetic and copies ran while one was open for 0% of the time, Pallas kernels for 8%

profile of v4, /device:TPU:1, one launch (start us, length us, event | category | flops | bytes accessed | tf_op | source)
XLA Modules:
  0.0 37.0 jit_solution(10579195934305300780)
XLA Ops:
  0.6 5.2 %collective-permute-start.3 = (bf16[1,2,9,128,128]{4,3,2,1,0:T(8,128)(2,1)}, bf16[1,2,9,128,128]{4,3,2,1,0:T(8,128)(2,1)S(1)}, u32[]{:S(2)}, u32[]{:S(2)}) collective-permute-start(bf16[1,2,9,128,128]{4,3,2,1,0:T(8,128)(2,1)} %own_ref.1), channel_id=1, source_target_pairs={{0,18},{1,19},{2,16},{3,17},{4,22},{5,23},{6,20},{7,21},{8,26},{9,... | collective-permute-start | bytes 1769480 | tf_op jit(solution)/shard_map/ppermute | solution.py:220
  5.9 5.5 %collective-permute-start.2 = (bf16[1,2,9,128,128]{4,3,2,1,0:T(8,128)(2,1)}, bf16[1,2,9,128,128]{4,3,2,1,0:T(8,128)(2,1)S(1)}, u32[]{:S(2)}, u32[]{:S(2)}) collective-permute-start(bf16[1,2,9,128,128]{4,3,2,1,0:T(8,128)(2,1)} %own_ref.1), channel_id=1, source_target_pairs={{0,1},{1,0},{2,3},{3,2},{4,5},{5,4},{6,7},{7,6},{8,9},{9,8},{10,11... | collective-permute-start | bytes 1769480 | tf_op jit(solution)/shard_map/ppermute | solution.py:222
  11.4 1.8 %shard_map.68 = (bf16[65,16,128]{2,1,0:T(8,128)(2,1)S(1)}, bf16[33,16,128]{2,1,0:T(8,128)(2,1)}, bf16[33,16,128]{2,1,0:T(8,128)(2,1)}) custom-call(bf16[2,8,32,128]{3,2,1,0:T(8,128)(2,1)} %atmos_ref.1, bf16[2,8,32,128]{3,2,1,0:T(8,128)(2,1)} %ocean_ref.1, s32[1,2]{1,0:T(1,128)} %rotation_ref.1, s32[8,32]{1,0:T(8,128)} %mask_ref.1), custom_call_target="tpu_custom_call" | custom-call | tf_op jit(solution)/shard_map/pallas_call | solution.py:204
  13.2 1.9 %collective-permute-start = (bf16[33,16,128]{2,1,0:T(8,128)(2,1)}, bf16[33,16,128]{2,1,0:T(8,128)(2,1)S(1)}, u32[]{:S(2)}, u32[]{:S(2)}) collective-permute-start(bf16[33,16,128]{2,1,0:T(8,128)(2,1)} %get-tuple-element.11), channel_id=1, source_target_pairs={{0,4},{4,8},{8,12},{12,16},{16,20},{20,24},{24,28},{28,32},{32,36}... | collective-permute-start | bytes 405512 | tf_op jit(solution)/shard_map/ppermute | solution.py:223
  15.1 10.6 %collective-permute-start.1 = (bf16[33,16,128]{2,1,0:T(8,128)(2,1)}, bf16[33,16,128]{2,1,0:T(8,128)(2,1)S(1)}, u32[]{:S(2)}, u32[]{:S(2)}) collective-permute-start(bf16[33,16,128]{2,1,0:T(8,128)(2,1)} %get-tuple-element.12), channel_id=1, source_target_pairs={{4,0},{8,4},{12,8},{16,12},{20,16},{24,20},{28,24},{32,28},{36,32}... | collective-permute-start | bytes 405512 | tf_op jit(solution)/shard_map/ppermute | solution.py:224
  25.7 0.0 collective-permute-done.3.far_ref
  25.7 2.2 %collective-permute-start.4 = (bf16[1,2,9,128,128]{4,3,2,1,0:T(8,128)(2,1)S(1)}, bf16[1,2,9,128,128]{4,3,2,1,0:T(8,128)(2,1)S(1)}, u32[]{:S(2)}, u32[]{:S(2)}) collective-permute-start(bf16[1,2,9,128,128]{4,3,2,1,0:T(8,128)(2,1)S(1)} %collective-permute-done.3.far_ref), channel_id=1, source_target_pairs={{0,1},{1,0},{2,3},{3,2},{4,5},{5,4},{6,7},{7,6},{8,9},{9,8},{10,11... | collective-permute-start | bytes 1769480 | tf_op jit(solution)/shard_map/ppermute | solution.py:226
  27.9 0.0 collective-permute-done.before_ref
  27.9 1.1 %collective-permute-done.1.after_ref = bf16[33,16,128]{2,1,0:T(8,128)(2,1)S(1)} collective-permute-done((bf16[33,16,128]{2,1,0:T(8,128)(2,1)}, bf16[33,16,128]{2,1,0:T(8,128)(2,1)S(1)}, u32[]{:S(2)}, u32[]{:S(2)}) %collective-permute-start.1) | collective-permute-done | bytes 135200 | tf_op jit(solution)/shard_map/ppermute | solution.py:224
  29.0 0.0 collective-permute-done.2.sibling_ref
  29.0 1.1 %shard_map.69 = (bf16[280,16,128]{2,1,0:T(8,128)(2,1)S(1)}, bf16[4,2,9,128,128]{4,3,2,1,0:T(8,128)(2,1)S(1)}) custom-call(bf16[65,16,128]{2,1,0:T(8,128)(2,1)S(1)} %get-tuple-element.10.fields_ref, bf16[33,16,128]{2,1,0:T(8,128)(2,1)S(1)} %collective-permute-done.before_ref, bf16[33,16,128]{2,1,0:T(8,128)(2,1)S(1)} %collective-permute-done.1.after_ref, ...), custom_call_target="tpu_custom_call" | custom-call | flops 20000000000 | bytes 1048576 | tf_op jit(solution)/shard_map/pallas_call | solution.py:231
  30.1 0.0 collective-permute-done.4.last_ref
  30.1 6.9 %shard_map.70 = (bf16[2,2,32,128]{3,2,1,0:T(8,128)(2,1)}, bf16[2,2,32,128]{3,2,1,0:T(8,128)(2,1)}, bf16[4,2,9,128,128]{4,3,2,1,0:T(8,128)(2,1)S(1)}) custom-call(bf16[280,16,128]{2,1,0:T(8,128)(2,1)S(1)} %get-tuple-element.14.state_ref, bf16[4,2,9,128,128]{4,3,2,1,0:T(8,128)(2,1)S(1)} %get-tuple-element.15.weight_in, ...), custom_call_target="tpu_custom_call", output_to_operand_aliasing={{2}: (1, {})} | custom-call | tf_op jit(solution)/shard_map/pallas_call | solution.py:243
Async XLA Ops:
  0.6 25.1 %collective-permute-start.3 = (bf16[1,2,9,128,128]{4,3,2,1,0:T(8,128)(2,1)}, bf16[1,2,9,128,128]{4,3,2,1,0:T(8,128)(2,1)S(1)}, u32[]{:S(2)}, u32[]{:S(2)}) collective-permute-start(bf16[1,2,9,128,128]{4,3,2,1,0:T(8,128)(2,1)} %own_ref.1), channel_id=1, source_target_pairs={{0,18},{1,19},{2,16},{3,17},{4,22},{5,23},{6,20},{7,21},{8,26},{9,... | collective-permute-start | bytes 1769480 | tf_op jit(solution)/shard_map/ppermute | solution.py:220
  5.9 23.2 %collective-permute-start.2 = (bf16[1,2,9,128,128]{4,3,2,1,0:T(8,128)(2,1)}, bf16[1,2,9,128,128]{4,3,2,1,0:T(8,128)(2,1)S(1)}, u32[]{:S(2)}, u32[]{:S(2)}) collective-permute-start(bf16[1,2,9,128,128]{4,3,2,1,0:T(8,128)(2,1)} %own_ref.1), channel_id=1, source_target_pairs={{0,1},{1,0},{2,3},{3,2},{4,5},{5,4},{6,7},{7,6},{8,9},{9,8},{10,11... | collective-permute-start | bytes 1769480 | tf_op jit(solution)/shard_map/ppermute | solution.py:222
  13.2 14.8 %collective-permute-start = (bf16[33,16,128]{2,1,0:T(8,128)(2,1)}, bf16[33,16,128]{2,1,0:T(8,128)(2,1)S(1)}, u32[]{:S(2)}, u32[]{:S(2)}) collective-permute-start(bf16[33,16,128]{2,1,0:T(8,128)(2,1)} %get-tuple-element.11), channel_id=1, source_target_pairs={{0,4},{4,8},{8,12},{12,16},{16,20},{20,24},{24,28},{28,32},{32,36}... | collective-permute-start | bytes 405512 | tf_op jit(solution)/shard_map/ppermute | solution.py:223
  15.1 13.9 %collective-permute-start.1 = (bf16[33,16,128]{2,1,0:T(8,128)(2,1)}, bf16[33,16,128]{2,1,0:T(8,128)(2,1)S(1)}, u32[]{:S(2)}, u32[]{:S(2)}) collective-permute-start(bf16[33,16,128]{2,1,0:T(8,128)(2,1)} %get-tuple-element.12), channel_id=1, source_target_pairs={{4,0},{8,4},{12,8},{16,12},{20,16},{24,20},{28,24},{32,28},{36,32}... | collective-permute-start | bytes 405512 | tf_op jit(solution)/shard_map/ppermute | solution.py:224
  25.7 4.4 %collective-permute-start.4 = (bf16[1,2,9,128,128]{4,3,2,1,0:T(8,128)(2,1)S(1)}, bf16[1,2,9,128,128]{4,3,2,1,0:T(8,128)(2,1)S(1)}, u32[]{:S(2)}, u32[]{:S(2)}) collective-permute-start(bf16[1,2,9,128,128]{4,3,2,1,0:T(8,128)(2,1)S(1)} %collective-permute-done.3.far_ref), channel_id=1, source_target_pairs={{0,1},{1,0},{2,3},{3,2},{4,5},{5,4},{6,7},{7,6},{8,9},{9,8},{10,11... | collective-permute-start | bytes 1769480 | tf_op jit(solution)/shard_map/ppermute | solution.py:226

commit v5 on v4

--- a/solution.py
+++ b/solution.py
@@ -16,10 +16,14 @@
 OWN = DEPTH + 2
 RIGHT = OWN + WIDTH + 2
 TOTAL = RIGHT + DEPTH
-PARTS = 4
-
-
-def pack_kernel(atmos_ref, ocean_ref, rotation_ref, mask_ref, fields_ref, up_ref, down_ref, tile):
+PARTS = 6
+
+
+def pack_kernel(
+    atmos_ref, ocean_ref, rotation_ref, mask_ref, own_ref, fields_ref, up_ref, down_ref, own_out, tile, semaphore
+):
+    copy = pltpu.make_async_copy(own_ref.at[0], own_out, semaphore)
+    copy.start()
     for index, ref in enumerate((atmos_ref, ocean_ref)):
         value = ref[...].astype(F32).reshape(16, WIDTH, 128)
         value = jnp.swapaxes(value, 0, 1).astype(BF)
@@ -37,6 +41,7 @@
     fields_ref[2 * WIDTH] = packed
     up_ref[2 * DEPTH] = packed
     down_ref[2 * DEPTH] = packed
+    copy.wait()
 
 
 def shift_rows(value, by):
@@ -94,17 +99,11 @@
     return keep.astype(BF), swap.astype(BF)
 
 
-def state_kernel(fields_ref, before_ref, after_ref, own_ref, sibling_ref, far_ref, state_ref, weight_ref, semaphores):
+def state_kernel(fields_ref, before_ref, after_ref, own_ref, sibling_ref, far_ref, state_ref, weight_ref):
     comp = lax.axis_index("comp")
-    core = lax.rem(comp, 2)
-    copies = [
-        pltpu.make_async_copy(ref.at[0], weight_ref.at[place], semaphores.at[index])
-        for index, (ref, place) in enumerate(
-            ((own_ref, comp), (sibling_ref, comp + 1 - 2 * core), (far_ref, lax.rem(comp + 2, 4)))
-        )
-    ]
-    for copy in copies:
-        copy.start()
+    weight_ref[comp] = own_ref[...]
+    weight_ref[comp + 1 - 2 * lax.rem(comp, 2)] = sibling_ref[0]
+    weight_ref[lax.rem(comp + 2, 4)] = far_ref[0]
 
     def broadcast(tile, column):
         return jnp.broadcast_to(tile[:, column : column + 1], (16, 128))
@@ -135,20 +134,16 @@
         atmos_value = ref[pl.ds(origin, count)].astype(F32)
         store((hidden, hidden_down), span, atmos_value + sea[span].astype(F32) * ocean_value.astype(F32))
     close_seams((hidden, hidden_down), factors)
-    for copy in copies:
-        copy.wait()
 
 
 def main_kernel(
     state_ref, weight_in, last_ref, atmos_out, ocean_out, weight_ref,
-    hidden_ref, hidden_down, inner, inner_down, flux, flux_down, ocean_ref, final, semaphore,
+    hidden_ref, hidden_down, inner, inner_down, flux, flux_down, ocean_ref, final,
 ):
     comp = lax.axis_index("comp")
-    copy = pltpu.make_async_copy(last_ref.at[0], weight_ref.at[3 - comp], semaphore)
-    copy.start()
+    weight_ref[3 - comp] = last_ref[0]
     hidden, first_down, ocean, sea, factors = parts_of(state_ref)
     field = (hidden, first_down)
-    copy.wait()
 
     def load(ref, span):
         return ref[span].astype(F32)
@@ -201,17 +196,18 @@
 def per_device(atmos_state, ocean_state, conv_weight, rotation, sea_mask):
     tiles = lax.axis_size("pix")
     vmem = pl.BlockSpec(memory_space=pltpu.VMEM)
-    fields, up, down = pl.pallas_call(
+    fields, up, down, own = pl.pallas_call(
         pack_kernel,
         out_shape=(
             pltpu.VMEM((2 * WIDTH + 1, 16, 128), BF),
             jax.ShapeDtypeStruct((2 * DEPTH + 1, 16, 128), BF),
             jax.ShapeDtypeStruct((2 * DEPTH + 1, 16, 128), BF),
+            pltpu.VMEM(conv_weight.shape[1:], BF),
         ),
-        in_specs=[vmem, vmem, pl.BlockSpec(memory_space=pltpu.SMEM), vmem],
-        out_specs=(vmem, vmem, vmem),
-        scratch_shapes=[pltpu.VMEM((16, 128), F32)],
-    )(atmos_state, ocean_state, rotation, sea_mask)
+        in_specs=[vmem, vmem, pl.BlockSpec(memory_space=pltpu.SMEM), vmem, pl.BlockSpec(memory_space=pltpu.HBM)],
+        out_specs=(vmem, vmem, vmem, vmem),
+        scratch_shapes=[pltpu.VMEM((16, 128), F32), pltpu.SemaphoreType.DMA(())],
+    )(atmos_state, ocean_state, rotation, sea_mask, pltpu.with_memory_space_constraint(conv_weight, pltpu.HBM))
 
     names = ("pix", "comp")
     flip = 4 if tiles % 8 == 0 else 0
@@ -225,28 +221,26 @@
     far, _ = lax.optimization_barrier((far, (up, down)))
     far_sibling = lax.ppermute(far, names, swap)
 
-    anywhere = pl.BlockSpec(memory_space=pl.ANY)
     section_weights = pltpu.VMEM((4,) + conv_weight.shape[1:], BF)
     params = pltpu.CompilerParams(vmem_limit_bytes=40 << 20)
     state, weight = pl.pallas_call(
         state_kernel,
         out_shape=(pltpu.VMEM((4 * TOTAL + 2 * len(SEAMS), 16, 128), BF), section_weights),
-        in_specs=[vmem, vmem, vmem, pl.BlockSpec(memory_space=pltpu.HBM), anywhere, anywhere],
+        in_specs=[vmem] * 6,
         out_specs=(vmem, vmem),
-        scratch_shapes=[pltpu.SemaphoreType.DMA((3,))],
         cost_estimate=pl.CostEstimate(flops=2 * 10**10, bytes_accessed=1 << 20, transcendentals=0),
         compiler_params=params,
-    )(fields, before, after, pltpu.with_memory_space_constraint(conv_weight, pltpu.HBM), sibling, far)
+    )(fields, before, after, own, sibling, far)
 
     band = jax.ShapeDtypeStruct((2, 2, WIDTH, 128), BF)
     field = pltpu.VMEM((TOTAL, 16, 128), BF)
     return pl.pallas_call(
         main_kernel,
         out_shape=(band, band, section_weights),
-        in_specs=[vmem, vmem, anywhere],
+        in_specs=[vmem, vmem, vmem],
         out_specs=(vmem, vmem, vmem),
         input_output_aliases={1: 2},
-        scratch_shapes=[field] * 7 + [pltpu.VMEM((16, WIDTH, 128), F32), pltpu.SemaphoreType.DMA(())],
+        scratch_shapes=[field] * 7 + [pltpu.VMEM((16, WIDTH, 128), F32)],
         compiler_params=params,
     )(state, weight, far_sibling)[:2]
 

time: 37.3 us -> 37.4 us (level)
    pallas_call x1, Pallas kernels: 1.83 us -> 2.75 us  [per_device(): pl.pallas_call(pack_kernel, out_shape=(pltpu.VMEM((2 * WIDTH + 1, 16, 128...]
    pallas_call x1, Pallas kernels: 1.09 us -> 0.42 us  [per_device(): pl.pallas_call(state_kernel, out_shape=(pltpu.VMEM((4 * TOTAL + 2 * len(S...]
  transfers between devices with their start and end apart: 5 -> 5, of which waited for: 1 -> 2; matrix products, arithmetic and copies ran while one was open for 0% -> 0% of each run, Pallas kernels for 8% -> 9%
where the time goes in v5:
time: 37.4 us; the launch traced here: 37.1 us
  starting transfers between devices  25.4 us (68%)
  Pallas kernels  9.73 us (26%)
  waiting for transfers between devices  1.26 us (3%)
  between operations  0.7 us (2%)
    ppermute x1, starting transfers between devices, per_device(): after = lax.ppermute(down, 'pix', [(j, i) for i, j in rightward])  10.6 us
    pallas_call x1, Pallas kernels, per_device(): pl.pallas_call(main_kernel, out_shape=(band, band, section_weights), in_s...  6.56 us
    ppermute x1, starting transfers between devices, per_device(): sibling = lax.ppermute(conv_weight, names, swap)  5.49 us
    ppermute x1, starting transfers between devices, per_device(): far = lax.ppermute(conv_weight, names, across)  5.22 us
    pallas_call x1, Pallas kernels, per_device(): pl.pallas_call(pack_kernel, out_shape=(pltpu.VMEM((2 * WIDTH + 1, 16, 128...  2.75 us
    ppermute x1, starting transfers between devices, per_device(): far_sibling = lax.ppermute(far, names, swap)  2.2 us
    ppermute x1, starting transfers between devices, per_device(): before = lax.ppermute(up, 'pix', rightward)  1.92 us
    ppermute x1, waiting for transfers between devices, per_device(): after = lax.ppermute(down, 'pix', [(j, i) for i, j in rightward])  1.07 us
  transfers between devices with their start and end apart: 5, of which 2 were waited for; matrix products, arithmetic and copies ran while one was open for 0% of the time, Pallas kernels for 9%

profile of v5, /device:TPU:1, one launch (start us, length us, event | category | flops | bytes accessed | tf_op | source)
XLA Modules:
  0.0 37.1 jit_solution(12501363636454529623)
XLA Ops:
  0.6 5.2 %collective-permute-start.3 = (bf16[1,2,9,128,128]{4,3,2,1,0:T(8,128)(2,1)}, bf16[1,2,9,128,128]{4,3,2,1,0:T(8,128)(2,1)S(1)}, u32[]{:S(2)}, u32[]{:S(2)}) collective-permute-start(bf16[1,2,9,128,128]{4,3,2,1,0:T(8,128)(2,1)} %own_ref.1), channel_id=1, source_target_pairs={{0,18},{1,19},{2,16},{3,17},{4,22},{5,23},{6,20},{7,21},{8,26},{9,... | collective-permute-start | bytes 1769480 | tf_op jit(solution)/shard_map/ppermute | solution.py:216
  5.9 5.5 %collective-permute-start.2 = (bf16[1,2,9,128,128]{4,3,2,1,0:T(8,128)(2,1)}, bf16[1,2,9,128,128]{4,3,2,1,0:T(8,128)(2,1)S(1)}, u32[]{:S(2)}, u32[]{:S(2)}) collective-permute-start(bf16[1,2,9,128,128]{4,3,2,1,0:T(8,128)(2,1)} %own_ref.1), channel_id=1, source_target_pairs={{0,1},{1,0},{2,3},{3,2},{4,5},{5,4},{6,7},{7,6},{8,9},{9,8},{10,11... | collective-permute-start | bytes 1769480 | tf_op jit(solution)/shard_map/ppermute | solution.py:218
  11.4 2.8 %shard_map.68 = (bf16[65,16,128]{2,1,0:T(8,128)(2,1)S(1)}, bf16[33,16,128]{2,1,0:T(8,128)(2,1)}, bf16[33,16,128]{2,1,0:T(8,128)(2,1)}, bf16[2,9,128,128]{3,2,1,0:T(8,128)(2,1)S(1)}) custom-call(bf16[2,8,32,128]{3,2,1,0:T(8,128)(2,1)} %atmos_ref.1, bf16[2,8,32,128]{3,2,1,0:T(8,128)(2,1)} %ocean_ref.1, s32[1,2]{1,0:T(1,128)} %rotation_ref.1, ...), custom_call_target="tpu_custom_call" | custom-call | tf_op jit(solution)/shard_map/pallas_call | solution.py:199
  14.1 1.9 %collective-permute-start = (bf16[33,16,128]{2,1,0:T(8,128)(2,1)}, bf16[33,16,128]{2,1,0:T(8,128)(2,1)S(1)}, u32[]{:S(2)}, u32[]{:S(2)}) collective-permute-start(bf16[33,16,128]{2,1,0:T(8,128)(2,1)} %get-tuple-element.12), channel_id=1, source_target_pairs={{0,4},{4,8},{8,12},{12,16},{16,20},{20,24},{24,28},{28,32},{32,36}... | collective-permute-start | bytes 405512 | tf_op jit(solution)/shard_map/ppermute | solution.py:219
  16.0 10.6 %collective-permute-start.1 = (bf16[33,16,128]{2,1,0:T(8,128)(2,1)}, bf16[33,16,128]{2,1,0:T(8,128)(2,1)S(1)}, u32[]{:S(2)}, u32[]{:S(2)}) collective-permute-start(bf16[33,16,128]{2,1,0:T(8,128)(2,1)} %get-tuple-element.13), channel_id=1, source_target_pairs={{4,0},{8,4},{12,8},{16,12},{20,16},{24,20},{28,24},{32,28},{36,32}... | collective-permute-start | bytes 405512 | tf_op jit(solution)/shard_map/ppermute | solution.py:220
  26.7 0.0 collective-permute-done.3.far_ref
  26.7 2.2 %collective-permute-start.4 = (bf16[1,2,9,128,128]{4,3,2,1,0:T(8,128)(2,1)S(1)}, bf16[1,2,9,128,128]{4,3,2,1,0:T(8,128)(2,1)S(1)}, u32[]{:S(2)}, u32[]{:S(2)}) collective-permute-start(bf16[1,2,9,128,128]{4,3,2,1,0:T(8,128)(2,1)S(1)} %collective-permute-done.3.far_ref), channel_id=1, source_target_pairs={{0,1},{1,0},{2,3},{3,2},{4,5},{5,4},{6,7},{7,6},{8,9},{9,8},{10,11... | collective-permute-start | bytes 1769480 | tf_op jit(solution)/shard_map/ppermute | solution.py:222
  28.9 0.0 collective-permute-done.before_ref
  28.9 1.1 %collective-permute-done.1.after_ref = bf16[33,16,128]{2,1,0:T(8,128)(2,1)S(1)} collective-permute-done((bf16[33,16,128]{2,1,0:T(8,128)(2,1)}, bf16[33,16,128]{2,1,0:T(8,128)(2,1)S(1)}, u32[]{:S(2)}, u32[]{:S(2)}) %collective-permute-start.1) | collective-permute-done | bytes 135200 | tf_op jit(solution)/shard_map/ppermute | solution.py:220
  30.0 0.0 collective-permute-done.2.sibling_ref
  30.0 0.4 %shard_map.69 = (bf16[280,16,128]{2,1,0:T(8,128)(2,1)S(1)}, bf16[4,2,9,128,128]{4,3,2,1,0:T(8,128)(2,1)S(1)}) custom-call(bf16[65,16,128]{2,1,0:T(8,128)(2,1)S(1)} %get-tuple-element.11.fields_ref, bf16[33,16,128]{2,1,0:T(8,128)(2,1)S(1)} %collective-permute-done.before_ref, bf16[33,16,128]{2,1,0:T(8,128)(2,1)S(1)} %collective-permute-done.1.after_ref, ...), custom_call_target="tpu_custom_call" | custom-call | flops 20000000000 | bytes 1048576 | tf_op jit(solution)/shard_map/pallas_call | solution.py:226
  30.4 0.2 collective-permute-done.4.last_ref
  30.6 6.6 %shard_map.70 = (bf16[2,2,32,128]{3,2,1,0:T(8,128)(2,1)}, bf16[2,2,32,128]{3,2,1,0:T(8,128)(2,1)}, bf16[4,2,9,128,128]{4,3,2,1,0:T(8,128)(2,1)S(1)}) custom-call(bf16[280,16,128]{2,1,0:T(8,128)(2,1)S(1)} %get-tuple-element.16.state_ref, bf16[4,2,9,128,128]{4,3,2,1,0:T(8,128)(2,1)S(1)} %get-tuple-element.17.weight_in, ...), custom_call_target="tpu_custom_call", output_to_operand_aliasing={{2}: (1, {})} | custom-call | tf_op jit(solution)/shard_map/pallas_call | solution.py:237
Async XLA Ops:
  0.6 26.0 %collective-permute-start.3 = (bf16[1,2,9,128,128]{4,3,2,1,0:T(8,128)(2,1)}, bf16[1,2,9,128,128]{4,3,2,1,0:T(8,128)(2,1)S(1)}, u32[]{:S(2)}, u32[]{:S(2)}) collective-permute-start(bf16[1,2,9,128,128]{4,3,2,1,0:T(8,128)(2,1)} %own_ref.1), channel_id=1, source_target_pairs={{0,18},{1,19},{2,16},{3,17},{4,22},{5,23},{6,20},{7,21},{8,26},{9,... | collective-permute-start | bytes 1769480 | tf_op jit(solution)/shard_map/ppermute | solution.py:216
  5.9 24.1 %collective-permute-start.2 = (bf16[1,2,9,128,128]{4,3,2,1,0:T(8,128)(2,1)}, bf16[1,2,9,128,128]{4,3,2,1,0:T(8,128)(2,1)S(1)}, u32[]{:S(2)}, u32[]{:S(2)}) collective-permute-start(bf16[1,2,9,128,128]{4,3,2,1,0:T(8,128)(2,1)} %own_ref.1), channel_id=1, source_target_pairs={{0,1},{1,0},{2,3},{3,2},{4,5},{5,4},{6,7},{7,6},{8,9},{9,8},{10,11... | collective-permute-start | bytes 1769480 | tf_op jit(solution)/shard_map/ppermute | solution.py:218
  14.1 14.8 %collective-permute-start = (bf16[33,16,128]{2,1,0:T(8,128)(2,1)}, bf16[33,16,128]{2,1,0:T(8,128)(2,1)S(1)}, u32[]{:S(2)}, u32[]{:S(2)}) collective-permute-start(bf16[33,16,128]{2,1,0:T(8,128)(2,1)} %get-tuple-element.12), channel_id=1, source_target_pairs={{0,4},{4,8},{8,12},{12,16},{16,20},{20,24},{24,28},{28,32},{32,36}... | collective-permute-start | bytes 405512 | tf_op jit(solution)/shard_map/ppermute | solution.py:219
  16.0 13.9 %collective-permute-start.1 = (bf16[33,16,128]{2,1,0:T(8,128)(2,1)}, bf16[33,16,128]{2,1,0:T(8,128)(2,1)S(1)}, u32[]{:S(2)}, u32[]{:S(2)}) collective-permute-start(bf16[33,16,128]{2,1,0:T(8,128)(2,1)} %get-tuple-element.13), channel_id=1, source_target_pairs={{4,0},{8,4},{12,8},{16,12},{20,16},{24,20},{28,24},{32,28},{36,32}... | collective-permute-start | bytes 405512 | tf_op jit(solution)/shard_map/ppermute | solution.py:220
  26.7 3.9 %collective-permute-start.4 = (bf16[1,2,9,128,128]{4,3,2,1,0:T(8,128)(2,1)S(1)}, bf16[1,2,9,128,128]{4,3,2,1,0:T(8,128)(2,1)S(1)}, u32[]{:S(2)}, u32[]{:S(2)}) collective-permute-start(bf16[1,2,9,128,128]{4,3,2,1,0:T(8,128)(2,1)S(1)} %collective-permute-done.3.far_ref), channel_id=1, source_target_pairs={{0,1},{1,0},{2,3},{3,2},{4,5},{5,4},{6,7},{7,6},{8,9},{9,8},{10,11... | collective-permute-start | bytes 1769480 | tf_op jit(solution)/shard_map/ppermute | solution.py:222

commit v6 on v4

--- a/solution.py
+++ b/solution.py
@@ -16,7 +16,7 @@
 OWN = DEPTH + 2
 RIGHT = OWN + WIDTH + 2
 TOTAL = RIGHT + DEPTH
-PARTS = 4
+PARTS = 6
 
 
 def pack_kernel(atmos_ref, ocean_ref, rotation_ref, mask_ref, fields_ref, up_ref, down_ref, tile):
@@ -94,17 +94,10 @@
     return keep.astype(BF), swap.astype(BF)
 
 
-def state_kernel(fields_ref, before_ref, after_ref, own_ref, sibling_ref, far_ref, state_ref, weight_ref, semaphores):
+def state_kernel(fields_ref, before_ref, after_ref, sibling_ref, far_ref, state_ref, weight_ref):
     comp = lax.axis_index("comp")
-    core = lax.rem(comp, 2)
-    copies = [
-        pltpu.make_async_copy(ref.at[0], weight_ref.at[place], semaphores.at[index])
-        for index, (ref, place) in enumerate(
-            ((own_ref, comp), (sibling_ref, comp + 1 - 2 * core), (far_ref, lax.rem(comp + 2, 4)))
-        )
-    ]
-    for copy in copies:
-        copy.start()
+    weight_ref[comp + 1 - 2 * lax.rem(comp, 2)] = sibling_ref[0]
+    weight_ref[lax.rem(comp + 2, 4)] = far_ref[0]
 
     def broadcast(tile, column):
         return jnp.broadcast_to(tile[:, column : column + 1], (16, 128))
@@ -135,20 +128,18 @@
         atmos_value = ref[pl.ds(origin, count)].astype(F32)
         store((hidden, hidden_down), span, atmos_value + sea[span].astype(F32) * ocean_value.astype(F32))
     close_seams((hidden, hidden_down), factors)
-    for copy in copies:
-        copy.wait()
 
 
 def main_kernel(
-    state_ref, weight_in, last_ref, atmos_out, ocean_out, weight_ref,
+    state_ref, weight_in, last_ref, own_ref, atmos_out, ocean_out, weight_ref,
     hidden_ref, hidden_down, inner, inner_down, flux, flux_down, ocean_ref, final, semaphore,
 ):
     comp = lax.axis_index("comp")
-    copy = pltpu.make_async_copy(last_ref.at[0], weight_ref.at[3 - comp], semaphore)
+    copy = pltpu.make_async_copy(own_ref.at[0], weight_ref.at[comp], semaphore)
     copy.start()
+    weight_ref[3 - comp] = last_ref[0]
     hidden, first_down, ocean, sea, factors = parts_of(state_ref)
     field = (hidden, first_down)
-    copy.wait()
 
     def load(ref, span):
         return ref[span].astype(F32)
@@ -173,6 +164,8 @@
                     span = pl.ds(start, stop - start)
                     store(source, span, load(hidden, span) + load(ocean, span))
                 close_seams(source, factors)
+            if step == 0 and section < 2:
+                pl.when(comp == 0 if section == 0 else comp != 0)(copy.wait)
             done += 1
             for start, stop in pieces(done):
                 value = convolve_columns(source, weight_ref.at[section, 0], start, stop)
@@ -225,30 +218,28 @@
     far, _ = lax.optimization_barrier((far, (up, down)))
     far_sibling = lax.ppermute(far, names, swap)
 
-    anywhere = pl.BlockSpec(memory_space=pl.ANY)
     section_weights = pltpu.VMEM((4,) + conv_weight.shape[1:], BF)
     params = pltpu.CompilerParams(vmem_limit_bytes=40 << 20)
     state, weight = pl.pallas_call(
         state_kernel,
         out_shape=(pltpu.VMEM((4 * TOTAL + 2 * len(SEAMS), 16, 128), BF), section_weights),
-        in_specs=[vmem, vmem, vmem, pl.BlockSpec(memory_space=pltpu.HBM), anywhere, anywhere],
+        in_specs=[vmem] * 5,
         out_specs=(vmem, vmem),
-        scratch_shapes=[pltpu.SemaphoreType.DMA((3,))],
         cost_estimate=pl.CostEstimate(flops=2 * 10**10, bytes_accessed=1 << 20, transcendentals=0),
         compiler_params=params,
-    )(fields, before, after, pltpu.with_memory_space_constraint(conv_weight, pltpu.HBM), sibling, far)
+    )(fields, before, after, sibling, far)
 
     band = jax.ShapeDtypeStruct((2, 2, WIDTH, 128), BF)
     field = pltpu.VMEM((TOTAL, 16, 128), BF)
     return pl.pallas_call(
         main_kernel,
         out_shape=(band, band, section_weights),
-        in_specs=[vmem, vmem, anywhere],
+        in_specs=[vmem, vmem, vmem, pl.BlockSpec(memory_space=pltpu.HBM)],
         out_specs=(vmem, vmem, vmem),
         input_output_aliases={1: 2},
         scratch_shapes=[field] * 7 + [pltpu.VMEM((16, WIDTH, 128), F32), pltpu.SemaphoreType.DMA(())],
         compiler_params=params,
-    )(state, weight, far_sibling)[:2]
+    )(state, weight, far_sibling, pltpu.with_memory_space_constraint(conv_weight, pltpu.HBM))[:2]
 
 
 def solution(mesh):

time: 37.3 us -> 36.8 us (0.987)
  Pallas kernels: 9.79 us -> 9.06 us
    pallas_call x1, Pallas kernels: 1.09 us -> 0.39 us  [per_device(): pl.pallas_call(state_kernel, out_shape=(pltpu.VMEM((4 * TOTAL + 2 * len(S...]
  transfers between devices with their start and end apart: 5 -> 5, of which waited for: 1 -> 2; matrix products, arithmetic and copies ran while one was open for 0% -> 0% of each run, Pallas kernels for 8% -> 6%
where the time goes in v6:
time: 36.8 us; the launch traced here: 36.5 us
  starting transfers between devices  25.4 us (69%)
  Pallas kernels  9.06 us (25%)
  waiting for transfers between devices  1.28 us (3%)
  between operations  0.7 us (2%)
    ppermute x1, starting transfers between devices, per_device(): after = lax.ppermute(down, 'pix', [(j, i) for i, j in rightward])  10.6 us
    pallas_call x1, Pallas kernels, per_device(): pl.pallas_call(main_kernel, out_shape=(band, band, section_weights), in_s...  6.83 us
    ppermute x1, starting transfers between devices, per_device(): sibling = lax.ppermute(conv_weight, names, swap)  5.49 us
    ppermute x1, starting transfers between devices, per_device(): far = lax.ppermute(conv_weight, names, across)  5.22 us
    ppermute x1, starting transfers between devices, per_device(): far_sibling = lax.ppermute(far, names, swap)  2.2 us
    ppermute x1, starting transfers between devices, per_device(): before = lax.ppermute(up, 'pix', rightward)  1.91 us
    pallas_call x1, Pallas kernels, per_device(): pl.pallas_call(pack_kernel, out_shape=(pltpu.VMEM((2 * WIDTH + 1, 16, 128...  1.83 us
    ppermute x1, waiting for transfers between devices, per_device(): after = lax.ppermute(down, 'pix', [(j, i) for i, j in rightward])  1.07 us
  transfers between devices with their start and end apart: 5, of which 2 were waited for; matrix products, arithmetic and copies ran while one was open for 0% of the time, Pallas kernels for 6%

profile of v6, /device:TPU:1, one launch (start us, length us, event | category | flops | bytes accessed | tf_op | source)
XLA Modules:
  0.0 36.5 jit_solution(13350806024604156596)
XLA Ops:
  0.6 5.2 %collective-permute-start.3 = (bf16[1,2,9,128,128]{4,3,2,1,0:T(8,128)(2,1)}, bf16[1,2,9,128,128]{4,3,2,1,0:T(8,128)(2,1)S(1)}, u32[]{:S(2)}, u32[]{:S(2)}) collective-permute-start(bf16[1,2,9,128,128]{4,3,2,1,0:T(8,128)(2,1)} %own_ref.1), channel_id=1, source_target_pairs={{0,18},{1,19},{2,16},{3,17},{4,22},{5,23},{6,20},{7,21},{8,26},{9,... | collective-permute-start | bytes 1769480 | tf_op jit(solution)/shard_map/ppermute | solution.py:213
  5.9 5.5 %collective-permute-start.2 = (bf16[1,2,9,128,128]{4,3,2,1,0:T(8,128)(2,1)}, bf16[1,2,9,128,128]{4,3,2,1,0:T(8,128)(2,1)S(1)}, u32[]{:S(2)}, u32[]{:S(2)}) collective-permute-start(bf16[1,2,9,128,128]{4,3,2,1,0:T(8,128)(2,1)} %own_ref.1), channel_id=1, source_target_pairs={{0,1},{1,0},{2,3},{3,2},{4,5},{5,4},{6,7},{7,6},{8,9},{9,8},{10,11... | collective-permute-start | bytes 1769480 | tf_op jit(solution)/shard_map/ppermute | solution.py:215
  11.4 1.8 %shard_map.68 = (bf16[65,16,128]{2,1,0:T(8,128)(2,1)S(1)}, bf16[33,16,128]{2,1,0:T(8,128)(2,1)}, bf16[33,16,128]{2,1,0:T(8,128)(2,1)}) custom-call(bf16[2,8,32,128]{3,2,1,0:T(8,128)(2,1)} %atmos_ref.1, bf16[2,8,32,128]{3,2,1,0:T(8,128)(2,1)} %ocean_ref.1, s32[1,2]{1,0:T(1,128)} %rotation_ref.1, s32[8,32]{1,0:T(8,128)} %mask_ref.1), custom_call_target="tpu_custom_call" | custom-call | tf_op jit(solution)/shard_map/pallas_call | solution.py:197
  13.2 1.9 %collective-permute-start = (bf16[33,16,128]{2,1,0:T(8,128)(2,1)}, bf16[33,16,128]{2,1,0:T(8,128)(2,1)S(1)}, u32[]{:S(2)}, u32[]{:S(2)}) collective-permute-start(bf16[33,16,128]{2,1,0:T(8,128)(2,1)} %get-tuple-element.11), channel_id=1, source_target_pairs={{0,4},{4,8},{8,12},{12,16},{16,20},{20,24},{24,28},{28,32},{32,36}... | collective-permute-start | bytes 405512 | tf_op jit(solution)/shard_map/ppermute | solution.py:216
  15.1 10.6 %collective-permute-start.1 = (bf16[33,16,128]{2,1,0:T(8,128)(2,1)}, bf16[33,16,128]{2,1,0:T(8,128)(2,1)S(1)}, u32[]{:S(2)}, u32[]{:S(2)}) collective-permute-start(bf16[33,16,128]{2,1,0:T(8,128)(2,1)} %get-tuple-element.12), channel_id=1, source_target_pairs={{4,0},{8,4},{12,8},{16,12},{20,16},{24,20},{28,24},{32,28},{36,32}... | collective-permute-start | bytes 405512 | tf_op jit(solution)/shard_map/ppermute | solution.py:217
  25.7 0.0 collective-permute-done.3.far_ref
  25.7 2.2 %collective-permute-start.4 = (bf16[1,2,9,128,128]{4,3,2,1,0:T(8,128)(2,1)S(1)}, bf16[1,2,9,128,128]{4,3,2,1,0:T(8,128)(2,1)S(1)}, u32[]{:S(2)}, u32[]{:S(2)}) collective-permute-start(bf16[1,2,9,128,128]{4,3,2,1,0:T(8,128)(2,1)S(1)} %collective-permute-done.3.far_ref), channel_id=1, source_target_pairs={{0,1},{1,0},{2,3},{3,2},{4,5},{5,4},{6,7},{7,6},{8,9},{9,8},{10,11... | collective-permute-start | bytes 1769480 | tf_op jit(solution)/shard_map/ppermute | solution.py:219
  27.9 0.0 collective-permute-done.before_ref
  27.9 1.1 %collective-permute-done.1.after_ref = bf16[33,16,128]{2,1,0:T(8,128)(2,1)S(1)} collective-permute-done((bf16[33,16,128]{2,1,0:T(8,128)(2,1)}, bf16[33,16,128]{2,1,0:T(8,128)(2,1)S(1)}, u32[]{:S(2)}, u32[]{:S(2)}) %collective-permute-start.1) | collective-permute-done | bytes 135200 | tf_op jit(solution)/shard_map/ppermute | solution.py:217
  29.0 0.0 collective-permute-done.2.sibling_ref
  29.0 0.4 %shard_map.69 = (bf16[280,16,128]{2,1,0:T(8,128)(2,1)S(1)}, bf16[4,2,9,128,128]{4,3,2,1,0:T(8,128)(2,1)S(1)}) custom-call(bf16[65,16,128]{2,1,0:T(8,128)(2,1)S(1)} %get-tuple-element.10.fields_ref, bf16[33,16,128]{2,1,0:T(8,128)(2,1)S(1)} %collective-permute-done.before_ref, bf16[33,16,128]{2,1,0:T(8,128)(2,1)S(1)} %collective-permute-done.1.after_ref, ...), custom_call_target="tpu_custom_call" | custom-call | flops 20000000000 | bytes 1048576 | tf_op jit(solution)/shard_map/pallas_call | solution.py:223
  29.4 0.2 collective-permute-done.4.last_ref
  29.6 6.8 %shard_map.70 = (bf16[2,2,32,128]{3,2,1,0:T(8,128)(2,1)}, bf16[2,2,32,128]{3,2,1,0:T(8,128)(2,1)}, bf16[4,2,9,128,128]{4,3,2,1,0:T(8,128)(2,1)S(1)}) custom-call(bf16[280,16,128]{2,1,0:T(8,128)(2,1)S(1)} %get-tuple-element.14.state_ref, bf16[4,2,9,128,128]{4,3,2,1,0:T(8,128)(2,1)S(1)} %get-tuple-element.15.weight_in, ...), custom_call_target="tpu_custom_call", output_to_operand_aliasing={{2}: (1, {})} | custom-call | tf_op jit(solution)/shard_map/pallas_call | solution.py:234
Async XLA Ops:
  0.6 25.1 %collective-permute-start.3 = (bf16[1,2,9,128,128]{4,3,2,1,0:T(8,128)(2,1)}, bf16[1,2,9,128,128]{4,3,2,1,0:T(8,128)(2,1)S(1)}, u32[]{:S(2)}, u32[]{:S(2)}) collective-permute-start(bf16[1,2,9,128,128]{4,3,2,1,0:T(8,128)(2,1)} %own_ref.1), channel_id=1, source_target_pairs={{0,18},{1,19},{2,16},{3,17},{4,22},{5,23},{6,20},{7,21},{8,26},{9,... | collective-permute-start | bytes 1769480 | tf_op jit(solution)/shard_map/ppermute | solution.py:213
  5.9 23.2 %collective-permute-start.2 = (bf16[1,2,9,128,128]{4,3,2,1,0:T(8,128)(2,1)}, bf16[1,2,9,128,128]{4,3,2,1,0:T(8,128)(2,1)S(1)}, u32[]{:S(2)}, u32[]{:S(2)}) collective-permute-start(bf16[1,2,9,128,128]{4,3,2,1,0:T(8,128)(2,1)} %own_ref.1), channel_id=1, source_target_pairs={{0,1},{1,0},{2,3},{3,2},{4,5},{5,4},{6,7},{7,6},{8,9},{9,8},{10,11... | collective-permute-start | bytes 1769480 | tf_op jit(solution)/shard_map/ppermute | solution.py:215
  13.2 14.8 %collective-permute-start = (bf16[33,16,128]{2,1,0:T(8,128)(2,1)}, bf16[33,16,128]{2,1,0:T(8,128)(2,1)S(1)}, u32[]{:S(2)}, u32[]{:S(2)}) collective-permute-start(bf16[33,16,128]{2,1,0:T(8,128)(2,1)} %get-tuple-element.11), channel_id=1, source_target_pairs={{0,4},{4,8},{8,12},{12,16},{16,20},{20,24},{24,28},{28,32},{32,36}... | collective-permute-start | bytes 405512 | tf_op jit(solution)/shard_map/ppermute | solution.py:216
  15.1 13.9 %collective-permute-start.1 = (bf16[33,16,128]{2,1,0:T(8,128)(2,1)}, bf16[33,16,128]{2,1,0:T(8,128)(2,1)S(1)}, u32[]{:S(2)}, u32[]{:S(2)}) collective-permute-start(bf16[33,16,128]{2,1,0:T(8,128)(2,1)} %get-tuple-element.12), channel_id=1, source_target_pairs={{4,0},{8,4},{12,8},{16,12},{20,16},{24,20},{28,24},{32,28},{36,32}... | collective-permute-start | bytes 405512 | tf_op jit(solution)/shard_map/ppermute | solution.py:217
  25.7 3.9 %collective-permute-start.4 = (bf16[1,2,9,128,128]{4,3,2,1,0:T(8,128)(2,1)S(1)}, bf16[1,2,9,128,128]{4,3,2,1,0:T(8,128)(2,1)S(1)}, u32[]{:S(2)}, u32[]{:S(2)}) collective-permute-start(bf16[1,2,9,128,128]{4,3,2,1,0:T(8,128)(2,1)S(1)} %collective-permute-done.3.far_ref), channel_id=1, source_target_pairs={{0,1},{1,0},{2,3},{3,2},{4,5},{5,4},{6,7},{7,6},{8,9},{9,8},{10,11... | collective-permute-start | bytes 1769480 | tf_op jit(solution)/shard_map/ppermute | solution.py:219

commit v7 on v6

--- a/solution.py
+++ b/solution.py
@@ -16,7 +16,7 @@
 OWN = DEPTH + 2
 RIGHT = OWN + WIDTH + 2
 TOTAL = RIGHT + DEPTH
-PARTS = 6
+PARTS = 8
 
 
 def pack_kernel(atmos_ref, ocean_ref, rotation_ref, mask_ref, fields_ref, up_ref, down_ref, tile):

time: 36.8 us -> 38.7 us (1.052)
  Pallas kernels: 9.06 us -> 11 us
    pallas_call x1, Pallas kernels: 6.83 us -> 8.77 us  [per_device(): pl.pallas_call(main_kernel, out_shape=(band, band, section_weights), in_s...]
where the time goes in v7:
time: 38.7 us; the launch traced here: 38.4 us
  starting transfers between devices  25.4 us (66%)
  Pallas kernels  11 us (28%)
  waiting for transfers between devices  1.28 us (3%)
  between operations  0.7 us (2%)
    ppermute x1, starting transfers between devices, per_device(): after = lax.ppermute(down, 'pix', [(j, i) for i, j in rightward])  10.6 us
    pallas_call x1, Pallas kernels, per_device(): pl.pallas_call(main_kernel, out_shape=(band, band, section_weights), in_s...  8.77 us
    ppermute x1, starting transfers between devices, per_device(): sibling = lax.ppermute(conv_weight, names, swap)  5.49 us
    ppermute x1, starting transfers between devices, per_device(): far = lax.ppermute(conv_weight, names, across)  5.22 us
    ppermute x1, starting transfers between devices, per_device(): far_sibling = lax.ppermute(far, names, swap)  2.2 us
    ppermute x1, starting transfers between devices, per_device(): before = lax.ppermute(up, 'pix', rightward)  1.91 us
    pallas_call x1, Pallas kernels, per_device(): pl.pallas_call(pack_kernel, out_shape=(pltpu.VMEM((2 * WIDTH + 1, 16, 128...  1.83 us
    ppermute x1, waiting for transfers between devices, per_device(): after = lax.ppermute(down, 'pix', [(j, i) for i, j in rightward])  1.07 us
  transfers between devices with their start and end apart: 5, of which 2 were waited for; matrix products, arithmetic and copies ran while one was open for 0% of the time, Pallas kernels for 6%

profile of v7, /device:TPU:1, one launch (start us, length us, event | category | flops | bytes accessed | tf_op | source)
XLA Modules:
  0.0 38.4 jit_solution(14324456205511016430)
XLA Ops:
  0.6 5.2 %collective-permute-start.3 = (bf16[1,2,9,128,128]{4,3,2,1,0:T(8,128)(2,1)}, bf16[1,2,9,128,128]{4,3,2,1,0:T(8,128)(2,1)S(1)}, u32[]{:S(2)}, u32[]{:S(2)}) collective-permute-start(bf16[1,2,9,128,128]{4,3,2,1,0:T(8,128)(2,1)} %own_ref.1), channel_id=1, source_target_pairs={{0,18},{1,19},{2,16},{3,17},{4,22},{5,23},{6,20},{7,21},{8,26},{9,... | collective-permute-start | bytes 1769480 | tf_op jit(solution)/shard_map/ppermute | solution.py:213
  5.9 5.5 %collective-permute-start.2 = (bf16[1,2,9,128,128]{4,3,2,1,0:T(8,128)(2,1)}, bf16[1,2,9,128,128]{4,3,2,1,0:T(8,128)(2,1)S(1)}, u32[]{:S(2)}, u32[]{:S(2)}) collective-permute-start(bf16[1,2,9,128,128]{4,3,2,1,0:T(8,128)(2,1)} %own_ref.1), channel_id=1, source_target_pairs={{0,1},{1,0},{2,3},{3,2},{4,5},{5,4},{6,7},{7,6},{8,9},{9,8},{10,11... | collective-permute-start | bytes 1769480 | tf_op jit(solution)/shard_map/ppermute | solution.py:215
  11.4 1.8 %shard_map.68 = (bf16[65,16,128]{2,1,0:T(8,128)(2,1)S(1)}, bf16[33,16,128]{2,1,0:T(8,128)(2,1)}, bf16[33,16,128]{2,1,0:T(8,128)(2,1)}) custom-call(bf16[2,8,32,128]{3,2,1,0:T(8,128)(2,1)} %atmos_ref.1, bf16[2,8,32,128]{3,2,1,0:T(8,128)(2,1)} %ocean_ref.1, s32[1,2]{1,0:T(1,128)} %rotation_ref.1, s32[8,32]{1,0:T(8,128)} %mask_ref.1), custom_call_target="tpu_custom_call" | custom-call | tf_op jit(solution)/shard_map/pallas_call | solution.py:197
  13.2 1.9 %collective-permute-start = (bf16[33,16,128]{2,1,0:T(8,128)(2,1)}, bf16[33,16,128]{2,1,0:T(8,128)(2,1)S(1)}, u32[]{:S(2)}, u32[]{:S(2)}) collective-permute-start(bf16[33,16,128]{2,1,0:T(8,128)(2,1)} %get-tuple-element.11), channel_id=1, source_target_pairs={{0,4},{4,8},{8,12},{12,16},{16,20},{20,24},{24,28},{28,32},{32,36}... | collective-permute-start | bytes 405512 | tf_op jit(solution)/shard_map/ppermute | solution.py:216
  15.1 10.6 %collective-permute-start.1 = (bf16[33,16,128]{2,1,0:T(8,128)(2,1)}, bf16[33,16,128]{2,1,0:T(8,128)(2,1)S(1)}, u32[]{:S(2)}, u32[]{:S(2)}) collective-permute-start(bf16[33,16,128]{2,1,0:T(8,128)(2,1)} %get-tuple-element.12), channel_id=1, source_target_pairs={{4,0},{8,4},{12,8},{16,12},{20,16},{24,20},{28,24},{32,28},{36,32}... | collective-permute-start | bytes 405512 | tf_op jit(solution)/shard_map/ppermute | solution.py:217
  25.7 0.0 collective-permute-done.3.far_ref
  25.7 2.2 %collective-permute-start.4 = (bf16[1,2,9,128,128]{4,3,2,1,0:T(8,128)(2,1)S(1)}, bf16[1,2,9,128,128]{4,3,2,1,0:T(8,128)(2,1)S(1)}, u32[]{:S(2)}, u32[]{:S(2)}) collective-permute-start(bf16[1,2,9,128,128]{4,3,2,1,0:T(8,128)(2,1)S(1)} %collective-permute-done.3.far_ref), channel_id=1, source_target_pairs={{0,1},{1,0},{2,3},{3,2},{4,5},{5,4},{6,7},{7,6},{8,9},{9,8},{10,11... | collective-permute-start | bytes 1769480 | tf_op jit(solution)/shard_map/ppermute | solution.py:219
  27.9 0.0 collective-permute-done.before_ref
  27.9 1.1 %collective-permute-done.1.after_ref = bf16[33,16,128]{2,1,0:T(8,128)(2,1)S(1)} collective-permute-done((bf16[33,16,128]{2,1,0:T(8,128)(2,1)}, bf16[33,16,128]{2,1,0:T(8,128)(2,1)S(1)}, u32[]{:S(2)}, u32[]{:S(2)}) %collective-permute-start.1) | collective-permute-done | bytes 135200 | tf_op jit(solution)/shard_map/ppermute | solution.py:217
  29.0 0.0 collective-permute-done.2.sibling_ref
  29.0 0.4 %shard_map.69 = (bf16[280,16,128]{2,1,0:T(8,128)(2,1)S(1)}, bf16[4,2,9,128,128]{4,3,2,1,0:T(8,128)(2,1)S(1)}) custom-call(bf16[65,16,128]{2,1,0:T(8,128)(2,1)S(1)} %get-tuple-element.10.fields_ref, bf16[33,16,128]{2,1,0:T(8,128)(2,1)S(1)} %collective-permute-done.before_ref, bf16[33,16,128]{2,1,0:T(8,128)(2,1)S(1)} %collective-permute-done.1.after_ref, ...), custom_call_target="tpu_custom_call" | custom-call | flops 20000000000 | bytes 1048576 | tf_op jit(solution)/shard_map/pallas_call | solution.py:223
  29.4 0.2 collective-permute-done.4.last_ref
  29.6 8.8 %shard_map.70 = (bf16[2,2,32,128]{3,2,1,0:T(8,128)(2,1)}, bf16[2,2,32,128]{3,2,1,0:T(8,128)(2,1)}, bf16[4,2,9,128,128]{4,3,2,1,0:T(8,128)(2,1)S(1)}) custom-call(bf16[280,16,128]{2,1,0:T(8,128)(2,1)S(1)} %get-tuple-element.14.state_ref, bf16[4,2,9,128,128]{4,3,2,1,0:T(8,128)(2,1)S(1)} %get-tuple-element.15.weight_in, ...), custom_call_target="tpu_custom_call", output_to_operand_aliasing={{2}: (1, {})} | custom-call | tf_op jit(solution)/shard_map/pallas_call | solution.py:234
Async XLA Ops:
  0.6 25.1 %collective-permute-start.3 = (bf16[1,2,9,128,128]{4,3,2,1,0:T(8,128)(2,1)}, bf16[1,2,9,128,128]{4,3,2,1,0:T(8,128)(2,1)S(1)}, u32[]{:S(2)}, u32[]{:S(2)}) collective-permute-start(bf16[1,2,9,128,128]{4,3,2,1,0:T(8,128)(2,1)} %own_ref.1), channel_id=1, source_target_pairs={{0,18},{1,19},{2,16},{3,17},{4,22},{5,23},{6,20},{7,21},{8,26},{9,... | collective-permute-start | bytes 1769480 | tf_op jit(solution)/shard_map/ppermute | solution.py:213
  5.9 23.2 %collective-permute-start.2 = (bf16[1,2,9,128,128]{4,3,2,1,0:T(8,128)(2,1)}, bf16[1,2,9,128,128]{4,3,2,1,0:T(8,128)(2,1)S(1)}, u32[]{:S(2)}, u32[]{:S(2)}) collective-permute-start(bf16[1,2,9,128,128]{4,3,2,1,0:T(8,128)(2,1)} %own_ref.1), channel_id=1, source_target_pairs={{0,1},{1,0},{2,3},{3,2},{4,5},{5,4},{6,7},{7,6},{8,9},{9,8},{10,11... | collective-permute-start | bytes 1769480 | tf_op jit(solution)/shard_map/ppermute | solution.py:215
  13.2 14.8 %collective-permute-start = (bf16[33,16,128]{2,1,0:T(8,128)(2,1)}, bf16[33,16,128]{2,1,0:T(8,128)(2,1)S(1)}, u32[]{:S(2)}, u32[]{:S(2)}) collective-permute-start(bf16[33,16,128]{2,1,0:T(8,128)(2,1)} %get-tuple-element.11), channel_id=1, source_target_pairs={{0,4},{4,8},{8,12},{12,16},{16,20},{20,24},{24,28},{28,32},{32,36}... | collective-permute-start | bytes 405512 | tf_op jit(solution)/shard_map/ppermute | solution.py:216
  15.1 13.9 %collective-permute-start.1 = (bf16[33,16,128]{2,1,0:T(8,128)(2,1)}, bf16[33,16,128]{2,1,0:T(8,128)(2,1)S(1)}, u32[]{:S(2)}, u32[]{:S(2)}) collective-permute-start(bf16[33,16,128]{2,1,0:T(8,128)(2,1)} %get-tuple-element.12), channel_id=1, source_target_pairs={{4,0},{8,4},{12,8},{16,12},{20,16},{24,20},{28,24},{32,28},{36,32}... | collective-permute-start | bytes 405512 | tf_op jit(solution)/shard_map/ppermute | solution.py:217
  25.7 3.9 %collective-permute-start.4 = (bf16[1,2,9,128,128]{4,3,2,1,0:T(8,128)(2,1)S(1)}, bf16[1,2,9,128,128]{4,3,2,1,0:T(8,128)(2,1)S(1)}, u32[]{:S(2)}, u32[]{:S(2)}) collective-permute-start(bf16[1,2,9,128,128]{4,3,2,1,0:T(8,128)(2,1)S(1)} %collective-permute-done.3.far_ref), channel_id=1, source_target_pairs={{0,1},{1,0},{2,3},{3,2},{4,5},{5,4},{6,7},{7,6},{8,9},{9,8},{10,11... | collective-permute-start | bytes 1769480 | tf_op jit(solution)/shard_map/ppermute | solution.py:219
